TPU v7x, 32 devices: a whole 2x2x4 slice. The times are simulated.
32 devices in a mesh: segment: 2 (over x), seq: 8 (over z, core), tensor: 2 (over y).
Axes of the slice: x: 2, y: 2, z: 4, core: 2. Of those that a mesh axis runs over, the one named last changes fastest.
Arguments:
- vision_states: bfloat16 [1536, 7680], P(('segment', 'seq'), 'tensor'), may hold values from -6 to 6
- kv_weight: bfloat16 [7680, 2048], P('tensor'), may hold values from -0.09375 to 0.09375
- key_gain: float32 [128], replicated, may hold values from 0.5 to 1.5
- queries: bfloat16 [4096, 8, 1024], P('seq', 'tensor', 'segment'), may hold values from -700 to 700
- tile_tokens: int32 [4], replicated, may hold values from 192 to 384, as said below
- text_tiles: int32 [4096, 2], P('seq'), may hold values from 0 to 4, as said below
Outputs:
- attended: bfloat16 [4096, 8, 1024], P('seq', 'tensor', 'segment')
Inputs may be any that keep to these rules, and one draw needn't show every extreme that they name: The valid tokens of tile i are its first tile_tokens[i] positions of 384; some tile is full. Text token r sees tiles text_tiles[r, 0] to text_tiles[r, 1] - 1, with text_tiles[r, 0] <= text_tiles[r, 1]; an empty range means it sees no image.
All inputs are finite; a program needn't handle non-finite values.
Results may differ from a plain program's by a relative error of at most 0.012.
The roundings to bfloat16 on the way count: a program that leaves them out, or rounds other values in their place, can miss the bound.
Values may be sent and summed in bfloat16 or wider, within the bound.
No kernel may reach another device: no remote copies, remote signals or barrier semaphores. Data moves between devices by JAX's collectives and lax.ppermute only.
A program may use at most 128 MiB of HBM per device.

v0:
```python
import jax
import jax.numpy as jnp
from jax import lax
from jax.sharding import PartitionSpec as P


def block_count(total_rows, limit_rows):
    for parts_count in range(1, total_rows + 1):
        if total_rows % parts_count == 0 and total_rows // parts_count <= limit_rows:
            return parts_count
    return total_rows


def visibility(positions, tile_len, tile_tokens, lower, upper):
    tile_ids = positions // tile_len
    within_tile = positions % tile_len
    tile_table = jnp.arange(tile_tokens.shape[0], dtype=jnp.int32)
    valid_count = jnp.sum(
        jnp.where(tile_ids[:, None] == tile_table[None, :], tile_tokens[None, :], 0), axis=-1
    )
    key_valid = within_tile < valid_count
    return (
        key_valid[None, :]
        & (tile_ids[None, :] >= lower[:, None])
        & (tile_ids[None, :] < upper[:, None])
    )


def update(running, query_heads, kv_piece, visible, score_scale, head_dim):
    row_max, row_sum, summed = running
    scores = (
        jnp.einsum(
            "rkhd,knd->rkhn",
            query_heads,
            kv_piece[:, :, :head_dim],
            preferred_element_type=jnp.float32,
        )
        * score_scale
    )
    key_mask = visible[:, None, None, :]
    masked = jnp.where(key_mask, scores, -1e30)
    new_max = jnp.maximum(row_max, jnp.max(masked, axis=-1))
    factor = jnp.exp(row_max - new_max)
    expterm = jnp.where(key_mask, jnp.exp(masked - new_max[..., None]), 0.0)
    row_sum = row_sum * factor + jnp.sum(expterm, axis=-1)
    weights = expterm.astype(jnp.bfloat16)
    summed = summed * factor[..., None] + jnp.einsum(
        "rkhn,knd->rkhd", weights, kv_piece[:, :, head_dim:], preferred_element_type=jnp.float32
    )
    return (new_max, row_sum, summed)


def shards(vision_states, kv_weight, key_gain, queries, tile_tokens, text_tiles):
    head_dim = key_gain.shape[0]
    key_rows = vision_states.shape[0]
    all_heads = kv_weight.shape[1] // (2 * head_dim)
    local_heads = all_heads // lax.axis_size("tensor")
    weight_heads = kv_weight.reshape(kv_weight.shape[0], all_heads, 2 * head_dim)
    sums = lax.psum_scatter(
        jnp.einsum("rd,dch->crh", vision_states, weight_heads, preferred_element_type=jnp.float32),
        "tensor",
        scatter_dimension=0,
        tiled=True,
    )
    keys_raw = sums[:, :, :head_dim]
    mean_sq = jnp.mean(keys_raw * keys_raw, axis=-1, keepdims=True)
    normed = keys_raw * lax.rsqrt(mean_sq + 1e-05) * key_gain
    kv_block = jnp.concatenate([normed, sums[:, :, head_dim:]], axis=-1).astype(jnp.bfloat16)
    segment_count = lax.axis_size("segment")
    seq_count = lax.axis_size("seq")
    tile_len = key_rows * segment_count * seq_count // tile_tokens.shape[0]
    text_rows = queries.shape[0]
    query_count = queries.shape[2] // head_dim
    query_heads = queries.reshape(text_rows, local_heads, query_count, head_dim)
    lower = text_tiles[:, 0]
    upper = text_tiles[:, 1]
    unseen = (upper <= lower).astype(jnp.float32)
    score_scale = head_dim ** (-0.5)
    start_state = (
        jnp.full((text_rows, local_heads, query_count), -1e30, jnp.float32),
        jnp.zeros((text_rows, local_heads, query_count), jnp.float32),
        jnp.zeros((text_rows, local_heads, query_count, head_dim), jnp.float32),
    )
    gathered = lax.all_gather(kv_block, ("segment", "seq"), axis=1, tiled=True)
    total_rows = gathered.shape[1]
    blocks = block_count(total_rows, 768)
    block_rows = total_rows // blocks

    def one_block(block_index, state_now):
        block_piece = lax.dynamic_slice_in_dim(gathered, block_index * block_rows, block_rows, 1)
        local_rows = block_index * block_rows + jnp.arange(block_rows, dtype=jnp.int32)
        visible = visibility(local_rows, tile_len, tile_tokens, lower, upper)
        return update(state_now, query_heads, block_piece, visible, score_scale, head_dim)

    row_max, row_sum, summed = lax.fori_loop(0, blocks, one_block, start_state)
    attended = summed / (row_sum + unseen[:, None, None])[..., None]
    return attended.reshape(text_rows, local_heads, query_count * head_dim).astype(jnp.bfloat16)


def solution(mesh):
    placed = (
        P(("segment", "seq"), "tensor"),
        P("tensor", None),
        P(),
        P("seq", "tensor", "segment"),
        P(),
        P("seq", None),
    )
    return jax.shard_map(
        shards, mesh=mesh, in_specs=placed, out_specs=P("seq", "tensor", "segment"), check_vma=False
    )
```

profile of v0, /device:TPU:0, one launch (start us, length us, event | category | flops | bytes accessed | tf_op | source)
XLA Modules:
  0.0 174.0 jit_solution(9531326906504809965)
XLA Ops:
  6.5 1.1 copy-done
  7.7 9.1 %fusion.24 = f32[8,96,256]{2,1,0:T(8,128)} fusion(bf16[480,8,8,256]{3,2,1,0:T(8,128)(2,1)} %bitcast.67, bf16[96,3840]{1,0:T(8,128)(2,1)S(1)} %copy-done), kind=kOutput, calls=%fused_computation.38 | convolution fusion | flops 1509949440 | bytes 17252352 | tf_op jit(solution)/shard_map/rd,dch->crh/dot_general | solution.py:60
  16.8 20.2 %reduce-scatter.2.cloned.1.call-done = f32[4,96,256]{2,1,0:T(8,128)} async-done(((f32[8,96,256]{2,1,0:T(8,128)}), f32[4,96,256]{2,1,0:T(8,128)}) %reduce-scatter.2.cloned.1.call-update) | async-done | bytes 393232 | tf_op jit(solution)/shard_map/reduce_scatter | solution.py:59
  37.1 1.1 multiply_reduce_fusion
  38.2 0.9 slice.46
  39.1 1.0 multiply_convert_fusion
  40.2 0.7 pad_maximum_fusion
  40.9 3.0 %copy.20 = bf16[512,4,512]{0,2,1:T(8,128)(2,1)} copy(bf16[512,4,512]{2,1,0:T(4,128)(2,1)S(1)} %copy-done.1) | data formatting | bytes 4194304 | tf_op args[3]
  43.9 3.0 %copy.21 = bf16[512,4,4,128]{3,0,2,1:T(8,128)(2,1)S(1)} copy(bf16[512,4,4,128]{0,3,2,1:T(8,128)(2,1)} %bitcast.63) | data formatting | bytes 4194304
  46.9 0.6 compare_convert_fusion
  47.5 39.0 %all-gather.2.cloned.1.call-done = bf16[4,1536,256]{2,1,0:T(8,128)(2,1)} async-done(((bf16[4,96,256]{2,1,0:T(8,128)(2,1)}), bf16[4,1536,256]{2,1,0:T(8,128)(2,1)}) %all-gather.2.cloned.1.call-update) | async-done | bytes 3145744 | tf_op jit(solution)/shard_map/all_gather | solution.py:84
  86.5 74.8 %while.20 = (s32[]{:T(128)}, f32[512,4,4]{0,2,1:T(4,128)S(1)}, f32[512,4,4]{0,2,1:T(4,128)S(1)}, f32[512,4,4,128]{0,3,2,1:T(8,128)}, s32[4]{0:T(128)S(1)}, /*ind...) while((s32[]{:T(128)}, f32[512,4,4]{0,2,1:T(4,128)S(1)}, ...), condition=%wide.region_6.7_spmd.clone, body=%wide.region_2.6_spmd.clone.sunk | while | flops 3307795456 | bytes 89674472 | solution.py:95
  86.5 0.1 select_reduce_fusion.2
  86.6 0.5 compare_and_fusion.2
  87.1 11.5 %fusion.39 = (f32[512,4,4]{0,2,1:T(4,128)S(1)}, f32[4,768,512,4]{2,1,3,0:T(8,128)}) fusion(pred[512,768]{0,1:T(8,128)(4,1)S(1)} %compare_and_fusion.2, bf16[512,4,4,128]{3,0,2,1:T(8,128)(2,1)S(1)} %get-tuple-element.402, bf16[4,1536,256]{2,1,0:T(8,128)(2,1)} %get-tuple-element.401, s32[]{:T(128)S(6)} %select_n.139), kind=kOutput, calls=%fused_computation.2.clone.1 | convolution fusion | flops 1629478912 | bytes 28475396 | tf_op jit(solution)/shard_map/while/body/eval_jaxpr/rkhd,knd->rkhn/dot_general | solution.py:32
  98.6 11.5 %fusion.40 = f32[512,4,4]{0,2,1:T(4,128)S(1)} fusion(f32[4,768,512,4]{2,1,3,0:T(8,128)} %get-tuple-element.363, f32[512,4,4]{0,2,1:T(4,128)S(1)} %select_maximum_fusion.2, pred[512,768]{0,1:T(8,128)(4,1)S(1)} %compare_and_fusion.2), kind=kLoop, calls=%fused_computation.4.clone.1 | loop fusion | flops 31449088 | bytes 25624576 | tf_op jit(solution)/shard_map/while/body/eval_jaxpr/reduce_sum | solution.py:45
  110.2 13.1 %bitcast_add_fusion.2 = f32[512,4,4,128]{0,3,2,1:T(8,128)} fusion(f32[512,4,4,128]{0,3,2,1:T(8,128)} %get-tuple-element.383, f32[4,768,512,4]{2,1,3,0:T(8,128)} %get-tuple-element.363, f32[512,4,4]{0,2,1:T(4,128)S(1)} %select_maximum_fusion.2, pred[512,768]{0,1:T(8,128)(4,1)S(1)} %compare_and_fusion.2, f32[512,4,4]{0,2,1:T(4,128)S(1)} %get-tuple-element.365, ...), kind=kOutput, calls=%fused_computation.7.clone.1 | convolution fusion | flops 1645215744 | bytes 34799624 | tf_op jit(solution)/shard_map/while/body/eval_jaxpr/rkhn,knd->rkhd/dot_general | solution.py:47
  123.3 0.1 select_reduce_fusion.2
  123.4 0.5 compare_and_fusion.2
  123.9 11.5 %fusion.39 = (f32[512,4,4]{0,2,1:T(4,128)S(1)}, f32[4,768,512,4]{2,1,3,0:T(8,128)}) fusion(pred[512,768]{0,1:T(8,128)(4,1)S(1)} %compare_and_fusion.2, bf16[512,4,4,128]{3,0,2,1:T(8,128)(2,1)S(1)} %get-tuple-element.402, bf16[4,1536,256]{2,1,0:T(8,128)(2,1)} %get-tuple-element.401, s32[]{:T(128)S(6)} %select_n.139), kind=kOutput, calls=%fused_computation.2.clone.1 | convolution fusion | flops 1629478912 | bytes 28475396 | tf_op jit(solution)/shard_map/while/body/eval_jaxpr/rkhd,knd->rkhn/dot_general | solution.py:32
  135.4 11.5 %fusion.40 = f32[512,4,4]{0,2,1:T(4,128)S(1)} fusion(f32[4,768,512,4]{2,1,3,0:T(8,128)} %get-tuple-element.363, f32[512,4,4]{0,2,1:T(4,128)S(1)} %select_maximum_fusion.2, pred[512,768]{0,1:T(8,128)(4,1)S(1)} %compare_and_fusion.2), kind=kLoop, calls=%fused_computation.4.clone.1 | loop fusion | flops 31449088 | bytes 25624576 | tf_op jit(solution)/shard_map/while/body/eval_jaxpr/reduce_sum | solution.py:45
  147.0 14.3 %bitcast_add_fusion.2 = f32[512,4,4,128]{0,3,2,1:T(8,128)} fusion(f32[512,4,4,128]{0,3,2,1:T(8,128)} %get-tuple-element.383, f32[4,768,512,4]{2,1,3,0:T(8,128)} %get-tuple-element.363, f32[512,4,4]{0,2,1:T(4,128)S(1)} %select_maximum_fusion.2, pred[512,768]{0,1:T(8,128)(4,1)S(1)} %compare_and_fusion.2, f32[512,4,4]{0,2,1:T(4,128)S(1)} %get-tuple-element.365, ...), kind=kOutput, calls=%fused_computation.7.clone.1 | convolution fusion | flops 1645215744 | bytes 34799624 | tf_op jit(solution)/shard_map/while/body/eval_jaxpr/rkhn,knd->rkhd/dot_general | solution.py:47
  161.3 2.8 %divide_convert_fusion = bf16[512,4,4,128]{0,3,2,1:T(8,128)(2,1)S(1)} fusion(f32[512,4,4,128]{0,3,2,1:T(8,128)} %get-tuple-element.229, f32[512,4,4]{0,2,1:T(4,128)S(1)} %broadcast_add_fusion), kind=kLoop, calls=%fused_computation.37 | loop fusion | flops 2097152 | bytes 6324224 | tf_op jit(solution)/shard_map/convert_element_type | solution.py:97
  164.1 3.1 %copy.26 = bf16[512,4,512]{2,1,0:T(4,128)(2,1)} copy(bf16[512,4,512]{0,2,1:T(8,128)(2,1)S(1)} %bitcast.62) | data formatting | bytes 4194304 | tf_op jit(solution)/shard_map/convert_element_type | solution.py:97
  (31 shorter events, 0.3 us)
Async XLA Ops:
  6.5 1.1 copy-start
  6.5 30.5 %reduce-scatter.2.cloned.1.call-start = ((), (), s32[]{:S(2)}) async-start(), calls=%async_computation.1 | async-start | bytes 1179648 | tf_op jit(solution)/shard_map/reduce_scatter | solution.py:59
  7.7 31.5 %copy-start.5 = (f32[128]{0:T(128)S(1)}, f32[128]{0:T(128)}, u32[]{:S(2)}) copy-start(f32[128]{0:T(128)} %param.10) | copy-start | bytes 1540
  7.7 33.3 %copy-start.1 = (bf16[512,4,512]{2,1,0:T(4,128)(2,1)S(1)}, bf16[512,4,512]{2,1,0:T(4,128)(2,1)}, u32[]{:S(2)}) copy-start(bf16[512,4,512]{2,1,0:T(4,128)(2,1)} %param.11) | copy-start | bytes 6291460
  16.8 30.1 %copy-start.2 = (s32[512,2]{0,1:T(2,128)S(1)}, s32[512,2]{0,1:T(2,128)}, u32[]{:S(2)}) copy-start(s32[512,2]{0,1:T(2,128)} %param.13) | copy-start | bytes 12292
  16.8 69.7 %copy-start.3 = (s32[4]{0:T(128)S(1)}, s32[4]{0:T(128)}, u32[]{:S(2)}) copy-start(s32[4]{0:T(128)} %param.12) | copy-start | bytes 52
  16.8 69.7 %all-gather.2.cloned.1.call-start = ((), (), s32[]{:S(2)}) async-start(), calls=%async_computation.2 | async-start | bytes 3342336 | tf_op jit(solution)/shard_map/all_gather | solution.py:84
  86.5 74.8 %copy-start.4 = (f32[512,1]{0,1:T(1,128)S(1)}, f32[512,1]{0,1:T(1,128)}, u32[]{:S(2)}) copy-start(f32[512,1]{0,1:T(1,128)} %compare_convert_fusion) | copy-start | bytes 6148
Sparse Core Ops, SparseCore 0:
  16.9 20.1 reduce-scatter.1
  41.0 45.4 all-gather.1
where the time goes:
time: 175 us; the launch traced here: 174 us
  matrix products  59.5 us (34%)
  waiting for transfers between devices  59.3 us (34%)
  other arithmetic  30.6 us (17%)
  between operations  13.5 us (8%)
  local copies, waits for them, and re-layouts  11.1 us (6%)
    all_gather x1, waiting for transfers between devices, shards(): gathered = lax.all_gather(kv_block, ('segment', 'seq'), axis=1, tiled=True)  39 us
    dot_general x2, matrix products, update(): jnp.einsum('rkhn,knd->rkhd', weights, kv_piece[:, :, head_dim:], preferre...  27.4 us
    reduce_sum x2, other arithmetic, update(): row_sum = row_sum * factor + jnp.sum(expterm, axis=-1)  23.1 us
    dot_general x2, matrix products, update(): jnp.einsum('rkhd,knd->rkhn', query_heads, kv_piece[:, :, :head_dim], pref...  22.9 us
    reduce_scatter x1, waiting for transfers between devices, shards(): lax.psum_scatter(jnp.einsum('rd,dch->crh', vision_states, weight_heads, p...  20.2 us
    dot_general x1, matrix products, shards(): jnp.einsum('rd,dch->crh', vision_states, weight_heads, preferred_element_...  9.1 us
    unnamed x14, local copies, waits for them, and re-layouts  7.1 us
  transfers between devices with their start and end apart: 2, of which 2 were waited for; matrix products, arithmetic and copies ran while one was open for 4% of the time, Pallas kernels for 0%

commit v1 on v0

v1 whole, which is shorter than its diff:
```python
import functools

import jax
import jax.numpy as jnp
from jax import lax
from jax.experimental import pallas as pl
from jax.experimental.pallas import tpu as pltpu
from jax.sharding import PartitionSpec as P

MASKED = -1e30
LOG2E = 1.4426950408889634
VMEM = pl.BlockSpec(memory_space=pltpu.VMEM)
SMEM = pl.BlockSpec(memory_space=pltpu.SMEM)
ANY = pl.BlockSpec(memory_space=pl.ANY)


def project_kernel(block_ref, vision_ref, weight_ref, out_ref):
    out_ref[...] = jnp.dot(vision_ref[...], weight_ref[...], preferred_element_type=jnp.float32)


def project(vision, weight, first_block, block_cols, blocks):
    rows, depth = vision.shape
    return pl.pallas_call(
        project_kernel,
        grid_spec=pltpu.PrefetchScalarGridSpec(
            num_scalar_prefetch=1,
            grid=(blocks,),
            in_specs=[
                pl.BlockSpec((rows, depth), lambda i, first: (0, 0)),
                pl.BlockSpec((depth, block_cols), lambda i, first: (0, first[0] + i)),
            ],
            out_specs=pl.BlockSpec((rows, block_cols), lambda i, first: (0, i)),
        ),
        out_shape=jax.ShapeDtypeStruct((rows, blocks * block_cols), jnp.float32),
        compiler_params=pltpu.CompilerParams(vmem_limit_bytes=32 * 1024 * 1024),
        cost_estimate=pl.CostEstimate(
            flops=2 * rows * depth * blocks * block_cols,
            bytes_accessed=2 * depth * blocks * block_cols,
            transcendentals=0,
        ),
    )(first_block.reshape(1), vision, weight)


def finish_kernel(heads, dim, own_ref, other_ref, gain_ref, out_ref):
    for head in range(heads):
        at = head * 2 * dim
        keys = own_ref[:, at : at + dim] + other_ref[:, at : at + dim]
        mean_sq = jnp.mean(keys * keys, axis=-1, keepdims=True)
        keys = keys * lax.rsqrt(mean_sq + 1e-05) * gain_ref[...]
        values = own_ref[:, at + dim : at + 2 * dim] + other_ref[:, at + dim : at + 2 * dim]
        out_ref[head, :, :dim] = keys.astype(jnp.bfloat16)
        out_ref[head, :, dim:] = values.astype(jnp.bfloat16)


def finish(own, other, gain, heads, dim):
    rows = own.shape[0]
    return pl.pallas_call(
        functools.partial(finish_kernel, heads, dim),
        in_specs=[VMEM, VMEM, VMEM],
        out_specs=VMEM,
        out_shape=jax.ShapeDtypeStruct((heads, rows, 2 * dim), jnp.bfloat16),
        cost_estimate=pl.CostEstimate(flops=8 * own.size, bytes_accessed=10 * own.size, transcendentals=rows),
    )(own, other, gain.reshape(1, dim))


def attend_kernel(heads, group, dim, tiles, block_rows, pieces, place_ref, tokens_ref, *refs):
    kv_refs = refs[:pieces]
    q_ref, range_ref, out_ref, k_ref, v_ref, qm_ref, s_ref, sems = refs[pieces:]
    text_rows = q_ref.shape[1]
    total = k_ref.shape[1]
    piece_rows = kv_refs[0].shape[1]
    tile_len = total // tiles
    copies = []
    for piece in range(pieces):
        at = pl.multiple_of(place_ref[piece] * piece_rows, piece_rows)
        for part, into in enumerate((k_ref.at[:, pl.ds(at, piece_rows), pl.ds(0, dim)], v_ref.at[:, pl.ds(at, piece_rows), :])):
            copy = pltpu.make_async_copy(kv_refs[piece].at[:, :, pl.ds(part * dim, dim)], into, sems.at[piece, part])
            copy.start()
            copies.append(copy)
    lanes = lax.broadcasted_iota(jnp.int32, (text_rows, dim), 1)
    lower, upper = range_ref[:, 0:1], range_ref[:, 1:2]
    hidden = (lanes < lower) | (lanes >= upper) | (lanes >= tiles)
    qm_ref[...] = jnp.where(hidden & (lanes <= tiles), 1.0, 0.0).astype(jnp.bfloat16)
    key_lanes = lax.broadcasted_iota(jnp.int32, (tile_len, dim), 1)
    key_place = lax.broadcasted_iota(jnp.int32, (tile_len, dim), 0)
    for tile in range(tiles):
        off = (key_lanes == tile) | ((key_lanes == tiles) & (key_place >= tokens_ref[tile]))
        for head in range(heads):
            k_ref[head, tile * tile_len : (tile + 1) * tile_len, dim:] = jnp.where(off, MASKED, 0.0).astype(jnp.bfloat16)
    for copy in copies:
        copy.wait()
    row_blocks = text_rows // block_rows
    steps = heads * group * row_blocks
    scale = LOG2E * dim ** (-0.5)

    def where(step):
        head = step // (group * row_blocks)
        rest = step % (group * row_blocks)
        return head, rest // row_blocks, rest % row_blocks

    def score(step, slot):
        head, member, block = where(step)
        rows = pl.ds(block * block_rows, block_rows)
        cols = pl.ds(pl.multiple_of(member * dim, dim), dim)
        q = jnp.concatenate([q_ref[head, rows, cols], qm_ref[rows, :]], axis=1)
        s_ref[slot] = lax.dot_general(
            q, k_ref[head], (((1,), (1,)), ((), ())), preferred_element_type=jnp.float32
        )

    def weigh(step, slot):
        head, member, block = where(step)
        rows = pl.ds(block * block_rows, block_rows)
        cols = pl.ds(pl.multiple_of(member * dim, dim), dim)
        scores = s_ref[slot]
        row_max = jnp.max(scores, axis=1, keepdims=True)
        terms = jnp.exp2((scores - row_max) * scale)
        denominator = jnp.sum(terms, axis=1, keepdims=True)
        summed = jnp.dot(terms.astype(jnp.bfloat16), v_ref[head], preferred_element_type=jnp.float32)
        seen = range_ref[rows, 1:2] > range_ref[rows, 0:1]
        attended = jnp.where(seen, summed / denominator, 0.0)
        out_ref[head, rows, cols] = attended.astype(jnp.bfloat16)

    score(0, 0)

    @pl.loop(0, steps // 2)
    def _(pair):
        step = pair * 2
        score(step + 1, 1)
        weigh(step, 0)
        score(jnp.minimum(step + 2, steps - 1), 0)
        weigh(step + 1, 1)


def attend(q, kv, places, tokens, text_tiles, tiles):
    heads, text_rows, width = q.shape
    dim = kv[0].shape[2] // 2
    group = width // dim
    total = sum(piece.shape[1] for piece in kv)
    block_rows = min(256, text_rows)
    cells = heads * group * text_rows * total
    return pl.pallas_call(
        functools.partial(attend_kernel, heads, group, dim, tiles, block_rows, len(kv)),
        in_specs=[SMEM, SMEM] + [ANY] * len(kv) + [VMEM, VMEM],
        out_specs=VMEM,
        out_shape=jax.ShapeDtypeStruct(q.shape, jnp.bfloat16),
        scratch_shapes=[
            pltpu.VMEM((heads, total, 2 * dim), jnp.bfloat16),
            pltpu.VMEM((heads, total, dim), jnp.bfloat16),
            pltpu.VMEM((text_rows, dim), jnp.bfloat16),
            pltpu.VMEM((2, block_rows, total), jnp.float32),
            pltpu.SemaphoreType.DMA((len(kv), 2)),
        ],
        compiler_params=pltpu.CompilerParams(vmem_limit_bytes=48 * 1024 * 1024),
        cost_estimate=pl.CostEstimate(
            flops=4 * cells * dim, bytes_accessed=4 * q.size + 4 * heads * total * dim, transcendentals=cells
        ),
    )(places, tokens, *kv, q, text_tiles)


def shards(vision_states, kv_weight, key_gain, queries, tile_tokens, text_tiles):
    dim = key_gain.shape[0]
    vision_rows = vision_states.shape[0]
    all_heads = kv_weight.shape[1] // (2 * dim)
    tensor, segment, seq = lax.axis_size("tensor"), lax.axis_size("segment"), lax.axis_size("seq")
    heads = all_heads // tensor
    tiles = tile_tokens.shape[0]
    q = jnp.transpose(queries, (1, 0, 2))
    if tensor == 2 and segment == 2 and seq == 8:
        kv, places = exchange(vision_states, kv_weight, key_gain, heads, dim)
    else:
        weight_heads = kv_weight.reshape(kv_weight.shape[0], all_heads, 2 * dim)
        partial = jnp.einsum("rd,dch->crh", vision_states, weight_heads, preferred_element_type=jnp.float32)
        sums = lax.psum_scatter(partial, "tensor", scatter_dimension=0, tiled=True)
        keys = sums[:, :, :dim]
        mean_sq = jnp.mean(keys * keys, axis=-1, keepdims=True)
        keys = keys * lax.rsqrt(mean_sq + 1e-05) * key_gain
        block = jnp.concatenate([keys, sums[:, :, dim:]], axis=-1).astype(jnp.bfloat16)
        kv = [lax.all_gather(block, ("segment", "seq"), axis=1, tiled=True)]
        places = jnp.zeros((1,), jnp.int32)
    attended = attend(q, kv, places, tile_tokens, text_tiles, tiles)
    return jnp.transpose(attended, (1, 0, 2))


def exchange(vision_states, kv_weight, key_gain, heads, dim):
    me_tensor, me_segment, me_seq = lax.axis_index("tensor"), lax.axis_index("segment"), lax.axis_index("seq")
    cols = heads * 2 * dim
    block_cols = 2 * dim
    theirs = project(vision_states, kv_weight, (1 - me_tensor) * heads, block_cols, heads)
    arrived = lax.ppermute(theirs, "tensor", [(0, 1), (1, 0)])
    mine = project(vision_states, kv_weight, me_tensor * heads, block_cols, heads)
    block = finish(mine, arrived, key_gain, heads, dim)
    lane = [block] + [lax.ppermute(block, "seq", [(s, s ^ (2 * far)) for s in range(8)]) for far in (1, 2, 3)]
    lane += [lax.ppermute(piece, "segment", [(0, 1), (1, 0)]) for piece in lane]
    both = lane + [lax.ppermute(piece, "seq", [(s, s ^ 1) for s in range(8)]) for piece in lane]
    places = jnp.stack(
        [
            (me_segment ^ side) * 8 + (me_seq ^ (2 * far + core))
            for core in range(2)
            for side in range(2)
            for far in range(4)
        ]
    ).astype(jnp.int32)
    return both, places


def solution(mesh):
    placed = (
        P(("segment", "seq"), "tensor"),
        P("tensor", None),
        P(),
        P("seq", "tensor", "segment"),
        P(),
        P("seq", None),
    )
    return jax.shard_map(
        shards, mesh=mesh, in_specs=placed, out_specs=P("seq", "tensor", "segment"), check_vma=False
    )
```

time: 175 us -> 90.2 us (0.52)
  matrix products: 59.5 us -> 0 us
  waiting for transfers between devices: 59.3 us -> 22.5 us
  Pallas kernels: 0 us -> 33.6 us
  other arithmetic: 30.6 us -> 0 us
  between operations: 13.5 us -> 0.14 us
  starting transfers between devices: 0.04 us -> 12.1 us
  local copies, waits for them, and re-layouts: 11.1 us -> 20.1 us
    dot_general x5 -> x0, matrix products: 59.5 us -> none  [the longest x2 27.4 us: update(): jnp.einsum('rkhn,knd->rkhd', weights, kv_piece[:, :, head_dim:], preferre...]
    all_gather x1 -> x0, waiting for transfers between devices: 39 us -> none  [shards(): gathered = lax.all_gather(kv_block, ('segment', 'seq'), axis=1, tiled=True)]
    pallas_call x0 -> x4, Pallas kernels: none -> 33.6 us  [the longest x1 25.6 us: attend(): pl.pallas_call(functools.partial(attend_kernel, heads, group, dim, tiles,...]
    reduce_sum x5 -> x0, other arithmetic: 24.3 us -> none  [the longest x2 23.1 us: update(): row_sum = row_sum * factor + jnp.sum(expterm, axis=-1)]
    ppermute x0 -> x16, waiting for transfers between devices: none -> 22.5 us  [the longest x3 14.3 us: exchange(): lax.ppermute(block, 'seq', [(s, s ^ 2 * far) for s in range(8)])]
    reduce_scatter x1 -> x0, waiting for transfers between devices: 20.2 us -> none  [shards(): lax.psum_scatter(jnp.einsum('rd,dch->crh', vision_states, weight_heads, p...]
    ppermute x0 -> x16, starting transfers between devices: none -> 12.1 us  [the longest x3 4.39 us: exchange(): lax.ppermute(block, 'seq', [(s, s ^ 2 * far) for s in range(8)])]
    unnamed x14 -> x20, local copies, waits for them, and re-layouts: 7.1 us -> 17.1 us
  transfers between devices with their start and end apart: 2 -> 16, of which waited for: 2 -> 5; matrix products, arithmetic and copies ran while one was open for 4% -> 4% of each run, Pallas kernels for 0% -> 3%
where the time goes in v1:
time: 90.2 us; the launch traced here: 88.4 us
  Pallas kernels  33.6 us (37%)
  waiting for transfers between devices  22.5 us (25%)
  local copies, waits for them, and re-layouts  20.1 us (22%)
  starting transfers between devices  12.1 us (13%)
    pallas_call x1, Pallas kernels, attend(): pl.pallas_call(functools.partial(attend_kernel, heads, group, dim, tiles,...  25.6 us
    unnamed x20, local copies, waits for them, and re-layouts  17.1 us
    ppermute x3, waiting for transfers between devices, exchange(): lax.ppermute(block, 'seq', [(s, s ^ 2 * far) for s in range(8)])  14.3 us
    ppermute x4, waiting for transfers between devices, exchange(): lane += [lax.ppermute(piece, 'segment', [(0, 1), (1, 0)]) for piece in lane]  8.12 us
    pallas_call x2, Pallas kernels, project(): pl.pallas_call(project_kernel, grid_spec=pltpu.PrefetchScalarGridSpec(num...  6.12 us
    ppermute x3, starting transfers between devices, exchange(): lax.ppermute(block, 'seq', [(s, s ^ 2 * far) for s in range(8)])  4.39 us
    ppermute x4, starting transfers between devices, exchange(): lane += [lax.ppermute(piece, 'segment', [(0, 1), (1, 0)]) for piece in lane]  4.09 us
    ppermute x1, starting transfers between devices, exchange(): arrived = lax.ppermute(theirs, 'tensor', [(0, 1), (1, 0)])  3.03 us
  transfers between devices with their start and end apart: 16, of which 5 were waited for; matrix products, arithmetic and copies ran while one was open for 4% of the time, Pallas kernels for 3%

profile of v1, /device:TPU:0, one launch (start us, length us, event | category | flops | bytes accessed | tf_op | source)
XLA Modules:
  0.0 88.4 jit_solution(10567187782664801276)
XLA Ops:
  0.0 5.5 %copy-done = bf16[3840,2048]{1,0:T(8,128)(2,1)S(1)} copy-done((bf16[3840,2048]{1,0:T(8,128)(2,1)S(1)}, bf16[3840,2048]{1,0:T(8,128)(2,1)}, u32[]{:S(2)}) %copy-start) | copy-done | bytes 15728664
  5.5 1.1 %copy-done.2 = bf16[96,3840]{1,0:T(8,128)(2,1)S(1)} copy-done((bf16[96,3840]{1,0:T(8,128)(2,1)S(1)}, bf16[96,3840]{1,0:T(8,128)(2,1)}, u32[]{:S(2)}) %copy-start.2) | copy-done | bytes 737304
  6.6 3.1 %shard_map.65 = f32[96,1024]{1,0:T(8,128)S(1)} custom-call(s32[1]{0:T(128)} %bitcast.17.block_ref, bf16[96,3840]{1,0:T(8,128)(2,1)S(1)} %copy-done.2, bf16[3840,2048]{1,0:T(8,128)(2,1)S(1)} %copy-done), custom_call_target="tpu_custom_call" | custom-call | flops 754974720 | bytes 7864320 | tf_op jit(solution)/shard_map/pallas_call | solution.py:23
  9.7 3.0 %collective-permute-start = (f32[96,1024]{1,0:T(8,128)S(1)}, f32[96,1024]{1,0:T(8,128)S(1)}, u32[]{:S(2)}, u32[]{:S(2)}) collective-permute-start(f32[96,1024]{1,0:T(8,128)S(1)} %shard_map.65), channel_id=1, source_target_pairs={{0,1},{1,0},{2,3},{3,2},{4,5},{5,4},{6,7},{7,6},{8,9},{9,8},{10,11... | collective-permute-start | bytes 1179656 | tf_op jit(solution)/shard_map/ppermute | solution.py:189
  12.7 5.5 %copy-done.1 = bf16[3840,2048]{1,0:T(8,128)(2,1)S(1)} copy-done((bf16[3840,2048]{1,0:T(8,128)(2,1)S(1)}, bf16[3840,2048]{1,0:T(8,128)(2,1)}, u32[]{:S(2)}) %copy-start.1) | copy-done | bytes 15728664
  18.2 3.1 %shard_map.64.own_ref = f32[96,1024]{1,0:T(8,128)S(1)} custom-call(s32[1]{0:T(128)} %bitcast.16.block_ref, bf16[96,3840]{1,0:T(8,128)(2,1)S(1)} %copy-done.3, bf16[3840,2048]{1,0:T(8,128)(2,1)S(1)} %copy-done.1), custom_call_target="tpu_custom_call" | custom-call | flops 754974720 | bytes 7864320 | tf_op jit(solution)/shard_map/pallas_call | solution.py:23
  21.2 0.7 copy-done.4
  22.0 0.7 copy-done.7
  22.7 1.9 %shard_map.66.refs_0_ = bf16[4,96,256]{2,1,0:T(8,128)(2,1)} custom-call(f32[96,1024]{1,0:T(8,128)} %copy-done.4, f32[96,1024]{1,0:T(8,128)} %copy-done.7, f32[1,128]{1,0:T(1,128)} %bitcast.25), custom_call_target="tpu_custom_call" | custom-call | flops 786432 | bytes 983040 | tf_op jit(solution)/shard_map/pallas_call | solution.py:57
  24.7 1.5 %collective-permute-start.4 = (bf16[4,96,256]{2,1,0:T(8,128)(2,1)}, bf16[4,96,256]{2,1,0:T(8,128)(2,1)S(1)}, u32[]{:S(2)}, u32[]{:S(2)}) collective-permute-start(bf16[4,96,256]{2,1,0:T(8,128)(2,1)} %shard_map.66.refs_0_), channel_id=1, source_target_pairs={{0,16},{16,0},{1,17},{17,1},{2,18},{18,2},{3,19},{19,3},{4,20},{20... | collective-permute-start | bytes 589832 | tf_op jit(solution)/shard_map/ppermute | solution.py:193
  26.2 3.6 %collective-permute-start.3 = (bf16[4,96,256]{2,1,0:T(8,128)(2,1)}, bf16[4,96,256]{2,1,0:T(8,128)(2,1)S(1)}, u32[]{:S(2)}, u32[]{:S(2)}) collective-permute-start(bf16[4,96,256]{2,1,0:T(8,128)(2,1)} %shard_map.66.refs_0_), channel_id=1, source_target_pairs={{0,12},{2,14},{4,8},{6,10},{8,4},{10,6},{12,0},{14,2},{1,13},{3,15... | collective-permute-start | bytes 589832 | tf_op jit(solution)/shard_map/ppermute | solution.py:192
  29.8 0.8 collective-permute-start.1
  30.6 0.7 collective-permute-done.4.refs_4_
  31.2 4.6 %collective-permute-done.3.refs_3_ = bf16[4,96,256]{2,1,0:T(8,128)(2,1)S(1)} collective-permute-done((bf16[4,96,256]{2,1,0:T(8,128)(2,1)}, bf16[4,96,256]{2,1,0:T(8,128)(2,1)S(1)}, u32[]{:S(2)}, u32[]{:S(2)}) %collective-permute-start.3) | collective-permute-done | bytes 196640 | tf_op jit(solution)/shard_map/ppermute | solution.py:192
  35.8 0.5 collective-permute-start.7
  36.3 9.8 %collective-permute-done.2.refs_2_ = bf16[4,96,256]{2,1,0:T(8,128)(2,1)S(1)} collective-permute-done((bf16[4,96,256]{2,1,0:T(8,128)(2,1)}, bf16[4,96,256]{2,1,0:T(8,128)(2,1)S(1)}, u32[]{:S(2)}, u32[]{:S(2)}) %collective-permute-start.2) | collective-permute-done | bytes 196640 | tf_op jit(solution)/shard_map/ppermute | solution.py:192
  46.1 0.5 collective-permute-start.6
  46.6 1.5 %collective-permute-start.5 = (bf16[4,96,256]{2,1,0:T(8,128)(2,1)S(1)}, bf16[4,96,256]{2,1,0:T(8,128)(2,1)S(1)}, u32[]{:S(2)}, u32[]{:S(2)}) collective-permute-start(bf16[4,96,256]{2,1,0:T(8,128)(2,1)S(1)} %collective-permute-done.1.refs_1_), channel_id=1, source_target_pairs={{0,16},{16,0},{1,17},{17,1},{2,18},{18,2},{3,19},{19,3},{4,20},{20... | collective-permute-start | bytes 589832 | tf_op jit(solution)/shard_map/ppermute | solution.py:193
  48.1 0.5 collective-permute-start.9
  48.7 5.2 %collective-permute-done.6.refs_6_ = bf16[4,96,256]{2,1,0:T(8,128)(2,1)S(1)} collective-permute-done((bf16[4,96,256]{2,1,0:T(8,128)(2,1)S(1)}, bf16[4,96,256]{2,1,0:T(8,128)(2,1)S(1)}, u32[]{:S(2)}, u32[]{:S(2)}) %collective-permute-start.6) | collective-permute-done | bytes 196640 | tf_op jit(solution)/shard_map/ppermute | solution.py:193
  53.9 2.3 %collective-permute-done.5.refs_5_ = bf16[4,96,256]{2,1,0:T(8,128)(2,1)S(1)} collective-permute-done((bf16[4,96,256]{2,1,0:T(8,128)(2,1)S(1)}, bf16[4,96,256]{2,1,0:T(8,128)(2,1)S(1)}, u32[]{:S(2)}, u32[]{:S(2)}) %collective-permute-start.5) | collective-permute-done | bytes 196640 | tf_op jit(solution)/shard_map/ppermute | solution.py:193
  56.4 3.4 %copy.11 = bf16[512,4,512]{2,0,1:T(8,128)(2,1)} copy(bf16[512,4,512]{2,1,0:T(4,128)(2,1)} %param.9) | data formatting | bytes 4194304 | tf_op args[3]
  59.9 25.6 %shard_map.67 = bf16[4,512,512]{2,1,0:T(8,128)(2,1)S(1)} custom-call(s32[16]{0:T(128)S(1)} %stack.67.place_ref, s32[4]{0:T(128)S(1)} %copy-done.6, bf16[4,96,256]{2,1,0:T(8,128)(2,1)S(1)} %copy-done.5, bf16[4,96,256]{2,1,0:T(8,128)(2,1)S(1)} %collective-permute-done.1.refs_1_, bf16[4,96,256]{2,1,0:T(8,128)(2,1)S(1)} %collective-permute-done.2.refs_2_, ...), custom_call_target="tpu_custom_call" | custom-call | flops 6442450944 | bytes 7340032 | tf_op jit(solution)/shard_map/pallas_call | solution.py:141
  85.5 2.9 %copy.9 = bf16[512,4,512]{2,1,0:T(4,128)(2,1)} copy(bf16[512,4,512]{2,0,1:T(8,128)(2,1)S(1)} %bitcast.23) | data formatting | bytes 4194304 | tf_op jit(solution)/shard_map/transpose | solution.py:181
  (34 shorter events, 0.4 us)
Async XLA Ops:
  0.0 5.5 %copy-start = (bf16[3840,2048]{1,0:T(8,128)(2,1)S(1)}, bf16[3840,2048]{1,0:T(8,128)(2,1)}, u32[]{:S(2)}) copy-start(bf16[3840,2048]{1,0:T(8,128)(2,1)} %weight_ref.3) | copy-start | bytes 47185924
  5.5 1.1 %copy-start.2 = (bf16[96,3840]{1,0:T(8,128)(2,1)S(1)}, bf16[96,3840]{1,0:T(8,128)(2,1)}, u32[]{:S(2)}) copy-start(bf16[96,3840]{1,0:T(8,128)(2,1)} %vision_ref.3) | copy-start | bytes 2211844
  6.6 6.1 %copy-start.3 = (bf16[96,3840]{1,0:T(8,128)(2,1)S(1)}, bf16[96,3840]{1,0:T(8,128)(2,1)}, u32[]{:S(2)}) copy-start(bf16[96,3840]{1,0:T(8,128)(2,1)} %vision_ref.3) | copy-start | bytes 2211844
  9.7 12.3 %collective-permute-start = (f32[96,1024]{1,0:T(8,128)S(1)}, f32[96,1024]{1,0:T(8,128)S(1)}, u32[]{:S(2)}, u32[]{:S(2)}) collective-permute-start(f32[96,1024]{1,0:T(8,128)S(1)} %shard_map.65), channel_id=1, source_target_pairs={{0,1},{1,0},{2,3},{3,2},{4,5},{5,4},{6,7},{7,6},{8,9},{9,8},{10,11... | collective-permute-start | bytes 1179656 | tf_op jit(solution)/shard_map/ppermute | solution.py:189
  12.7 5.5 %copy-start.1 = (bf16[3840,2048]{1,0:T(8,128)(2,1)S(1)}, bf16[3840,2048]{1,0:T(8,128)(2,1)}, u32[]{:S(2)}) copy-start(bf16[3840,2048]{1,0:T(8,128)(2,1)} %weight_ref.3) | copy-start | bytes 47185924
  18.2 38.0 %copy-start.8 = (s32[512,2]{0,1:T(2,128)S(1)}, s32[512,2]{0,1:T(2,128)}, u32[]{:S(2)}) copy-start(s32[512,2]{0,1:T(2,128)} %param.11) | copy-start | bytes 12292
  22.0 0.8 copy-start.7
  24.7 6.6 %collective-permute-start.4 = (bf16[4,96,256]{2,1,0:T(8,128)(2,1)}, bf16[4,96,256]{2,1,0:T(8,128)(2,1)S(1)}, u32[]{:S(2)}, u32[]{:S(2)}) collective-permute-start(bf16[4,96,256]{2,1,0:T(8,128)(2,1)} %shard_map.66.refs_0_), channel_id=1, source_target_pairs={{0,16},{16,0},{1,17},{17,1},{2,18},{18,2},{3,19},{19,3},{4,20},{20... | collective-permute-start | bytes 589832 | tf_op jit(solution)/shard_map/ppermute | solution.py:193
  26.2 9.6 %collective-permute-start.3 = (bf16[4,96,256]{2,1,0:T(8,128)(2,1)}, bf16[4,96,256]{2,1,0:T(8,128)(2,1)S(1)}, u32[]{:S(2)}, u32[]{:S(2)}) collective-permute-start(bf16[4,96,256]{2,1,0:T(8,128)(2,1)} %shard_map.66.refs_0_), channel_id=1, source_target_pairs={{0,12},{2,14},{4,8},{6,10},{8,4},{10,6},{12,0},{14,2},{1,13},{3,15... | collective-permute-start | bytes 589832 | tf_op jit(solution)/shard_map/ppermute | solution.py:192
  29.8 6.0 %collective-permute-start.8 = (bf16[4,96,256]{2,1,0:T(8,128)(2,1)}, bf16[4,96,256]{2,1,0:T(8,128)(2,1)S(1)}, u32[]{:S(2)}, u32[]{:S(2)}) collective-permute-start(bf16[4,96,256]{2,1,0:T(8,128)(2,1)} %shard_map.66.refs_0_), channel_id=1, source_target_pairs={{0,2},{2,0},{4,6},{6,4},{8,10},{10,8},{12,14},{14,12},{1,3},{3,1},... | collective-permute-start | bytes 589832 | tf_op jit(solution)/shard_map/ppermute | solution.py:194
  29.8 16.3 %collective-permute-start.2 = (bf16[4,96,256]{2,1,0:T(8,128)(2,1)}, bf16[4,96,256]{2,1,0:T(8,128)(2,1)S(1)}, u32[]{:S(2)}, u32[]{:S(2)}) collective-permute-start(bf16[4,96,256]{2,1,0:T(8,128)(2,1)} %shard_map.66.refs_0_), channel_id=1, source_target_pairs={{0,8},{2,10},{4,12},{6,14},{8,0},{10,2},{12,4},{14,6},{1,9},{3,11}... | collective-permute-start | bytes 589832 | tf_op jit(solution)/shard_map/ppermute | solution.py:192
  29.8 16.8 %collective-permute-start.1 = (bf16[4,96,256]{2,1,0:T(8,128)(2,1)}, bf16[4,96,256]{2,1,0:T(8,128)(2,1)S(1)}, u32[]{:S(2)}, u32[]{:S(2)}) collective-permute-start(bf16[4,96,256]{2,1,0:T(8,128)(2,1)} %shard_map.66.refs_0_), channel_id=1, source_target_pairs={{0,4},{2,6},{4,0},{6,2},{8,12},{10,14},{12,8},{14,10},{1,5},{3,7},... | collective-permute-start | bytes 589832 | tf_op jit(solution)/shard_map/ppermute | solution.py:192
  31.2 16.9 %collective-permute-start.12 = (bf16[4,96,256]{2,1,0:T(8,128)(2,1)S(1)}, bf16[4,96,256]{2,1,0:T(8,128)(2,1)S(1)}, u32[]{:S(2)}, u32[]{:S(2)}) collective-permute-start(bf16[4,96,256]{2,1,0:T(8,128)(2,1)S(1)} %collective-permute-done.4.refs_4_), channel_id=1, source_target_pairs={{0,2},{2,0},{4,6},{6,4},{8,10},{10,8},{12,14},{14,12},{1,3},{3,1},... | collective-permute-start | bytes 589832 | tf_op jit(solution)/shard_map/ppermute | solution.py:194
  35.8 12.3 %collective-permute-start.11 = (bf16[4,96,256]{2,1,0:T(8,128)(2,1)S(1)}, bf16[4,96,256]{2,1,0:T(8,128)(2,1)S(1)}, u32[]{:S(2)}, u32[]{:S(2)}) collective-permute-start(bf16[4,96,256]{2,1,0:T(8,128)(2,1)S(1)} %collective-permute-done.3.refs_3_), channel_id=1, source_target_pairs={{0,2},{2,0},{4,6},{6,4},{8,10},{10,8},{12,14},{14,12},{1,3},{3,1},... | collective-permute-start | bytes 589832 | tf_op jit(solution)/shard_map/ppermute | solution.py:194
  35.8 12.8 %collective-permute-start.7 = (bf16[4,96,256]{2,1,0:T(8,128)(2,1)S(1)}, bf16[4,96,256]{2,1,0:T(8,128)(2,1)S(1)}, u32[]{:S(2)}, u32[]{:S(2)}) collective-permute-start(bf16[4,96,256]{2,1,0:T(8,128)(2,1)S(1)} %collective-permute-done.3.refs_3_), channel_id=1, source_target_pairs={{0,16},{16,0},{1,17},{17,1},{2,18},{18,2},{3,19},{19,3},{4,20},{20... | collective-permute-start | bytes 589832 | tf_op jit(solution)/shard_map/ppermute | solution.py:193
  46.1 7.8 %collective-permute-start.6 = (bf16[4,96,256]{2,1,0:T(8,128)(2,1)S(1)}, bf16[4,96,256]{2,1,0:T(8,128)(2,1)S(1)}, u32[]{:S(2)}, u32[]{:S(2)}) collective-permute-start(bf16[4,96,256]{2,1,0:T(8,128)(2,1)S(1)} %collective-permute-done.2.refs_2_), channel_id=1, source_target_pairs={{0,16},{16,0},{1,17},{17,1},{2,18},{18,2},{3,19},{19,3},{4,20},{20... | collective-permute-start | bytes 589832 | tf_op jit(solution)/shard_map/ppermute | solution.py:193
  46.6 9.6 %collective-permute-start.5 = (bf16[4,96,256]{2,1,0:T(8,128)(2,1)S(1)}, bf16[4,96,256]{2,1,0:T(8,128)(2,1)S(1)}, u32[]{:S(2)}, u32[]{:S(2)}) collective-permute-start(bf16[4,96,256]{2,1,0:T(8,128)(2,1)S(1)} %collective-permute-done.1.refs_1_), channel_id=1, source_target_pairs={{0,16},{16,0},{1,17},{17,1},{2,18},{18,2},{3,19},{19,3},{4,20},{20... | collective-permute-start | bytes 589832 | tf_op jit(solution)/shard_map/ppermute | solution.py:193
  48.1 11.7 %collective-permute-start.10 = (bf16[4,96,256]{2,1,0:T(8,128)(2,1)S(1)}, bf16[4,96,256]{2,1,0:T(8,128)(2,1)S(1)}, u32[]{:S(2)}, u32[]{:S(2)}) collective-permute-start(bf16[4,96,256]{2,1,0:T(8,128)(2,1)S(1)} %collective-permute-done.2.refs_2_), channel_id=1, source_target_pairs={{0,2},{2,0},{4,6},{6,4},{8,10},{10,8},{12,14},{14,12},{1,3},{3,1},... | collective-permute-start | bytes 589832 | tf_op jit(solution)/shard_map/ppermute | solution.py:194
  48.1 11.7 %collective-permute-start.9 = (bf16[4,96,256]{2,1,0:T(8,128)(2,1)S(1)}, bf16[4,96,256]{2,1,0:T(8,128)(2,1)S(1)}, u32[]{:S(2)}, u32[]{:S(2)}) collective-permute-start(bf16[4,96,256]{2,1,0:T(8,128)(2,1)S(1)} %collective-permute-done.1.refs_1_), channel_id=1, source_target_pairs={{0,2},{2,0},{4,6},{6,4},{8,10},{10,8},{12,14},{14,12},{1,3},{3,1},... | collective-permute-start | bytes 589832 | tf_op jit(solution)/shard_map/ppermute | solution.py:194
  48.7 11.2 %collective-permute-start.15 = (bf16[4,96,256]{2,1,0:T(8,128)(2,1)S(1)}, bf16[4,96,256]{2,1,0:T(8,128)(2,1)S(1)}, u32[]{:S(2)}, u32[]{:S(2)}) collective-permute-start(bf16[4,96,256]{2,1,0:T(8,128)(2,1)S(1)} %collective-permute-done.7.refs_7_), channel_id=1, source_target_pairs={{0,2},{2,0},{4,6},{6,4},{8,10},{10,8},{12,14},{14,12},{1,3},{3,1},... | collective-permute-start | bytes 589832 | tf_op jit(solution)/shard_map/ppermute | solution.py:194
  53.9 5.9 %collective-permute-start.14 = (bf16[4,96,256]{2,1,0:T(8,128)(2,1)S(1)}, bf16[4,96,256]{2,1,0:T(8,128)(2,1)S(1)}, u32[]{:S(2)}, u32[]{:S(2)}) collective-permute-start(bf16[4,96,256]{2,1,0:T(8,128)(2,1)S(1)} %collective-permute-done.6.refs_6_), channel_id=1, source_target_pairs={{0,2},{2,0},{4,6},{6,4},{8,10},{10,8},{12,14},{14,12},{1,3},{3,1},... | collective-permute-start | bytes 589832 | tf_op jit(solution)/shard_map/ppermute | solution.py:194
  56.2 3.7 %collective-permute-start.13 = (bf16[4,96,256]{2,1,0:T(8,128)(2,1)S(1)}, bf16[4,96,256]{2,1,0:T(8,128)(2,1)S(1)}, u32[]{:S(2)}, u32[]{:S(2)}) collective-permute-start(bf16[4,96,256]{2,1,0:T(8,128)(2,1)S(1)} %collective-permute-done.5.refs_5_), channel_id=1, source_target_pairs={{0,2},{2,0},{4,6},{6,4},{8,10},{10,8},{12,14},{14,12},{1,3},{3,1},... | collective-permute-start | bytes 589832 | tf_op jit(solution)/shard_map/ppermute | solution.py:194
  56.4 3.5 %copy-start.5 = (bf16[4,96,256]{2,1,0:T(8,128)(2,1)S(1)}, bf16[4,96,256]{2,1,0:T(8,128)(2,1)}, u32[]{:S(2)}) copy-start(bf16[4,96,256]{2,1,0:T(8,128)(2,1)} %shard_map.66.refs_0_) | copy-start | bytes 589828
  56.4 3.5 %copy-start.6 = (s32[4]{0:T(128)S(1)}, s32[4]{0:T(128)}, u32[]{:S(2)}) copy-start(s32[4]{0:T(128)} %tokens_ref.1) | copy-start | bytes 52
  (1 other events, 0.7 us)

commit v2 on v0

v2 whole, which is shorter than its diff:
```python
import functools

import jax
import jax.numpy as jnp
from jax import lax
from jax.experimental import pallas as pl
from jax.experimental.pallas import tpu as pltpu
from jax.sharding import PartitionSpec as P

MASKED = -1e30
CHUNKS = 1
STORES = 4
LOG2E = 1.4426950408889634
BLOCK_ROWS = 128
LARGE_VMEM = 52 * 1024 * 1024
MIDDLE_VMEM = 44 * 1024 * 1024
SMALL_VMEM = 16 * 1024 * 1024
VMEM = pl.BlockSpec(memory_space=pltpu.VMEM)
SMEM = pl.BlockSpec(memory_space=pltpu.SMEM)
ANY = pl.BlockSpec(memory_space=pl.ANY)
HBM = pl.BlockSpec(memory_space=pltpu.HBM)
ROWS_BY_ROWS = (((1,), (1,)), ((), ()))
COLS_BY_COLS = (((0,), (0,)), ((), ()))


def lasting(microseconds):
    return pl.CostEstimate(flops=0, bytes_accessed=int(3.6e6 * microseconds), transcendentals=0)


def project_kernel(pieces, block_ref, vision_hbm_ref, weight_ref, *refs):
    count = block_ref.shape[0]
    out_hbm_refs, (vision_ref, held_ref, out_ref, vision_sem, sems, out_sems) = refs[:count], refs[count:]
    depth, cols = held_ref.shape[1:]
    load = pltpu.make_async_copy(vision_hbm_ref, vision_ref, vision_sem)
    load.start()
    copies = []
    for step in range(count * pieces):
        which, piece = divmod(step, pieces)
        across = pl.ds(pl.multiple_of(block_ref[which] * cols, cols), cols)
        copies.append(
            pltpu.make_async_copy(weight_ref.at[pl.ds(piece * depth, depth), across], held_ref.at[step], sems.at[step])
        )
        copies[-1].start()
    load.wait()
    stores = []
    for which in range(count):
        total = None
        for piece in range(pieces):
            copies[which * pieces + piece].wait()
            part = vision_ref[:, piece * depth : (piece + 1) * depth]
            product = jnp.dot(part, held_ref[which * pieces + piece], preferred_element_type=jnp.float32)
            total = product if piece == 0 else total + product
        out_ref[which] = total
        stores.append(pltpu.make_async_copy(out_ref.at[which], out_hbm_refs[which], out_sems.at[which]))
        stores[-1].start()
    for store in stores:
        store.wait()


def project(vision, weight, blocks, cols):
    rows, depth = vision.shape
    count = len(blocks)
    pieces = next(parts for parts in (5, 3, 2, 1) if depth % (parts * 128) == 0)
    return pl.pallas_call(
        functools.partial(project_kernel, pieces),
        in_specs=[SMEM, ANY, ANY],
        out_specs=[ANY] * count,
        out_shape=[jax.ShapeDtypeStruct((rows, cols), jnp.float32)] * count,
        scratch_shapes=[
            pltpu.VMEM((rows, depth), jnp.bfloat16),
            pltpu.VMEM((count * pieces, depth // pieces, cols), jnp.bfloat16),
            pltpu.VMEM((count, rows, cols), jnp.float32),
            pltpu.SemaphoreType.DMA,
            pltpu.SemaphoreType.DMA((count * pieces,)),
            pltpu.SemaphoreType.DMA((count,)),
        ],
        compiler_params=pltpu.CompilerParams(vmem_limit_bytes=LARGE_VMEM),
        cost_estimate=lasting(2 + 1.2 * count),
    )(jnp.stack(blocks), vision, weight)


def finish_kernel(heads, dim, own_ref, other_ref, gain_ref, out_ref):
    for head in range(heads):
        at = head * 2 * dim
        keys = own_ref[:, at : at + dim] + other_ref[:, at : at + dim]
        mean_sq = jnp.mean(keys * keys, axis=-1, keepdims=True)
        keys = keys * lax.rsqrt(mean_sq + 1e-05) * gain_ref[...]
        values = own_ref[:, at + dim : at + 2 * dim] + other_ref[:, at + dim : at + 2 * dim]
        out_ref[head, :, :dim] = keys.astype(jnp.bfloat16)
        out_ref[head, :, dim:] = values.astype(jnp.bfloat16)


def finish(own, other, gain, heads, dim):
    rows = own.shape[0]
    return pl.pallas_call(
        functools.partial(finish_kernel, heads, dim),
        in_specs=[VMEM, VMEM, VMEM],
        out_specs=VMEM,
        out_shape=jax.ShapeDtypeStruct((heads, rows, 2 * dim), jnp.bfloat16),
        compiler_params=pltpu.CompilerParams(vmem_limit_bytes=SMALL_VMEM),
        cost_estimate=lasting(1.5),
    )(own, other, gain.reshape(1, dim))


def sort_kernel(tiles, group, q_ref, range_rows_ref, sorted_ref, hidden_ref, back_ref, hull_ref):
    rows, heads, width = q_ref.shape
    dim = width // group

    def order(lower, upper, at):
        key = jnp.where(upper > lower, (tiles - 1 - lower) * (tiles + 1) + tiles - upper, -1)
        return key * rows + at

    lower_row, upper_row = range_rows_ref[0:1, :], range_rows_ref[1:2, :]
    columns = jnp.concatenate([lower_row, upper_row] * 4, axis=0).astype(jnp.float32).T.astype(jnp.int32)
    lower, upper = columns[:, 0:1], columns[:, 1:2]
    order_col = order(lower, upper, lax.broadcasted_iota(jnp.int32, (rows, 1), 0))
    order_row = order(lower_row, upper_row, lax.broadcasted_iota(jnp.int32, (1, rows), 1))
    rank_row = jnp.sum(jnp.where(order_col < order_row, 1.0, 0.0), axis=0, keepdims=True).astype(jnp.int32)
    rank_col = jnp.sum(jnp.where(order_row < order_col, 1.0, 0.0), axis=1, keepdims=True).astype(jnp.int32)
    into = jnp.where(lax.broadcasted_iota(jnp.int32, (rows, rows), 0) == rank_row, 1.0, 0.0).astype(jnp.bfloat16)
    back = jnp.where(lax.broadcasted_iota(jnp.int32, (rows, rows), 1) == rank_col, 1.0, 0.0).astype(jnp.bfloat16)
    back_ref[...] = back
    seen_row = upper_row > lower_row
    blocks = rows // BLOCK_ROWS
    for block in range(blocks):
        inside = seen_row & (rank_row >= block * BLOCK_ROWS) & (rank_row < (block + 1) * BLOCK_ROWS)
        hull_ref[0, block] = jnp.min(jnp.where(inside, lower_row, tiles).astype(jnp.float32)).astype(jnp.int32)
        hull_ref[1, block] = jnp.max(jnp.where(inside, upper_row, 0).astype(jnp.float32)).astype(jnp.int32)
    hull_ref[2, 0] = jnp.sum(jnp.where(seen_row, 0.0, 1.0)).astype(jnp.int32)
    lanes = lax.broadcasted_iota(jnp.int32, (rows, dim), 1)
    unseen = (lanes < tiles) & ((lanes < lower) | (lanes >= upper)) | (lanes == tiles)
    hidden = jnp.where(unseen, 1.0, 0.0).astype(jnp.bfloat16)
    hidden_ref[...] = jnp.dot(into, hidden, preferred_element_type=jnp.float32).astype(jnp.bfloat16)
    q_heads = jnp.transpose(q_ref[...], (1, 0, 2))
    for head in range(heads):
        moved = jnp.dot(into, q_heads[head], preferred_element_type=jnp.float32).astype(jnp.bfloat16)
        for block in range(blocks):
            for member in range(group):
                at = (block * group + member) * BLOCK_ROWS
                sorted_ref[head, at : at + BLOCK_ROWS, :] = moved[
                    block * BLOCK_ROWS : (block + 1) * BLOCK_ROWS, member * dim : (member + 1) * dim
                ]


def sort_rows(queries, text_tiles, tiles, dim):
    rows, heads, width = queries.shape
    group = width // dim
    return pl.pallas_call(
        functools.partial(sort_kernel, tiles, group),
        in_specs=[VMEM, VMEM],
        out_specs=[VMEM, VMEM, VMEM, SMEM],
        out_shape=[
            jax.ShapeDtypeStruct((heads, rows * group, dim), jnp.bfloat16),
            jax.ShapeDtypeStruct((rows, dim), jnp.bfloat16),
            jax.ShapeDtypeStruct((rows, rows), jnp.bfloat16),
            jax.ShapeDtypeStruct((3, rows // BLOCK_ROWS), jnp.int32),
        ],
        compiler_params=pltpu.CompilerParams(vmem_limit_bytes=MIDDLE_VMEM),
        cost_estimate=lasting(5),
    )(queries, text_tiles.T)


def attend_kernel(shape, offsets, earlier, last, home_ref, tokens_ref, hull_ref, *refs):
    heads, first_head, blocks, group, dim, tiles, tile_len = shape
    pieces = len(offsets)
    kv_refs, refs = refs[:pieces], refs[pieces:]
    done_refs, refs = refs[:earlier], refs[earlier:]
    q_hbm_ref, hidden_hbm_ref, back_hbm_ref, result_hbm_ref = refs[:4]
    q_ref, hidden_ref, back_ref, done_ref, result_ref, k_ref, v_ref, turned_ref, sems, load_sems, store_sems = refs[4:]
    piece_rows = kv_refs[0].shape[1]
    columns = group * BLOCK_ROWS
    scale = LOG2E * dim ** (-0.5)
    copies = []
    for piece in range(pieces):
        at = pl.multiple_of((home_ref[0] ^ offsets[piece]) * piece_rows, piece_rows)
        into = k_ref.at[:, pl.ds(at, piece_rows), pl.ds(0, dim)], v_ref.at[:, pl.ds(at, piece_rows), :]
        for part in range(2):
            source = kv_refs[piece].at[:, :, pl.ds(part * dim, dim)]
            copies.append(pltpu.make_async_copy(source, into[part], sems.at[piece, part]))
            copies[-1].start()
    loads = [(q_hbm_ref.at[pl.ds(first_head, heads)], q_ref), (hidden_hbm_ref, hidden_ref), (back_hbm_ref, back_ref)]
    loads += [(ref, done_ref.at[pl.ds(i * heads, heads)]) for i, ref in enumerate(done_refs)]
    loads = [pltpu.make_async_copy(*ends, load_sems.at[i]) for i, ends in enumerate(loads)]
    for load in loads:
        load.start()
    lanes = lax.broadcasted_iota(jnp.int32, (tile_len, dim), 1)
    place = lax.broadcasted_iota(jnp.int32, (tile_len, dim), 0)
    for tile in range(tiles):
        off = (lanes == tile) | ((lanes == tiles) & (place >= tokens_ref[tile]))
        off = jnp.where(off, MASKED, 0.0).astype(jnp.bfloat16)
        for head in range(heads):
            k_ref[head, tile * tile_len : (tile + 1) * tile_len, dim:] = off
    for copy in [*copies, *loads[:2]]:
        copy.wait()

    def work(block, first, count):
        here = pl.ds(pl.multiple_of(block * BLOCK_ROWS, BLOCK_ROWS), BLOCK_ROWS)
        if count == 0:
            turned_ref[:, :, here] = jnp.zeros((heads, group * dim, BLOCK_ROWS), jnp.bfloat16)
            return
        rows = pl.ds(pl.multiple_of(block * columns, columns), columns)
        span = pl.ds(pl.multiple_of(first * tile_len, tile_len), count * tile_len)
        hidden = jnp.concatenate([hidden_ref[here, :]] * group, axis=0)
        row = lax.broadcasted_iota(jnp.int32, (1, columns), 1) % BLOCK_ROWS + block * BLOCK_ROWS
        scores = [
            lax.dot_general(
                k_ref[head, span, :],
                jnp.concatenate([q_ref[head, rows, :], hidden], axis=1),
                ROWS_BY_ROWS,
                preferred_element_type=jnp.float32,
            )
            for head in range(heads)
        ]
        for head in range(heads):
            row_max = jnp.max(scores[head], axis=0, keepdims=True)
            terms = jnp.exp2((scores[head] - row_max) * scale)
            denominator = jnp.sum(terms, axis=0, keepdims=True)
            summed = lax.dot_general(
                v_ref[head, span, :], terms.astype(jnp.bfloat16), COLS_BY_COLS, preferred_element_type=jnp.float32
            )
            inverse = jnp.where(row >= hull_ref[2, 0], 1.0 / denominator, 0.0)
            attended = (summed * inverse).astype(jnp.bfloat16)
            for member in range(group):
                turned_ref[head, member * dim : (member + 1) * dim, here] = attended[
                    :, member * BLOCK_ROWS : (member + 1) * BLOCK_ROWS
                ]

    @pl.loop(0, blocks)
    def _(block):
        first = hull_ref[0, block]
        seen = jnp.maximum(hull_ref[1, block] - first, 0)
        for count in range(tiles + 1):

            @pl.when(seen == count)
            def _():
                work(block, first, count)

    for load in loads[2:]:
        load.wait()
    if not last:
        store = pltpu.make_async_copy(turned_ref, result_hbm_ref, store_sems.at[0])
        store.start()
        store.wait()
        return
    stores = []
    rows = back_ref.shape[0] // STORES
    for part in range(STORES):
        here = pl.ds(part * rows, rows)
        back = back_ref[here, :]
        whole = [
            lax.dot_general(back, turned, ROWS_BY_ROWS, preferred_element_type=jnp.float32).astype(jnp.bfloat16)
            for turned in [done_ref[i] for i in range(first_head)] + [turned_ref[head] for head in range(heads)]
        ]
        result_ref[here] = jnp.transpose(jnp.stack(whole, axis=0), (1, 0, 2))
        stores.append(pltpu.make_async_copy(result_ref.at[here], result_hbm_ref.at[here], store_sems.at[part]))
        stores[-1].start()
    for store in stores:
        store.wait()


def attend(text, first, kv, offsets, home, tokens, tile_len, done, last):
    q, hidden, back, hull = text
    heads, dim = kv[0].shape[0], kv[0].shape[2] // 2
    text_rows, blocks = back.shape[0], hull.shape[1]
    group, tiles = q.shape[1] // text_rows, tokens.shape[0]
    width = group * dim
    total = sum(piece.shape[1] for piece in kv)
    whole = (text_rows, q.shape[0], width) if last else (heads, width, text_rows)
    return pl.pallas_call(
        functools.partial(attend_kernel, (heads, first, blocks, group, dim, tiles, tile_len), offsets, len(done), last),
        in_specs=[SMEM] * 3 + [ANY] * len(kv) + [HBM] * (len(done) + 3),
        out_specs=ANY,
        out_shape=jax.ShapeDtypeStruct(whole, jnp.bfloat16),
        scratch_shapes=[
            pltpu.VMEM((heads, *q.shape[1:]), jnp.bfloat16),
            pltpu.VMEM(hidden.shape, jnp.bfloat16),
            pltpu.VMEM(back.shape, jnp.bfloat16),
            pltpu.VMEM((max(first, 1), width, text_rows), jnp.bfloat16),
            pltpu.VMEM((text_rows, q.shape[0], width) if last else (8, 128), jnp.bfloat16),
            pltpu.VMEM((heads, total, 2 * dim), jnp.bfloat16),
            pltpu.VMEM((heads, total, dim), jnp.bfloat16),
            pltpu.VMEM((heads, width, text_rows), jnp.bfloat16),
            pltpu.SemaphoreType.DMA((len(kv), 2)),
            pltpu.SemaphoreType.DMA((3 + len(done),)),
            pltpu.SemaphoreType.DMA((STORES,)),
        ],
        compiler_params=pltpu.CompilerParams(vmem_limit_bytes=MIDDLE_VMEM),
        cost_estimate=lasting(5 * heads),
    )(home.reshape(1), tokens, hull, *kv, *done, q, hidden, back)


def shards(vision_states, kv_weight, key_gain, queries, tile_tokens, text_tiles):
    dim = key_gain.shape[0]
    all_heads = kv_weight.shape[1] // (2 * dim)
    tensor, segment, seq = lax.axis_size("tensor"), lax.axis_size("segment"), lax.axis_size("seq")
    heads = all_heads // tensor
    tiles = tile_tokens.shape[0]
    tile_len = vision_states.shape[0] * segment * seq // tiles
    if tensor == 2 and segment == 2 and seq == 8 and heads % CHUNKS == 0:
        return by_chunks(vision_states, kv_weight, key_gain, queries, tile_tokens, text_tiles, heads, tile_len)
    text = sort_rows(queries, text_tiles, tiles, dim)
    weight_heads = kv_weight.reshape(kv_weight.shape[0], all_heads, 2 * dim)
    partial = jnp.einsum("rd,dch->crh", vision_states, weight_heads, preferred_element_type=jnp.float32)
    sums = lax.psum_scatter(partial, "tensor", scatter_dimension=0, tiled=True)
    keys = sums[:, :, :dim]
    mean_sq = jnp.mean(keys * keys, axis=-1, keepdims=True)
    keys = keys * lax.rsqrt(mean_sq + 1e-05) * key_gain
    block = jnp.concatenate([keys, sums[:, :, dim:]], axis=-1).astype(jnp.bfloat16)
    kv = [lax.all_gather(block, ("segment", "seq"), axis=1, tiled=True)]
    return attend(text, 0, kv, [0], jnp.int32(0), tile_tokens, tile_len, [], True)


def after(first, then):
    return lax.optimization_barrier((first, then))[1]


def by_chunks(vision_states, kv_weight, key_gain, queries, tile_tokens, text_tiles, heads, tile_len):
    dim = key_gain.shape[0]
    me_tensor, me_segment, me_seq = lax.axis_index("tensor"), lax.axis_index("segment"), lax.axis_index("seq")
    count = heads // CHUNKS

    def across(array, axis, step):
        return lax.ppermute(array, axis, [(i, i ^ step) for i in range(lax.axis_size(axis))])

    def parts(*wanted):
        blocks = [(owner * CHUNKS + chunk).astype(jnp.int32) for owner, chunk in wanted]
        return project(vision_states, kv_weight, blocks, count * 2 * dim)

    text = sort_rows(queries, text_tiles, tile_tokens.shape[0], dim)
    home = me_segment * 8 + me_seq
    offsets = [8 * side + 2 * far + core for core in range(2) for side in range(2) for far in range(4)]
    other = 1 - me_tensor
    (theirs,) = parts((other, 0))
    arrived = [across(theirs, "tensor", 1)]
    rest = parts(*((other, chunk) for chunk in range(1, CHUNKS)), *((me_tensor, chunk) for chunk in range(CHUNKS)))
    arrived += [across(theirs, "tensor", 1) for theirs in rest[: CHUNKS - 1]]
    mine = rest[CHUNKS - 1 :]
    blocks = [finish(mine[chunk], arrived[chunk], key_gain, count, dim) for chunk in range(CHUNKS)]
    done = []
    for chunk, block in enumerate(blocks):
        last = chunk == CHUNKS - 1
        near, far = across(block, "seq", 2), across(block, "seq", 4)
        lane = [block, near, far, across(far, "seq", 2)]
        lane += [across(piece, "segment", 1) for piece in lane]
        if chunk == 0:
            lane[-2], text = lax.optimization_barrier((lane[-2], text))
        if done:
            lane[-1] = after(done[-1], lane[-1])
        kv = lane + [across(piece, "seq", 1) for piece in lane]
        done.append(attend(text, chunk * count, kv, offsets, home, tile_tokens, tile_len, done if last else [], last))
    return done[-1]


def solution(mesh):
    placed = (
        P(("segment", "seq"), "tensor"),
        P("tensor", None),
        P(),
        P("seq", "tensor", "segment"),
        P(),
        P("seq", None),
    )
    return jax.shard_map(
        shards, mesh=mesh, in_specs=placed, out_specs=P("seq", "tensor", "segment"), check_vma=False
    )
```

time: 175 us -> 67.6 us (0.39)
  matrix products: 59.5 us -> 0 us
  waiting for transfers between devices: 59.3 us -> 17.3 us
  other arithmetic: 30.6 us -> 0 us
  Pallas kernels: 0 us -> 28.9 us
  starting transfers between devices: 0.04 us -> 14.5 us
  between operations: 13.5 us -> 0.26 us
  local copies, waits for them, and re-layouts: 11.1 us -> 5.94 us
    dot_general x5 -> x0, matrix products: 59.5 us -> none  [the longest x2 27.4 us: update(): jnp.einsum('rkhn,knd->rkhd', weights, kv_piece[:, :, head_dim:], preferre...]
    all_gather x1 -> x0, waiting for transfers between devices: 39 us -> none  [shards(): gathered = lax.all_gather(kv_block, ('segment', 'seq'), axis=1, tiled=True)]
    pallas_call x0 -> x5, Pallas kernels: none -> 28.9 us  [the longest x1 17.4 us: attend(): pl.pallas_call(functools.partial(attend_kernel, (heads, first, blocks, gr...]
    reduce_sum x5 -> x0, other arithmetic: 24.3 us -> none  [the longest x2 23.1 us: update(): row_sum = row_sum * factor + jnp.sum(expterm, axis=-1)]
    reduce_scatter x1 -> x0, waiting for transfers between devices: 20.2 us -> none  [shards(): lax.psum_scatter(jnp.einsum('rd,dch->crh', vision_states, weight_heads, p...]
    ppermute x0 -> x16, waiting for transfers between devices: none -> 17.3 us  [across(): lax.ppermute(array, axis, [(i, i ^ step) for i in range(lax.axis_size(axi...]
    ppermute x0 -> x16, starting transfers between devices: none -> 14.5 us  [across(): lax.ppermute(array, axis, [(i, i ^ step) for i in range(lax.axis_size(axi...]
    convert_element_type x2 -> x0, other arithmetic: 3.38 us -> none  [the longest x1 2.79 us: shards(): attended.reshape(text_rows, local_heads, query_count * head_dim)]
  transfers between devices with their start and end apart: 2 -> 16, of which waited for: 2 -> 7; matrix products, arithmetic and copies ran while one was open for 4% -> 0% of each run, Pallas kernels for 0% -> 11%
where the time goes in v2:
time: 67.6 us; the launch traced here: 66.9 us
  Pallas kernels  28.9 us (43%)
  waiting for transfers between devices  17.3 us (26%)
  starting transfers between devices  14.5 us (21%)
  local copies, waits for them, and re-layouts  5.94 us (9%)
    pallas_call x1, Pallas kernels, attend(): pl.pallas_call(functools.partial(attend_kernel, (heads, first, blocks, gr...  17.4 us
    ppermute x16, waiting for transfers between devices, across(): lax.ppermute(array, axis, [(i, i ^ step) for i in range(lax.axis_size(axi...  17.3 us
    ppermute x16, starting transfers between devices, across(): lax.ppermute(array, axis, [(i, i ^ step) for i in range(lax.axis_size(axi...  14.5 us
    pallas_call x2, Pallas kernels, project(): pl.pallas_call(functools.partial(project_kernel, pieces), in_specs=[SMEM,...  8.64 us
    unnamed x24, local copies, waits for them, and re-layouts  5.94 us
    pallas_call x1, Pallas kernels, sort_rows(): pl.pallas_call(functools.partial(sort_kernel, tiles, group), in_specs=[VM...  2.78 us
  transfers between devices with their start and end apart: 16, of which 7 were waited for; matrix products, arithmetic and copies ran while one was open for 0% of the time, Pallas kernels for 11%

profile of v2, /device:TPU:0, one launch (start us, length us, event | category | flops | bytes accessed | tf_op | source)
XLA Modules:
  0.0 66.9 jit_solution(12202269670327360231)
XLA Ops:
  0.0 1.1 %copy-done = bf16[96,3840]{1,0:T(8,128)(2,1)S(1)} copy-done((bf16[96,3840]{1,0:T(8,128)(2,1)S(1)}, bf16[96,3840]{1,0:T(8,128)(2,1)}, u32[]{:S(2)}) %copy-start) | copy-done | bytes 737304
  1.1 4.2 %shard_map.65 = f32[96,1024]{1,0:T(8,128)S(1)} custom-call(s32[1]{0:T(128)} %bitcast.2.block_ref, bf16[96,3840]{1,0:T(8,128)(2,1)S(1)} %copy-done, bf16[3840,2048]{1,0:T(8,128)(2,1)} %weight_ref.3), custom_call_target="tpu_custom_call" | custom-call | bytes 11520000 | tf_op jit(solution)/shard_map/pallas_call | solution.py:64
  5.4 3.0 %collective-permute-start = (f32[96,1024]{1,0:T(8,128)S(1)}, f32[96,1024]{1,0:T(8,128)S(1)}, u32[]{:S(2)}, u32[]{:S(2)}) collective-permute-start(f32[96,1024]{1,0:T(8,128)S(1)} %shard_map.65), channel_id=1, source_target_pairs={{0,1},{1,0},{2,3},{3,2},{4,5},{5,4},{6,7},{7,6},{8,9},{9,8},{10,11... | collective-permute-start | bytes 1179656 | tf_op jit(solution)/shard_map/ppermute | solution.py:323
  8.4 4.4 %shard_map.64.own_ref = f32[96,1024]{1,0:T(8,128)S(1)} custom-call(s32[1]{0:T(128)} %bitcast.1.block_ref, bf16[96,3840]{1,0:T(8,128)(2,1)S(1)} %copy-done.1, bf16[3840,2048]{1,0:T(8,128)(2,1)} %weight_ref.3), custom_call_target="tpu_custom_call" | custom-call | bytes 11520000 | tf_op jit(solution)/shard_map/pallas_call | solution.py:64
  12.8 4.7 %collective-permute-done.other_ref = f32[96,1024]{1,0:T(8,128)S(1)} collective-permute-done((f32[96,1024]{1,0:T(8,128)S(1)}, f32[96,1024]{1,0:T(8,128)S(1)}, u32[]{:S(2)}, u32[]{:S(2)}) %collective-permute-start) | collective-permute-done | bytes 393248 | tf_op jit(solution)/shard_map/ppermute | solution.py:323
  17.6 2.9 %collective-permute-start.1 = (bf16[4,96,256]{2,1,0:T(8,128)(2,1)S(1)}, bf16[4,96,256]{2,1,0:T(8,128)(2,1)S(1)}, u32[]{:S(2)}, u32[]{:S(2)}) collective-permute-start(bf16[4,96,256]{2,1,0:T(8,128)(2,1)S(1)} %shard_map.66.refs_0_), channel_id=1, source_target_pairs={{0,8},{2,10},{4,12},{6,14},{8,0},{10,2},{12,4},{14,6},{1,9},{3,11}... | collective-permute-start | bytes 589832 | tf_op jit(solution)/shard_map/ppermute | solution.py:323
  20.5 1.5 %collective-permute-start.5 = (bf16[4,96,256]{2,1,0:T(8,128)(2,1)S(1)}, bf16[4,96,256]{2,1,0:T(8,128)(2,1)S(1)}, u32[]{:S(2)}, u32[]{:S(2)}) collective-permute-start(bf16[4,96,256]{2,1,0:T(8,128)(2,1)S(1)} %shard_map.66.refs_0_), channel_id=1, source_target_pairs={{0,16},{16,0},{1,17},{17,1},{2,18},{18,2},{3,19},{19,3},{4,20},{20... | collective-permute-start | bytes 589832 | tf_op jit(solution)/shard_map/ppermute | solution.py:323
  22.0 1.6 %collective-permute-start.3 = (bf16[4,96,256]{2,1,0:T(8,128)(2,1)S(1)}, bf16[4,96,256]{2,1,0:T(8,128)(2,1)S(1)}, u32[]{:S(2)}, u32[]{:S(2)}) collective-permute-start(bf16[4,96,256]{2,1,0:T(8,128)(2,1)S(1)} %shard_map.66.refs_0_), channel_id=1, source_target_pairs={{0,4},{2,6},{4,0},{6,2},{8,12},{10,14},{12,8},{14,10},{1,5},{3,7},... | collective-permute-start | bytes 589832 | tf_op jit(solution)/shard_map/ppermute | solution.py:323
  23.6 5.4 %collective-permute-done.1.refs_2_ = bf16[4,96,256]{2,1,0:T(8,128)(2,1)S(1)} collective-permute-done((bf16[4,96,256]{2,1,0:T(8,128)(2,1)S(1)}, bf16[4,96,256]{2,1,0:T(8,128)(2,1)S(1)}, u32[]{:S(2)}, u32[]{:S(2)}) %collective-permute-start.1) | collective-permute-done | bytes 196640 | tf_op jit(solution)/shard_map/ppermute | solution.py:323
  29.5 1.5 %collective-permute-start.2 = (bf16[4,96,256]{2,1,0:T(8,128)(2,1)S(1)}, bf16[4,96,256]{2,1,0:T(8,128)(2,1)}, u32[]{:S(2)}, u32[]{:S(2)}) collective-permute-start(bf16[4,96,256]{2,1,0:T(8,128)(2,1)S(1)} %collective-permute-done.1.refs_2_), channel_id=1, source_target_pairs={{0,16},{16,0},{1,17},{17,1},{2,18},{18,2},{3,19},{19,3},{4,20},{20... | collective-permute-start | bytes 589832 | tf_op jit(solution)/shard_map/ppermute | solution.py:323
  31.5 0.5 collective-permute-start.6
  32.0 2.8 %collective-permute-done.4.refs_3_ = bf16[4,96,256]{2,1,0:T(8,128)(2,1)} collective-permute-done((bf16[4,96,256]{2,1,0:T(8,128)(2,1)S(1)}, bf16[4,96,256]{2,1,0:T(8,128)(2,1)}, u32[]{:S(2)}, u32[]{:S(2)}) %collective-permute-start.4) | collective-permute-done | bytes 196640 | tf_op jit(solution)/shard_map/ppermute | solution.py:323
  34.9 2.5 %collective-permute-done.2.refs_6_ = bf16[4,96,256]{2,1,0:T(8,128)(2,1)} collective-permute-done((bf16[4,96,256]{2,1,0:T(8,128)(2,1)S(1)}, bf16[4,96,256]{2,1,0:T(8,128)(2,1)}, u32[]{:S(2)}, u32[]{:S(2)}) %collective-permute-start.2) | collective-permute-done | bytes 196640 | tf_op jit(solution)/shard_map/ppermute | solution.py:323
  37.4 1.5 %collective-permute-start.7 = (bf16[4,96,256]{2,1,0:T(8,128)(2,1)}, bf16[4,96,256]{2,1,0:T(8,128)(2,1)}, u32[]{:S(2)}, u32[]{:S(2)}) collective-permute-start(bf16[4,96,256]{2,1,0:T(8,128)(2,1)} %collective-permute-done.4.refs_3_), channel_id=1, source_target_pairs={{0,16},{16,0},{1,17},{17,1},{2,18},{18,2},{3,19},{19,3},{4,20},{20... | collective-permute-start | bytes 589832 | tf_op jit(solution)/shard_map/ppermute | solution.py:323
  38.9 2.8 %shard_map.67 = (bf16[4,2048,128]{2,1,0:T(8,128)(2,1)S(1)}, bf16[512,128]{1,0:T(8,128)(2,1)S(1)}, bf16[512,512]{1,0:T(8,128)(2,1)S(1)}, s32[3,4]{1,0:T(4,128)S(1)}) custom-call(bf16[512,4,512]{2,1,0:T(4,128)(2,1)S(1)} %copy-done.2, s32[2,512]{1,0:T(2,128)S(1)} %bitcast.5), custom_call_target="tpu_custom_call" | custom-call | bytes 18000000 | tf_op jit(solution)/shard_map/pallas_call | solution.py:148
  41.7 0.7 copy-done.3
  42.4 0.7 %copy-done.5 = bf16[4,96,256]{2,1,0:T(8,128)(2,1)} copy-done((bf16[4,96,256]{2,1,0:T(8,128)(2,1)}, bf16[4,96,256]{2,1,0:T(8,128)(2,1)S(1)}, u32[]{:S(2)}) %copy-start.5) | copy-done | bytes 196632
  43.6 0.7 %copy-done.7 = bf16[4,96,256]{2,1,0:T(8,128)(2,1)} copy-done((bf16[4,96,256]{2,1,0:T(8,128)(2,1)}, bf16[4,96,256]{2,1,0:T(8,128)(2,1)S(1)}, u32[]{:S(2)}) %copy-start.7) | copy-done | bytes 196632
  44.8 0.6 collective-permute-done.13.refs_13_
  45.4 0.8 %collective-permute-done.11.refs_11_ = bf16[4,96,256]{2,1,0:T(8,128)(2,1)} collective-permute-done((bf16[4,96,256]{2,1,0:T(8,128)(2,1)}, bf16[4,96,256]{2,1,0:T(8,128)(2,1)}, u32[]{:S(2)}, u32[]{:S(2)}) %collective-permute-start.11) | collective-permute-done | bytes 196640 | tf_op jit(solution)/shard_map/ppermute | solution.py:323
  46.6 0.9 %copy-done.4 = bf16[4,96,256]{2,1,0:T(8,128)(2,1)S(1)} copy-done((bf16[4,96,256]{2,1,0:T(8,128)(2,1)S(1)}, bf16[4,96,256]{2,1,0:T(8,128)(2,1)}, u32[]{:S(2)}) %copy-start.4) | copy-done | bytes 196632
  47.5 0.9 %copy-done.6 = bf16[4,96,256]{2,1,0:T(8,128)(2,1)S(1)} copy-done((bf16[4,96,256]{2,1,0:T(8,128)(2,1)S(1)}, bf16[4,96,256]{2,1,0:T(8,128)(2,1)}, u32[]{:S(2)}) %copy-start.6) | copy-done | bytes 196632
  48.4 0.9 %copy-done.8 = bf16[4,96,256]{2,1,0:T(8,128)(2,1)S(1)} copy-done((bf16[4,96,256]{2,1,0:T(8,128)(2,1)S(1)}, bf16[4,96,256]{2,1,0:T(8,128)(2,1)}, u32[]{:S(2)}) %copy-start.8) | copy-done | bytes 196632
  49.3 17.4 %shard_map.68 = bf16[512,4,512]{2,1,0:T(4,128)(2,1)} custom-call(s32[1]{0:T(128)} %bitcast.home_ref, s32[4]{0:T(128)S(1)} %copy-done.11, s32[3,4]{1,0:T(4,128)S(1)} %get-tuple-element.18.hull_ref, bf16[4,96,256]{2,1,0:T(8,128)(2,1)S(1)} %shard_map.66.refs_0_, bf16[4,96,256]{2,1,0:T(8,128)(2,1)S(1)} %collective-permute-done.3.refs_1_, ...), custom_call_target="tpu_custom_call" | custom-call | bytes 72000000 | tf_op jit(solution)/shard_map/pallas_call | solution.py:269
  (37 shorter events, 2.6 us)
Async XLA Ops:
  0.0 1.1 %copy-start = (bf16[96,3840]{1,0:T(8,128)(2,1)S(1)}, bf16[96,3840]{1,0:T(8,128)(2,1)}, u32[]{:S(2)}) copy-start(bf16[96,3840]{1,0:T(8,128)(2,1)} %vision_hbm_ref.3) | copy-start | bytes 2211844
  1.1 7.3 %copy-start.1 = (bf16[96,3840]{1,0:T(8,128)(2,1)S(1)}, bf16[96,3840]{1,0:T(8,128)(2,1)}, u32[]{:S(2)}) copy-start(bf16[96,3840]{1,0:T(8,128)(2,1)} %vision_hbm_ref.3) | copy-start | bytes 2211844
  5.4 12.1 %collective-permute-start = (f32[96,1024]{1,0:T(8,128)S(1)}, f32[96,1024]{1,0:T(8,128)S(1)}, u32[]{:S(2)}, u32[]{:S(2)}) collective-permute-start(f32[96,1024]{1,0:T(8,128)S(1)} %shard_map.65), channel_id=1, source_target_pairs={{0,1},{1,0},{2,3},{3,2},{4,5},{5,4},{6,7},{7,6},{8,9},{9,8},{10,11... | collective-permute-start | bytes 1179656 | tf_op jit(solution)/shard_map/ppermute | solution.py:323
  8.4 9.1 %copy-start.10 = (f32[128]{0:T(128)S(1)}, f32[128]{0:T(128)}, u32[]{:S(2)}) copy-start(f32[128]{0:T(128)} %param.8) | copy-start | bytes 1540
  8.4 30.5 %copy-start.2 = (bf16[512,4,512]{2,1,0:T(4,128)(2,1)S(1)}, bf16[512,4,512]{2,1,0:T(4,128)(2,1)}, u32[]{:S(2)}) copy-start(bf16[512,4,512]{2,1,0:T(4,128)(2,1)} %q_ref.1) | copy-start | bytes 6291460
  8.4 30.5 %copy-start.9 = (s32[512,2]{0,1:T(2,128)S(1)}, s32[512,2]{0,1:T(2,128)}, u32[]{:S(2)}) copy-start(s32[512,2]{0,1:T(2,128)} %param.11) | copy-start | bytes 12292
  12.8 33.7 %copy-start.11 = (s32[4]{0:T(128)S(1)}, s32[4]{0:T(128)}, u32[]{:S(2)}) copy-start(s32[4]{0:T(128)} %tokens_ref.1) | copy-start | bytes 52
  17.6 11.4 %collective-permute-start.1 = (bf16[4,96,256]{2,1,0:T(8,128)(2,1)S(1)}, bf16[4,96,256]{2,1,0:T(8,128)(2,1)S(1)}, u32[]{:S(2)}, u32[]{:S(2)}) collective-permute-start(bf16[4,96,256]{2,1,0:T(8,128)(2,1)S(1)} %shard_map.66.refs_0_), channel_id=1, source_target_pairs={{0,8},{2,10},{4,12},{6,14},{8,0},{10,2},{12,4},{14,6},{1,9},{3,11}... | collective-permute-start | bytes 589832 | tf_op jit(solution)/shard_map/ppermute | solution.py:323
  20.5 10.5 %collective-permute-start.5 = (bf16[4,96,256]{2,1,0:T(8,128)(2,1)S(1)}, bf16[4,96,256]{2,1,0:T(8,128)(2,1)S(1)}, u32[]{:S(2)}, u32[]{:S(2)}) collective-permute-start(bf16[4,96,256]{2,1,0:T(8,128)(2,1)S(1)} %shard_map.66.refs_0_), channel_id=1, source_target_pairs={{0,16},{16,0},{1,17},{17,1},{2,18},{18,2},{3,19},{19,3},{4,20},{20... | collective-permute-start | bytes 589832 | tf_op jit(solution)/shard_map/ppermute | solution.py:323
  22.0 9.5 %collective-permute-start.3 = (bf16[4,96,256]{2,1,0:T(8,128)(2,1)S(1)}, bf16[4,96,256]{2,1,0:T(8,128)(2,1)S(1)}, u32[]{:S(2)}, u32[]{:S(2)}) collective-permute-start(bf16[4,96,256]{2,1,0:T(8,128)(2,1)S(1)} %shard_map.66.refs_0_), channel_id=1, source_target_pairs={{0,4},{2,6},{4,0},{6,2},{8,12},{10,14},{12,8},{14,10},{1,5},{3,7},... | collective-permute-start | bytes 589832 | tf_op jit(solution)/shard_map/ppermute | solution.py:323
  29.0 5.8 %collective-permute-start.4 = (bf16[4,96,256]{2,1,0:T(8,128)(2,1)S(1)}, bf16[4,96,256]{2,1,0:T(8,128)(2,1)}, u32[]{:S(2)}, u32[]{:S(2)}) collective-permute-start(bf16[4,96,256]{2,1,0:T(8,128)(2,1)S(1)} %collective-permute-done.1.refs_2_), channel_id=1, source_target_pairs={{0,4},{2,6},{4,0},{6,2},{8,12},{10,14},{12,8},{14,10},{1,5},{3,7},... | collective-permute-start | bytes 589832 | tf_op jit(solution)/shard_map/ppermute | solution.py:323
  29.5 7.9 %collective-permute-start.2 = (bf16[4,96,256]{2,1,0:T(8,128)(2,1)S(1)}, bf16[4,96,256]{2,1,0:T(8,128)(2,1)}, u32[]{:S(2)}, u32[]{:S(2)}) collective-permute-start(bf16[4,96,256]{2,1,0:T(8,128)(2,1)S(1)} %collective-permute-done.1.refs_2_), channel_id=1, source_target_pairs={{0,16},{16,0},{1,17},{17,1},{2,18},{18,2},{3,19},{19,3},{4,20},{20... | collective-permute-start | bytes 589832 | tf_op jit(solution)/shard_map/ppermute | solution.py:323
  31.0 10.7 %collective-permute-start.8 = (bf16[4,96,256]{2,1,0:T(8,128)(2,1)S(1)}, bf16[4,96,256]{2,1,0:T(8,128)(2,1)S(1)}, u32[]{:S(2)}, u32[]{:S(2)}) collective-permute-start(bf16[4,96,256]{2,1,0:T(8,128)(2,1)S(1)} %shard_map.66.refs_0_), channel_id=1, source_target_pairs={{0,2},{2,0},{4,6},{6,4},{8,10},{10,8},{12,14},{14,12},{1,3},{3,1},... | collective-permute-start | bytes 589832 | tf_op jit(solution)/shard_map/ppermute | solution.py:323
  31.0 11.4 %collective-permute-start.12 = (bf16[4,96,256]{2,1,0:T(8,128)(2,1)S(1)}, bf16[4,96,256]{2,1,0:T(8,128)(2,1)S(1)}, u32[]{:S(2)}, u32[]{:S(2)}) collective-permute-start(bf16[4,96,256]{2,1,0:T(8,128)(2,1)S(1)} %collective-permute-done.5.refs_4_), channel_id=1, source_target_pairs={{0,2},{2,0},{4,6},{6,4},{8,10},{10,8},{12,14},{14,12},{1,3},{3,1},... | collective-permute-start | bytes 589832 | tf_op jit(solution)/shard_map/ppermute | solution.py:323
  31.5 12.1 %collective-permute-start.6 = (bf16[4,96,256]{2,1,0:T(8,128)(2,1)S(1)}, bf16[4,96,256]{2,1,0:T(8,128)(2,1)}, u32[]{:S(2)}, u32[]{:S(2)}) collective-permute-start(bf16[4,96,256]{2,1,0:T(8,128)(2,1)S(1)} %collective-permute-done.3.refs_1_), channel_id=1, source_target_pairs={{0,16},{16,0},{1,17},{17,1},{2,18},{18,2},{3,19},{19,3},{4,20},{20... | collective-permute-start | bytes 589832 | tf_op jit(solution)/shard_map/ppermute | solution.py:323
  34.9 8.7 %collective-permute-start.9 = (bf16[4,96,256]{2,1,0:T(8,128)(2,1)S(1)}, bf16[4,96,256]{2,1,0:T(8,128)(2,1)S(1)}, u32[]{:S(2)}, u32[]{:S(2)}) collective-permute-start(bf16[4,96,256]{2,1,0:T(8,128)(2,1)S(1)} %collective-permute-done.3.refs_1_), channel_id=1, source_target_pairs={{0,2},{2,0},{4,6},{6,4},{8,10},{10,8},{12,14},{14,12},{1,3},{3,1},... | collective-permute-start | bytes 589832 | tf_op jit(solution)/shard_map/ppermute | solution.py:323
  37.4 7.4 %collective-permute-start.7 = (bf16[4,96,256]{2,1,0:T(8,128)(2,1)}, bf16[4,96,256]{2,1,0:T(8,128)(2,1)}, u32[]{:S(2)}, u32[]{:S(2)}) collective-permute-start(bf16[4,96,256]{2,1,0:T(8,128)(2,1)} %collective-permute-done.4.refs_3_), channel_id=1, source_target_pairs={{0,16},{16,0},{1,17},{17,1},{2,18},{18,2},{3,19},{19,3},{4,20},{20... | collective-permute-start | bytes 589832 | tf_op jit(solution)/shard_map/ppermute | solution.py:323
  42.4 2.4 %collective-permute-start.10 = (bf16[4,96,256]{2,1,0:T(8,128)(2,1)S(1)}, bf16[4,96,256]{2,1,0:T(8,128)(2,1)}, u32[]{:S(2)}, u32[]{:S(2)}) collective-permute-start(bf16[4,96,256]{2,1,0:T(8,128)(2,1)S(1)} %collective-permute-done.1.refs_2_), channel_id=1, source_target_pairs={{0,2},{2,0},{4,6},{6,4},{8,10},{10,8},{12,14},{14,12},{1,3},{3,1},... | collective-permute-start | bytes 589832 | tf_op jit(solution)/shard_map/ppermute | solution.py:323
  43.1 3.1 %collective-permute-start.14 = (bf16[4,96,256]{2,1,0:T(8,128)(2,1)}, bf16[4,96,256]{2,1,0:T(8,128)(2,1)}, u32[]{:S(2)}, u32[]{:S(2)}) collective-permute-start(bf16[4,96,256]{2,1,0:T(8,128)(2,1)} %collective-permute-done.2.refs_6_), channel_id=1, source_target_pairs={{0,2},{2,0},{4,6},{6,4},{8,10},{10,8},{12,14},{14,12},{1,3},{3,1},... | collective-permute-start | bytes 589832 | tf_op jit(solution)/shard_map/ppermute | solution.py:323
  43.6 1.8 %collective-permute-start.13 = (bf16[4,96,256]{2,1,0:T(8,128)(2,1)}, bf16[4,96,256]{2,1,0:T(8,128)(2,1)}, u32[]{:S(2)}, u32[]{:S(2)}) collective-permute-start(bf16[4,96,256]{2,1,0:T(8,128)(2,1)} %collective-permute-done.6.refs_5_), channel_id=1, source_target_pairs={{0,2},{2,0},{4,6},{6,4},{8,10},{10,8},{12,14},{14,12},{1,3},{3,1},... | collective-permute-start | bytes 589832 | tf_op jit(solution)/shard_map/ppermute | solution.py:323
  44.3 1.9 %collective-permute-start.11 = (bf16[4,96,256]{2,1,0:T(8,128)(2,1)}, bf16[4,96,256]{2,1,0:T(8,128)(2,1)}, u32[]{:S(2)}, u32[]{:S(2)}) collective-permute-start(bf16[4,96,256]{2,1,0:T(8,128)(2,1)} %collective-permute-done.4.refs_3_), channel_id=1, source_target_pairs={{0,2},{2,0},{4,6},{6,4},{8,10},{10,8},{12,14},{14,12},{1,3},{3,1},... | collective-permute-start | bytes 589832 | tf_op jit(solution)/shard_map/ppermute | solution.py:323
  44.8 1.8 %collective-permute-start.15 = (bf16[4,96,256]{2,1,0:T(8,128)(2,1)}, bf16[4,96,256]{2,1,0:T(8,128)(2,1)}, u32[]{:S(2)}, u32[]{:S(2)}) collective-permute-start(bf16[4,96,256]{2,1,0:T(8,128)(2,1)} %collective-permute-done.7.refs_7_), channel_id=1, source_target_pairs={{0,2},{2,0},{4,6},{6,4},{8,10},{10,8},{12,14},{14,12},{1,3},{3,1},... | collective-permute-start | bytes 589832 | tf_op jit(solution)/shard_map/ppermute | solution.py:323
  46.6 0.9 %copy-start.4 = (bf16[4,96,256]{2,1,0:T(8,128)(2,1)S(1)}, bf16[4,96,256]{2,1,0:T(8,128)(2,1)}, u32[]{:S(2)}) copy-start(bf16[4,96,256]{2,1,0:T(8,128)(2,1)} %copy-done.3) | copy-start | bytes 589828
  47.5 0.9 %copy-start.6 = (bf16[4,96,256]{2,1,0:T(8,128)(2,1)S(1)}, bf16[4,96,256]{2,1,0:T(8,128)(2,1)}, u32[]{:S(2)}) copy-start(bf16[4,96,256]{2,1,0:T(8,128)(2,1)} %copy-done.5) | copy-start | bytes 589828
  (4 other events, 3.0 us)

commit v3 on v2

--- a/solution.py
+++ b/solution.py
@@ -9,7 +9,8 @@
 
 MASKED = -1e30
 CHUNKS = 1
-STORES = 4
+HALVES = 2
+STORES = 2
 LOG2E = 1.4426950408889634
 BLOCK_ROWS = 128
 LARGE_VMEM = 52 * 1024 * 1024
@@ -76,30 +77,32 @@
         ],
         compiler_params=pltpu.CompilerParams(vmem_limit_bytes=LARGE_VMEM),
         cost_estimate=lasting(2 + 1.2 * count),
-    )(jnp.stack(blocks), vision, weight)
-
-
-def finish_kernel(heads, dim, own_ref, other_ref, gain_ref, out_ref):
+    )(jnp.stack(blocks), pltpu.with_memory_space_constraint(vision, pltpu.HBM), weight)
+
+
+def finish_kernel(heads, dim, parts, own_ref, *refs):
+    other_refs, gain_ref, out_ref = refs[:parts], refs[parts], refs[parts + 1]
     for head in range(heads):
-        at = head * 2 * dim
-        keys = own_ref[:, at : at + dim] + other_ref[:, at : at + dim]
+        part, inside = divmod(head, heads // parts)
+        at, other_at = head * 2 * dim, inside * 2 * dim
+        keys = own_ref[:, at : at + dim] + other_refs[part][:, other_at : other_at + dim]
         mean_sq = jnp.mean(keys * keys, axis=-1, keepdims=True)
         keys = keys * lax.rsqrt(mean_sq + 1e-05) * gain_ref[...]
-        values = own_ref[:, at + dim : at + 2 * dim] + other_ref[:, at + dim : at + 2 * dim]
+        values = own_ref[:, at + dim : at + 2 * dim] + other_refs[part][:, other_at + dim : other_at + 2 * dim]
         out_ref[head, :, :dim] = keys.astype(jnp.bfloat16)
         out_ref[head, :, dim:] = values.astype(jnp.bfloat16)
 
 
-def finish(own, other, gain, heads, dim):
+def finish(own, others, gain, heads, dim):
     rows = own.shape[0]
     return pl.pallas_call(
-        functools.partial(finish_kernel, heads, dim),
-        in_specs=[VMEM, VMEM, VMEM],
+        functools.partial(finish_kernel, heads, dim, len(others)),
+        in_specs=[VMEM] * (2 + len(others)),
         out_specs=VMEM,
         out_shape=jax.ShapeDtypeStruct((heads, rows, 2 * dim), jnp.bfloat16),
         compiler_params=pltpu.CompilerParams(vmem_limit_bytes=SMALL_VMEM),
         cost_estimate=lasting(1.5),
-    )(own, other, gain.reshape(1, dim))
+    )(own, *others, gain.reshape(1, dim))
 
 
 def sort_kernel(tiles, group, q_ref, range_rows_ref, sorted_ref, hidden_ref, back_ref, hull_ref):
@@ -286,7 +289,7 @@
         ],
         compiler_params=pltpu.CompilerParams(vmem_limit_bytes=MIDDLE_VMEM),
         cost_estimate=lasting(5 * heads),
-    )(home.reshape(1), tokens, hull, *kv, *done, q, hidden, back)
+    )(home.reshape(1), tokens, hull, *(pltpu.with_memory_space_constraint(piece, pltpu.HBM) for piece in kv), *done, q, hidden, back)
 
 
 def shards(vision_states, kv_weight, key_gain, queries, tile_tokens, text_tiles):
@@ -322,20 +325,17 @@
     def across(array, axis, step):
         return lax.ppermute(array, axis, [(i, i ^ step) for i in range(lax.axis_size(axis))])
 
-    def parts(*wanted):
-        blocks = [(owner * CHUNKS + chunk).astype(jnp.int32) for owner, chunk in wanted]
-        return project(vision_states, kv_weight, blocks, count * 2 * dim)
+    def parts(count, *blocks):
+        return project(vision_states, kv_weight, [block.astype(jnp.int32) for block in blocks], heads * 2 * dim // count)
 
     text = sort_rows(queries, text_tiles, tile_tokens.shape[0], dim)
     home = me_segment * 8 + me_seq
     offsets = [8 * side + 2 * far + core for core in range(2) for side in range(2) for far in range(4)]
     other = 1 - me_tensor
-    (theirs,) = parts((other, 0))
-    arrived = [across(theirs, "tensor", 1)]
-    rest = parts(*((other, chunk) for chunk in range(1, CHUNKS)), *((me_tensor, chunk) for chunk in range(CHUNKS)))
-    arrived += [across(theirs, "tensor", 1) for theirs in rest[: CHUNKS - 1]]
-    mine = rest[CHUNKS - 1 :]
-    blocks = [finish(mine[chunk], arrived[chunk], key_gain, count, dim) for chunk in range(CHUNKS)]
+    theirs = [parts(HALVES, other * HALVES + half)[0] for half in range(HALVES)]
+    arrived = [across(half, "tensor", 1) for half in theirs]
+    (mine,) = parts(1, me_tensor)
+    blocks = [finish(mine, arrived, key_gain, count, dim)]
     done = []
     for chunk, block in enumerate(blocks):
         last = chunk == CHUNKS - 1

time: 67.6 us -> 61.1 us (0.904)
  local copies, waits for them, and re-layouts: 5.94 us -> 0.05 us
  waiting for transfers between devices: 17.3 us -> 15 us
  Pallas kernels: 28.9 us -> 30.9 us
    unnamed x24 -> x22, local copies, waits for them, and re-layouts: 5.94 us -> 0.05 us
    pallas_call x2 -> x3, Pallas kernels: 8.64 us -> 11.5 us  [project(): pl.pallas_call(functools.partial(project_kernel, pieces), in_specs=[SMEM,...]
    ppermute x16 -> x17, waiting for transfers between devices: 17.3 us -> 15 us  [across(): lax.ppermute(array, axis, [(i, i ^ step) for i in range(lax.axis_size(axi...]
    pallas_call x1, Pallas kernels: 17.4 us -> 16.4 us  [attend(): pl.pallas_call(functools.partial(attend_kernel, (heads, first, blocks, gr...]
    ppermute x16 -> x17, starting transfers between devices: 14.5 us -> 14.7 us  [across(): lax.ppermute(array, axis, [(i, i ^ step) for i in range(lax.axis_size(axi...]
  transfers between devices with their start and end apart: 16 -> 17, of which waited for: 7 -> 6; matrix products, arithmetic and copies ran while one was open for 0% -> 0% of each run, Pallas kernels for 11% -> 18%
where the time goes in v3:
time: 61.1 us; the launch traced here: 60.9 us
  Pallas kernels  30.9 us (51%)
  waiting for transfers between devices  15 us (25%)
  starting transfers between devices  14.7 us (24%)
    pallas_call x1, Pallas kernels, attend(): pl.pallas_call(functools.partial(attend_kernel, (heads, first, blocks, gr...  16.4 us
    ppermute x17, waiting for transfers between devices, across(): lax.ppermute(array, axis, [(i, i ^ step) for i in range(lax.axis_size(axi...  15 us
    ppermute x17, starting transfers between devices, across(): lax.ppermute(array, axis, [(i, i ^ step) for i in range(lax.axis_size(axi...  14.7 us
    pallas_call x3, Pallas kernels, project(): pl.pallas_call(functools.partial(project_kernel, pieces), in_specs=[SMEM,...  11.5 us
    pallas_call x1, Pallas kernels, sort_rows(): pl.pallas_call(functools.partial(sort_kernel, tiles, group), in_specs=[VM...  2.78 us
  transfers between devices with their start and end apart: 17, of which 6 were waited for; matrix products, arithmetic and copies ran while one was open for 0% of the time, Pallas kernels for 18%

profile of v3, /device:TPU:0, one launch (start us, length us, event | category | flops | bytes accessed | tf_op | source)
XLA Modules:
  0.0 60.9 jit_solution(18382576538159051599)
XLA Ops:
  0.0 3.3 %shard_map.65 = f32[96,512]{1,0:T(8,128)S(1)} custom-call(s32[1]{0:T(128)} %bitcast.2.block_ref, bf16[96,3840]{1,0:T(8,128)(2,1)} %vision_hbm_ref.5, bf16[3840,2048]{1,0:T(8,128)(2,1)} %weight_ref.5), custom_call_target="tpu_custom_call" | custom-call | bytes 11520000 | tf_op jit(solution)/shard_map/pallas_call | solution.py:65
  3.3 3.1 %collective-permute-start = (f32[96,512]{1,0:T(8,128)S(1)}, f32[96,512]{1,0:T(8,128)S(1)}, u32[]{:S(2)}, u32[]{:S(2)}) collective-permute-start(f32[96,512]{1,0:T(8,128)S(1)} %shard_map.65), channel_id=1, source_target_pairs={{0,1},{1,0},{2,3},{3,2},{4,5},{5,4},{6,7},{7,6},{8,9},{9,8},{10,11... | collective-permute-start | bytes 589832 | tf_op jit(solution)/shard_map/ppermute | solution.py:326
  6.4 3.3 %shard_map.66 = f32[96,512]{1,0:T(8,128)S(1)} custom-call(s32[1]{0:T(128)} %bitcast.3.block_ref, bf16[96,3840]{1,0:T(8,128)(2,1)} %vision_hbm_ref.5, bf16[3840,2048]{1,0:T(8,128)(2,1)} %weight_ref.5), custom_call_target="tpu_custom_call" | custom-call | bytes 11520000 | tf_op jit(solution)/shard_map/pallas_call | solution.py:65
  9.8 5.0 %shard_map.64.own_ref = f32[96,1024]{1,0:T(8,128)S(1)} custom-call(s32[1]{0:T(128)} %bitcast.1.block_ref, bf16[96,3840]{1,0:T(8,128)(2,1)} %vision_hbm_ref.5, bf16[3840,2048]{1,0:T(8,128)(2,1)} %weight_ref.5), custom_call_target="tpu_custom_call" | custom-call | bytes 11520000 | tf_op jit(solution)/shard_map/pallas_call | solution.py:65
  14.8 1.3 %collective-permute-done.1.refs_1_ = f32[96,512]{1,0:T(8,128)S(1)} collective-permute-done((f32[96,512]{1,0:T(8,128)S(1)}, f32[96,512]{1,0:T(8,128)S(1)}, u32[]{:S(2)}, u32[]{:S(2)}) %collective-permute-start.1) | collective-permute-done | bytes 196640 | tf_op jit(solution)/shard_map/ppermute | solution.py:326
  16.1 0.2 shard_map.67.refs_0_
  16.3 2.7 %collective-permute-start.2 = (bf16[4,96,256]{2,1,0:T(8,128)(2,1)S(1)}, bf16[4,96,256]{2,1,0:T(8,128)(2,1)S(1)}, u32[]{:S(2)}, u32[]{:S(2)}) collective-permute-start(bf16[4,96,256]{2,1,0:T(8,128)(2,1)S(1)} %shard_map.67.refs_0_), channel_id=1, source_target_pairs={{0,8},{2,10},{4,12},{6,14},{8,0},{10,2},{12,4},{14,6},{1,9},{3,11}... | collective-permute-start | bytes 589832 | tf_op jit(solution)/shard_map/ppermute | solution.py:326
  18.9 1.5 %collective-permute-start.6 = (bf16[4,96,256]{2,1,0:T(8,128)(2,1)S(1)}, bf16[4,96,256]{2,1,0:T(8,128)(2,1)S(1)}, u32[]{:S(2)}, u32[]{:S(2)}) collective-permute-start(bf16[4,96,256]{2,1,0:T(8,128)(2,1)S(1)} %shard_map.67.refs_0_), channel_id=1, source_target_pairs={{0,16},{16,0},{1,17},{17,1},{2,18},{18,2},{3,19},{19,3},{4,20},{20... | collective-permute-start | bytes 589832 | tf_op jit(solution)/shard_map/ppermute | solution.py:326
  20.4 1.6 %collective-permute-start.4 = (bf16[4,96,256]{2,1,0:T(8,128)(2,1)S(1)}, bf16[4,96,256]{2,1,0:T(8,128)(2,1)S(1)}, u32[]{:S(2)}, u32[]{:S(2)}) collective-permute-start(bf16[4,96,256]{2,1,0:T(8,128)(2,1)S(1)} %shard_map.67.refs_0_), channel_id=1, source_target_pairs={{0,4},{2,6},{4,0},{6,2},{8,12},{10,14},{12,8},{14,10},{1,5},{3,7},... | collective-permute-start | bytes 589832 | tf_op jit(solution)/shard_map/ppermute | solution.py:326
  22.0 5.0 %collective-permute-done.2.refs_2_ = bf16[4,96,256]{2,1,0:T(8,128)(2,1)S(1)} collective-permute-done((bf16[4,96,256]{2,1,0:T(8,128)(2,1)S(1)}, bf16[4,96,256]{2,1,0:T(8,128)(2,1)S(1)}, u32[]{:S(2)}, u32[]{:S(2)}) %collective-permute-start.2) | collective-permute-done | bytes 196640 | tf_op jit(solution)/shard_map/ppermute | solution.py:326
  27.0 0.6 %collective-permute-start.5 = (bf16[4,96,256]{2,1,0:T(8,128)(2,1)S(1)}, bf16[4,96,256]{2,1,0:T(8,128)(2,1)}, u32[]{:S(2)}, u32[]{:S(2)}) collective-permute-start(bf16[4,96,256]{2,1,0:T(8,128)(2,1)S(1)} %collective-permute-done.2.refs_2_), channel_id=1, source_target_pairs={{0,4},{2,6},{4,0},{6,2},{8,12},{10,14},{12,8},{14,10},{1,5},{3,7},... | collective-permute-start | bytes 589832 | tf_op jit(solution)/shard_map/ppermute | solution.py:326
  27.6 1.5 %collective-permute-start.3 = (bf16[4,96,256]{2,1,0:T(8,128)(2,1)S(1)}, bf16[4,96,256]{2,1,0:T(8,128)(2,1)}, u32[]{:S(2)}, u32[]{:S(2)}) collective-permute-start(bf16[4,96,256]{2,1,0:T(8,128)(2,1)S(1)} %collective-permute-done.2.refs_2_), channel_id=1, source_target_pairs={{0,16},{16,0},{1,17},{17,1},{2,18},{18,2},{3,19},{19,3},{4,20},{20... | collective-permute-start | bytes 589832 | tf_op jit(solution)/shard_map/ppermute | solution.py:326
  29.1 0.5 collective-permute-start.13
  29.6 0.5 collective-permute-start.7
  30.1 2.6 %collective-permute-done.5.refs_3_ = bf16[4,96,256]{2,1,0:T(8,128)(2,1)} collective-permute-done((bf16[4,96,256]{2,1,0:T(8,128)(2,1)S(1)}, bf16[4,96,256]{2,1,0:T(8,128)(2,1)}, u32[]{:S(2)}, u32[]{:S(2)}) %collective-permute-start.5) | collective-permute-done | bytes 196640 | tf_op jit(solution)/shard_map/ppermute | solution.py:326
  32.7 2.8 %collective-permute-done.3.refs_6_ = bf16[4,96,256]{2,1,0:T(8,128)(2,1)} collective-permute-done((bf16[4,96,256]{2,1,0:T(8,128)(2,1)S(1)}, bf16[4,96,256]{2,1,0:T(8,128)(2,1)}, u32[]{:S(2)}, u32[]{:S(2)}) %collective-permute-start.3) | collective-permute-done | bytes 196640 | tf_op jit(solution)/shard_map/ppermute | solution.py:326
  35.5 1.5 %collective-permute-start.8 = (bf16[4,96,256]{2,1,0:T(8,128)(2,1)}, bf16[4,96,256]{2,1,0:T(8,128)(2,1)}, u32[]{:S(2)}, u32[]{:S(2)}) collective-permute-start(bf16[4,96,256]{2,1,0:T(8,128)(2,1)} %collective-permute-done.5.refs_3_), channel_id=1, source_target_pairs={{0,16},{16,0},{1,17},{17,1},{2,18},{18,2},{3,19},{19,3},{4,20},{20... | collective-permute-start | bytes 589832 | tf_op jit(solution)/shard_map/ppermute | solution.py:326
  37.0 2.8 %shard_map.68 = (bf16[4,2048,128]{2,1,0:T(8,128)(2,1)S(1)}, bf16[512,128]{1,0:T(8,128)(2,1)S(1)}, bf16[512,512]{1,0:T(8,128)(2,1)S(1)}, s32[3,4]{1,0:T(4,128)S(1)}) custom-call(bf16[512,4,512]{2,1,0:T(4,128)(2,1)S(1)} %copy-done, s32[2,512]{1,0:T(2,128)S(1)} %bitcast.6), custom_call_target="tpu_custom_call" | custom-call | bytes 18000000 | tf_op jit(solution)/shard_map/pallas_call | solution.py:151
  39.9 0.5 collective-permute-start.15
  40.4 0.1 collective-permute-start.14
  40.5 0.5 collective-permute-start.12
  41.0 1.5 %collective-permute-done.8.refs_7_ = bf16[4,96,256]{2,1,0:T(8,128)(2,1)} collective-permute-done((bf16[4,96,256]{2,1,0:T(8,128)(2,1)}, bf16[4,96,256]{2,1,0:T(8,128)(2,1)}, u32[]{:S(2)}, u32[]{:S(2)}) %collective-permute-start.8) | collective-permute-done | bytes 196640 | tf_op jit(solution)/shard_map/ppermute | solution.py:326
  42.6 1.7 %collective-permute-done.16.refs_15_ = bf16[4,96,256]{2,1,0:T(8,128)(2,1)} collective-permute-done((bf16[4,96,256]{2,1,0:T(8,128)(2,1)}, bf16[4,96,256]{2,1,0:T(8,128)(2,1)}, u32[]{:S(2)}, u32[]{:S(2)}) %collective-permute-start.16) | collective-permute-done | bytes 196640 | tf_op jit(solution)/shard_map/ppermute | solution.py:326
  44.4 16.4 %shard_map.69 = bf16[512,4,512]{2,1,0:T(4,128)(2,1)} custom-call(s32[1]{0:T(128)} %bitcast.home_ref, s32[4]{0:T(128)S(1)} %copy-done.4, s32[3,4]{1,0:T(4,128)S(1)} %get-tuple-element.18.hull_ref, bf16[4,96,256]{2,1,0:T(8,128)(2,1)} %copy-done.1, bf16[4,96,256]{2,1,0:T(8,128)(2,1)} %copy-done.7, bf16[4,96,256]{2,1,0:T(8,128)(2,1)} %copy-done.5, ...), custom_call_target="tpu_custom_call" | custom-call | bytes 72000000 | tf_op jit(solution)/shard_map/pallas_call | solution.py:272
  (38 shorter events, 0.2 us)
Async XLA Ops:
  3.3 11.5 %collective-permute-start = (f32[96,512]{1,0:T(8,128)S(1)}, f32[96,512]{1,0:T(8,128)S(1)}, u32[]{:S(2)}, u32[]{:S(2)}) collective-permute-start(f32[96,512]{1,0:T(8,128)S(1)} %shard_map.65), channel_id=1, source_target_pairs={{0,1},{1,0},{2,3},{3,2},{4,5},{5,4},{6,7},{7,6},{8,9},{9,8},{10,11... | collective-permute-start | bytes 589832 | tf_op jit(solution)/shard_map/ppermute | solution.py:326
  9.7 6.4 %collective-permute-start.1 = (f32[96,512]{1,0:T(8,128)S(1)}, f32[96,512]{1,0:T(8,128)S(1)}, u32[]{:S(2)}, u32[]{:S(2)}) collective-permute-start(f32[96,512]{1,0:T(8,128)S(1)} %shard_map.66), channel_id=1, source_target_pairs={{0,1},{1,0},{2,3},{3,2},{4,5},{5,4},{6,7},{7,6},{8,9},{9,8},{10,11... | collective-permute-start | bytes 589832 | tf_op jit(solution)/shard_map/ppermute | solution.py:326
  9.8 27.2 %copy-start = (bf16[512,4,512]{2,1,0:T(4,128)(2,1)S(1)}, bf16[512,4,512]{2,1,0:T(4,128)(2,1)}, u32[]{:S(2)}) copy-start(bf16[512,4,512]{2,1,0:T(4,128)(2,1)} %q_ref.1) | copy-start | bytes 6291460
  9.8 27.2 %copy-start.2 = (s32[512,2]{0,1:T(2,128)S(1)}, s32[512,2]{0,1:T(2,128)}, u32[]{:S(2)}) copy-start(s32[512,2]{0,1:T(2,128)} %param.11) | copy-start | bytes 12292
  14.8 29.6 %copy-start.4 = (s32[4]{0:T(128)S(1)}, s32[4]{0:T(128)}, u32[]{:S(2)}) copy-start(s32[4]{0:T(128)} %tokens_ref.1) | copy-start | bytes 52
  16.3 28.1 %copy-start.1 = (bf16[4,96,256]{2,1,0:T(8,128)(2,1)}, bf16[4,96,256]{2,1,0:T(8,128)(2,1)S(1)}, u32[]{:S(2)}) copy-start(bf16[4,96,256]{2,1,0:T(8,128)(2,1)S(1)} %shard_map.67.refs_0_) | copy-start | bytes 589828
  16.3 10.7 %collective-permute-start.2 = (bf16[4,96,256]{2,1,0:T(8,128)(2,1)S(1)}, bf16[4,96,256]{2,1,0:T(8,128)(2,1)S(1)}, u32[]{:S(2)}, u32[]{:S(2)}) collective-permute-start(bf16[4,96,256]{2,1,0:T(8,128)(2,1)S(1)} %shard_map.67.refs_0_), channel_id=1, source_target_pairs={{0,8},{2,10},{4,12},{6,14},{8,0},{10,2},{12,4},{14,6},{1,9},{3,11}... | collective-permute-start | bytes 589832 | tf_op jit(solution)/shard_map/ppermute | solution.py:326
  18.9 10.1 %collective-permute-start.6 = (bf16[4,96,256]{2,1,0:T(8,128)(2,1)S(1)}, bf16[4,96,256]{2,1,0:T(8,128)(2,1)S(1)}, u32[]{:S(2)}, u32[]{:S(2)}) collective-permute-start(bf16[4,96,256]{2,1,0:T(8,128)(2,1)S(1)} %shard_map.67.refs_0_), channel_id=1, source_target_pairs={{0,16},{16,0},{1,17},{17,1},{2,18},{18,2},{3,19},{19,3},{4,20},{20... | collective-permute-start | bytes 589832 | tf_op jit(solution)/shard_map/ppermute | solution.py:326
  20.4 9.2 %collective-permute-start.4 = (bf16[4,96,256]{2,1,0:T(8,128)(2,1)S(1)}, bf16[4,96,256]{2,1,0:T(8,128)(2,1)S(1)}, u32[]{:S(2)}, u32[]{:S(2)}) collective-permute-start(bf16[4,96,256]{2,1,0:T(8,128)(2,1)S(1)} %shard_map.67.refs_0_), channel_id=1, source_target_pairs={{0,4},{2,6},{4,0},{6,2},{8,12},{10,14},{12,8},{14,10},{1,5},{3,7},... | collective-permute-start | bytes 589832 | tf_op jit(solution)/shard_map/ppermute | solution.py:326
  27.0 17.4 %copy-start.5 = (bf16[4,96,256]{2,1,0:T(8,128)(2,1)}, bf16[4,96,256]{2,1,0:T(8,128)(2,1)S(1)}, u32[]{:S(2)}) copy-start(bf16[4,96,256]{2,1,0:T(8,128)(2,1)S(1)} %collective-permute-done.2.refs_2_) | copy-start | bytes 589828
  27.0 5.8 %collective-permute-start.5 = (bf16[4,96,256]{2,1,0:T(8,128)(2,1)S(1)}, bf16[4,96,256]{2,1,0:T(8,128)(2,1)}, u32[]{:S(2)}, u32[]{:S(2)}) collective-permute-start(bf16[4,96,256]{2,1,0:T(8,128)(2,1)S(1)} %collective-permute-done.2.refs_2_), channel_id=1, source_target_pairs={{0,4},{2,6},{4,0},{6,2},{8,12},{10,14},{12,8},{14,10},{1,5},{3,7},... | collective-permute-start | bytes 589832 | tf_op jit(solution)/shard_map/ppermute | solution.py:326
  27.6 7.9 %collective-permute-start.3 = (bf16[4,96,256]{2,1,0:T(8,128)(2,1)S(1)}, bf16[4,96,256]{2,1,0:T(8,128)(2,1)}, u32[]{:S(2)}, u32[]{:S(2)}) collective-permute-start(bf16[4,96,256]{2,1,0:T(8,128)(2,1)S(1)} %collective-permute-done.2.refs_2_), channel_id=1, source_target_pairs={{0,16},{16,0},{1,17},{17,1},{2,18},{18,2},{3,19},{19,3},{4,20},{20... | collective-permute-start | bytes 589832 | tf_op jit(solution)/shard_map/ppermute | solution.py:326
  29.1 10.7 %collective-permute-start.9 = (bf16[4,96,256]{2,1,0:T(8,128)(2,1)S(1)}, bf16[4,96,256]{2,1,0:T(8,128)(2,1)S(1)}, u32[]{:S(2)}, u32[]{:S(2)}) collective-permute-start(bf16[4,96,256]{2,1,0:T(8,128)(2,1)S(1)} %shard_map.67.refs_0_), channel_id=1, source_target_pairs={{0,2},{2,0},{4,6},{6,4},{8,10},{10,8},{12,14},{14,12},{1,3},{3,1},... | collective-permute-start | bytes 589832 | tf_op jit(solution)/shard_map/ppermute | solution.py:326
  29.1 15.3 %copy-start.6 = (bf16[4,96,256]{2,1,0:T(8,128)(2,1)}, bf16[4,96,256]{2,1,0:T(8,128)(2,1)S(1)}, u32[]{:S(2)}) copy-start(bf16[4,96,256]{2,1,0:T(8,128)(2,1)S(1)} %collective-permute-done.6.refs_4_) | copy-start | bytes 589828
  29.1 10.8 %collective-permute-start.13 = (bf16[4,96,256]{2,1,0:T(8,128)(2,1)S(1)}, bf16[4,96,256]{2,1,0:T(8,128)(2,1)S(1)}, u32[]{:S(2)}, u32[]{:S(2)}) collective-permute-start(bf16[4,96,256]{2,1,0:T(8,128)(2,1)S(1)} %collective-permute-done.6.refs_4_), channel_id=1, source_target_pairs={{0,2},{2,0},{4,6},{6,4},{8,10},{10,8},{12,14},{14,12},{1,3},{3,1},... | collective-permute-start | bytes 589832 | tf_op jit(solution)/shard_map/ppermute | solution.py:326
  29.6 14.8 %copy-start.7 = (bf16[4,96,256]{2,1,0:T(8,128)(2,1)}, bf16[4,96,256]{2,1,0:T(8,128)(2,1)S(1)}, u32[]{:S(2)}) copy-start(bf16[4,96,256]{2,1,0:T(8,128)(2,1)S(1)} %collective-permute-done.4.refs_1_) | copy-start | bytes 589828
  29.6 10.8 %collective-permute-start.7 = (bf16[4,96,256]{2,1,0:T(8,128)(2,1)S(1)}, bf16[4,96,256]{2,1,0:T(8,128)(2,1)}, u32[]{:S(2)}, u32[]{:S(2)}) collective-permute-start(bf16[4,96,256]{2,1,0:T(8,128)(2,1)S(1)} %collective-permute-done.4.refs_1_), channel_id=1, source_target_pairs={{0,16},{16,0},{1,17},{17,1},{2,18},{18,2},{3,19},{19,3},{4,20},{20... | collective-permute-start | bytes 589832 | tf_op jit(solution)/shard_map/ppermute | solution.py:326
  32.7 7.8 %collective-permute-start.10 = (bf16[4,96,256]{2,1,0:T(8,128)(2,1)S(1)}, bf16[4,96,256]{2,1,0:T(8,128)(2,1)S(1)}, u32[]{:S(2)}, u32[]{:S(2)}) collective-permute-start(bf16[4,96,256]{2,1,0:T(8,128)(2,1)S(1)} %collective-permute-done.4.refs_1_), channel_id=1, source_target_pairs={{0,2},{2,0},{4,6},{6,4},{8,10},{10,8},{12,14},{14,12},{1,3},{3,1},... | collective-permute-start | bytes 589832 | tf_op jit(solution)/shard_map/ppermute | solution.py:326
  35.5 7.0 %collective-permute-start.8 = (bf16[4,96,256]{2,1,0:T(8,128)(2,1)}, bf16[4,96,256]{2,1,0:T(8,128)(2,1)}, u32[]{:S(2)}, u32[]{:S(2)}) collective-permute-start(bf16[4,96,256]{2,1,0:T(8,128)(2,1)} %collective-permute-done.5.refs_3_), channel_id=1, source_target_pairs={{0,16},{16,0},{1,17},{17,1},{2,18},{18,2},{3,19},{19,3},{4,20},{20... | collective-permute-start | bytes 589832 | tf_op jit(solution)/shard_map/ppermute | solution.py:326
  39.8 2.7 %collective-permute-start.11 = (bf16[4,96,256]{2,1,0:T(8,128)(2,1)S(1)}, bf16[4,96,256]{2,1,0:T(8,128)(2,1)}, u32[]{:S(2)}, u32[]{:S(2)}) collective-permute-start(bf16[4,96,256]{2,1,0:T(8,128)(2,1)S(1)} %collective-permute-done.2.refs_2_), channel_id=1, source_target_pairs={{0,2},{2,0},{4,6},{6,4},{8,10},{10,8},{12,14},{14,12},{1,3},{3,1},... | collective-permute-start | bytes 589832 | tf_op jit(solution)/shard_map/ppermute | solution.py:326
  39.9 2.7 %collective-permute-start.15 = (bf16[4,96,256]{2,1,0:T(8,128)(2,1)}, bf16[4,96,256]{2,1,0:T(8,128)(2,1)}, u32[]{:S(2)}, u32[]{:S(2)}) collective-permute-start(bf16[4,96,256]{2,1,0:T(8,128)(2,1)} %collective-permute-done.3.refs_6_), channel_id=1, source_target_pairs={{0,2},{2,0},{4,6},{6,4},{8,10},{10,8},{12,14},{14,12},{1,3},{3,1},... | collective-permute-start | bytes 589832 | tf_op jit(solution)/shard_map/ppermute | solution.py:326
  40.4 2.1 %collective-permute-start.14 = (bf16[4,96,256]{2,1,0:T(8,128)(2,1)}, bf16[4,96,256]{2,1,0:T(8,128)(2,1)}, u32[]{:S(2)}, u32[]{:S(2)}) collective-permute-start(bf16[4,96,256]{2,1,0:T(8,128)(2,1)} %collective-permute-done.7.refs_5_), channel_id=1, source_target_pairs={{0,2},{2,0},{4,6},{6,4},{8,10},{10,8},{12,14},{14,12},{1,3},{3,1},... | collective-permute-start | bytes 589832 | tf_op jit(solution)/shard_map/ppermute | solution.py:326
  40.5 2.1 %collective-permute-start.12 = (bf16[4,96,256]{2,1,0:T(8,128)(2,1)}, bf16[4,96,256]{2,1,0:T(8,128)(2,1)}, u32[]{:S(2)}, u32[]{:S(2)}) collective-permute-start(bf16[4,96,256]{2,1,0:T(8,128)(2,1)} %collective-permute-done.5.refs_3_), channel_id=1, source_target_pairs={{0,2},{2,0},{4,6},{6,4},{8,10},{10,8},{12,14},{14,12},{1,3},{3,1},... | collective-permute-start | bytes 589832 | tf_op jit(solution)/shard_map/ppermute | solution.py:326
  42.5 1.8 %collective-permute-start.16 = (bf16[4,96,256]{2,1,0:T(8,128)(2,1)}, bf16[4,96,256]{2,1,0:T(8,128)(2,1)}, u32[]{:S(2)}, u32[]{:S(2)}) collective-permute-start(bf16[4,96,256]{2,1,0:T(8,128)(2,1)} %collective-permute-done.8.refs_7_), channel_id=1, source_target_pairs={{0,2},{2,0},{4,6},{6,4},{8,10},{10,8},{12,14},{14,12},{1,3},{3,1},... | collective-permute-start | bytes 589832 | tf_op jit(solution)/shard_map/ppermute | solution.py:326
  (4 other events, 10.1 us)

commit v4 on v3

--- a/solution.py
+++ b/solution.py
@@ -8,7 +8,6 @@
 from jax.sharding import PartitionSpec as P
 
 MASKED = -1e30
-CHUNKS = 1
 HALVES = 2
 STORES = 2
 LOG2E = 1.4426950408889634
@@ -159,42 +158,30 @@
             jax.ShapeDtypeStruct((3, rows // BLOCK_ROWS), jnp.int32),
         ],
         compiler_params=pltpu.CompilerParams(vmem_limit_bytes=MIDDLE_VMEM),
-        cost_estimate=lasting(5),
+        cost_estimate=lasting(0.1),
     )(queries, text_tiles.T)
 
 
-def attend_kernel(shape, offsets, earlier, last, home_ref, tokens_ref, hull_ref, *refs):
-    heads, first_head, blocks, group, dim, tiles, tile_len = shape
+def attend_kernel(shape, offsets, home_ref, tokens_ref, hull_ref, *refs):
+    heads, blocks, group, dim, tiles, tile_len = shape
     pieces = len(offsets)
-    kv_refs, refs = refs[:pieces], refs[pieces:]
-    done_refs, refs = refs[:earlier], refs[earlier:]
-    q_hbm_ref, hidden_hbm_ref, back_hbm_ref, result_hbm_ref = refs[:4]
-    q_ref, hidden_ref, back_ref, done_ref, result_ref, k_ref, v_ref, turned_ref, sems, load_sems, store_sems = refs[4:]
-    piece_rows = kv_refs[0].shape[1]
+    piece_refs, refs = refs[:pieces], refs[pieces:]
+    q_ref, hidden_ref, back_ref, result_hbm_ref, kv_ref, off_ref, turned_ref, result_ref, load_sems, store_sems = refs
+    piece_rows = piece_refs[0].shape[1]
     columns = group * BLOCK_ROWS
     scale = LOG2E * dim ** (-0.5)
-    copies = []
+    loads = []
     for piece in range(pieces):
         at = pl.multiple_of((home_ref[0] ^ offsets[piece]) * piece_rows, piece_rows)
-        into = k_ref.at[:, pl.ds(at, piece_rows), pl.ds(0, dim)], v_ref.at[:, pl.ds(at, piece_rows), :]
-        for part in range(2):
-            source = kv_refs[piece].at[:, :, pl.ds(part * dim, dim)]
-            copies.append(pltpu.make_async_copy(source, into[part], sems.at[piece, part]))
-            copies[-1].start()
-    loads = [(q_hbm_ref.at[pl.ds(first_head, heads)], q_ref), (hidden_hbm_ref, hidden_ref), (back_hbm_ref, back_ref)]
-    loads += [(ref, done_ref.at[pl.ds(i * heads, heads)]) for i, ref in enumerate(done_refs)]
-    loads = [pltpu.make_async_copy(*ends, load_sems.at[i]) for i, ends in enumerate(loads)]
-    for load in loads:
-        load.start()
+        loads.append(pltpu.make_async_copy(piece_refs[piece], kv_ref.at[:, pl.ds(at, piece_rows), :], load_sems.at[piece]))
+        loads[-1].start()
     lanes = lax.broadcasted_iota(jnp.int32, (tile_len, dim), 1)
     place = lax.broadcasted_iota(jnp.int32, (tile_len, dim), 0)
     for tile in range(tiles):
         off = (lanes == tile) | ((lanes == tiles) & (place >= tokens_ref[tile]))
-        off = jnp.where(off, MASKED, 0.0).astype(jnp.bfloat16)
-        for head in range(heads):
-            k_ref[head, tile * tile_len : (tile + 1) * tile_len, dim:] = off
-    for copy in [*copies, *loads[:2]]:
-        copy.wait()
+        off_ref[tile * tile_len : (tile + 1) * tile_len, :] = jnp.where(off, MASKED, 0.0).astype(jnp.bfloat16)
+    for load in loads:
+        load.wait()
 
     def work(block, first, count):
         here = pl.ds(pl.multiple_of(block * BLOCK_ROWS, BLOCK_ROWS), BLOCK_ROWS)
@@ -204,10 +191,11 @@
         rows = pl.ds(pl.multiple_of(block * columns, columns), columns)
         span = pl.ds(pl.multiple_of(first * tile_len, tile_len), count * tile_len)
         hidden = jnp.concatenate([hidden_ref[here, :]] * group, axis=0)
+        off = off_ref[span, :]
         row = lax.broadcasted_iota(jnp.int32, (1, columns), 1) % BLOCK_ROWS + block * BLOCK_ROWS
         scores = [
             lax.dot_general(
-                k_ref[head, span, :],
+                jnp.concatenate([kv_ref[head, span, :dim], off], axis=1),
                 jnp.concatenate([q_ref[head, rows, :], hidden], axis=1),
                 ROWS_BY_ROWS,
                 preferred_element_type=jnp.float32,
@@ -217,11 +205,11 @@
         for head in range(heads):
             row_max = jnp.max(scores[head], axis=0, keepdims=True)
             terms = jnp.exp2((scores[head] - row_max) * scale)
-            denominator = jnp.sum(terms, axis=0, keepdims=True)
+            total = jnp.sum(terms, axis=0, keepdims=True)
             summed = lax.dot_general(
-                v_ref[head, span, :], terms.astype(jnp.bfloat16), COLS_BY_COLS, preferred_element_type=jnp.float32
+                kv_ref[head, span, dim:], terms.astype(jnp.bfloat16), COLS_BY_COLS, preferred_element_type=jnp.float32
             )
-            inverse = jnp.where(row >= hull_ref[2, 0], 1.0 / denominator, 0.0)
+            inverse = jnp.where(row >= hull_ref[2, 0], 1.0 / total, 0.0)
             attended = (summed * inverse).astype(jnp.bfloat16)
             for member in range(group):
                 turned_ref[head, member * dim : (member + 1) * dim, here] = attended[
@@ -238,58 +226,47 @@
             def _():
                 work(block, first, count)
 
-    for load in loads[2:]:
-        load.wait()
-    if not last:
-        store = pltpu.make_async_copy(turned_ref, result_hbm_ref, store_sems.at[0])
-        store.start()
-        store.wait()
-        return
     stores = []
     rows = back_ref.shape[0] // STORES
     for part in range(STORES):
         here = pl.ds(part * rows, rows)
         back = back_ref[here, :]
         whole = [
-            lax.dot_general(back, turned, ROWS_BY_ROWS, preferred_element_type=jnp.float32).astype(jnp.bfloat16)
-            for turned in [done_ref[i] for i in range(first_head)] + [turned_ref[head] for head in range(heads)]
+            lax.dot_general(back, turned_ref[head], ROWS_BY_ROWS, preferred_element_type=jnp.float32)
+            for head in range(heads)
         ]
-        result_ref[here] = jnp.transpose(jnp.stack(whole, axis=0), (1, 0, 2))
+        whole = jnp.stack([head.astype(jnp.bfloat16) for head in whole], axis=0)
+        result_ref[here] = jnp.transpose(whole, (1, 0, 2))
         stores.append(pltpu.make_async_copy(result_ref.at[here], result_hbm_ref.at[here], store_sems.at[part]))
         stores[-1].start()
     for store in stores:
         store.wait()
 
 
-def attend(text, first, kv, offsets, home, tokens, tile_len, done, last):
+def attend(text, kv, offsets, home, tokens, tile_len):
     q, hidden, back, hull = text
     heads, dim = kv[0].shape[0], kv[0].shape[2] // 2
     text_rows, blocks = back.shape[0], hull.shape[1]
     group, tiles = q.shape[1] // text_rows, tokens.shape[0]
     width = group * dim
     total = sum(piece.shape[1] for piece in kv)
-    whole = (text_rows, q.shape[0], width) if last else (heads, width, text_rows)
+    kv = [pltpu.with_memory_space_constraint(piece, pltpu.HBM) for piece in kv]
     return pl.pallas_call(
-        functools.partial(attend_kernel, (heads, first, blocks, group, dim, tiles, tile_len), offsets, len(done), last),
-        in_specs=[SMEM] * 3 + [ANY] * len(kv) + [HBM] * (len(done) + 3),
+        functools.partial(attend_kernel, (heads, blocks, group, dim, tiles, tile_len), offsets),
+        in_specs=[SMEM] * 3 + [ANY] * len(kv) + [VMEM] * 3,
         out_specs=ANY,
-        out_shape=jax.ShapeDtypeStruct(whole, jnp.bfloat16),
+        out_shape=jax.ShapeDtypeStruct((text_rows, heads, width), jnp.bfloat16),
         scratch_shapes=[
-            pltpu.VMEM((heads, *q.shape[1:]), jnp.bfloat16),
-            pltpu.VMEM(hidden.shape, jnp.bfloat16),
-            pltpu.VMEM(back.shape, jnp.bfloat16),
-            pltpu.VMEM((max(first, 1), width, text_rows), jnp.bfloat16),
-            pltpu.VMEM((text_rows, q.shape[0], width) if last else (8, 128), jnp.bfloat16),
             pltpu.VMEM((heads, total, 2 * dim), jnp.bfloat16),
-            pltpu.VMEM((heads, total, dim), jnp.bfloat16),
+            pltpu.VMEM((total, dim), jnp.bfloat16),
             pltpu.VMEM((heads, width, text_rows), jnp.bfloat16),
-            pltpu.SemaphoreType.DMA((len(kv), 2)),
-            pltpu.SemaphoreType.DMA((3 + len(done),)),
+            pltpu.VMEM((text_rows, heads, width), jnp.bfloat16),
+            pltpu.SemaphoreType.DMA((len(kv),)),
             pltpu.SemaphoreType.DMA((STORES,)),
         ],
         compiler_params=pltpu.CompilerParams(vmem_limit_bytes=MIDDLE_VMEM),
-        cost_estimate=lasting(5 * heads),
-    )(home.reshape(1), tokens, hull, *(pltpu.with_memory_space_constraint(piece, pltpu.HBM) for piece in kv), *done, q, hidden, back)
+        cost_estimate=lasting(15),
+    )(home.reshape(1), tokens, hull, *kv, q, hidden, back)
 
 
 def shards(vision_states, kv_weight, key_gain, queries, tile_tokens, text_tiles):
@@ -299,8 +276,8 @@
     heads = all_heads // tensor
     tiles = tile_tokens.shape[0]
     tile_len = vision_states.shape[0] * segment * seq // tiles
-    if tensor == 2 and segment == 2 and seq == 8 and heads % CHUNKS == 0:
-        return by_chunks(vision_states, kv_weight, key_gain, queries, tile_tokens, text_tiles, heads, tile_len)
+    if tensor == 2 and segment == 2 and seq == 8 and heads % HALVES == 0:
+        return by_swaps(vision_states, kv_weight, key_gain, queries, tile_tokens, text_tiles, heads, tile_len)
     text = sort_rows(queries, text_tiles, tiles, dim)
     weight_heads = kv_weight.reshape(kv_weight.shape[0], all_heads, 2 * dim)
     partial = jnp.einsum("rd,dch->crh", vision_states, weight_heads, preferred_element_type=jnp.float32)
@@ -310,17 +287,16 @@
     keys = keys * lax.rsqrt(mean_sq + 1e-05) * key_gain
     block = jnp.concatenate([keys, sums[:, :, dim:]], axis=-1).astype(jnp.bfloat16)
     kv = [lax.all_gather(block, ("segment", "seq"), axis=1, tiled=True)]
-    return attend(text, 0, kv, [0], jnp.int32(0), tile_tokens, tile_len, [], True)
+    return attend(text, kv, [0], jnp.int32(0), tile_tokens, tile_len)
 
 
 def after(first, then):
     return lax.optimization_barrier((first, then))[1]
 
 
-def by_chunks(vision_states, kv_weight, key_gain, queries, tile_tokens, text_tiles, heads, tile_len):
+def by_swaps(vision_states, kv_weight, key_gain, queries, tile_tokens, text_tiles, heads, tile_len):
     dim = key_gain.shape[0]
     me_tensor, me_segment, me_seq = lax.axis_index("tensor"), lax.axis_index("segment"), lax.axis_index("seq")
-    count = heads // CHUNKS
 
     def across(array, axis, step):
         return lax.ppermute(array, axis, [(i, i ^ step) for i in range(lax.axis_size(axis))])
@@ -335,20 +311,14 @@
     theirs = [parts(HALVES, other * HALVES + half)[0] for half in range(HALVES)]
     arrived = [across(half, "tensor", 1) for half in theirs]
     (mine,) = parts(1, me_tensor)
-    blocks = [finish(mine, arrived, key_gain, count, dim)]
-    done = []
-    for chunk, block in enumerate(blocks):
-        last = chunk == CHUNKS - 1
-        near, far = across(block, "seq", 2), across(block, "seq", 4)
-        lane = [block, near, far, across(far, "seq", 2)]
-        lane += [across(piece, "segment", 1) for piece in lane]
-        if chunk == 0:
-            lane[-2], text = lax.optimization_barrier((lane[-2], text))
-        if done:
-            lane[-1] = after(done[-1], lane[-1])
-        kv = lane + [across(piece, "seq", 1) for piece in lane]
-        done.append(attend(text, chunk * count, kv, offsets, home, tile_tokens, tile_len, done if last else [], last))
-    return done[-1]
+    block = finish(mine, arrived, key_gain, heads, dim)
+    near, far, side = across(block, "seq", 2), across(block, "seq", 4), across(block, "segment", 1)
+    far_near, side_far = across(far, "seq", 2), across(far, "segment", 1)
+    side_near = across(after(far_near, side), "seq", 2)
+    side_far, text = lax.optimization_barrier((side_far, text))
+    lane = [block, near, far, far_near, side, side_near, side_far, across(far_near, "segment", 1)]
+    kv = lane + [across(piece, "seq", 1) for piece in lane]
+    return attend(text, kv, offsets, home, tile_tokens, tile_len)
 
 
 def solution(mesh):

time: 61.1 us -> 58.6 us (0.959)
  waiting for transfers between devices: 15 us -> 11.8 us
  starting transfers between devices: 14.7 us -> 15.7 us
    ppermute x17, waiting for transfers between devices: 15 us -> 11.8 us  [across(): lax.ppermute(array, axis, [(i, i ^ step) for i in range(lax.axis_size(axi...]
    ppermute x17, starting transfers between devices: 14.7 us -> 15.7 us  [across(): lax.ppermute(array, axis, [(i, i ^ step) for i in range(lax.axis_size(axi...]
  transfers between devices with their start and end apart: 17 -> 17, of which waited for: 6 -> 7; matrix products, arithmetic and copies ran while one was open for 0% -> 0% of each run, Pallas kernels for 18% -> 19%
where the time goes in v4:
time: 58.6 us; the launch traced here: 58.3 us
  Pallas kernels  30.4 us (52%)
  starting transfers between devices  15.7 us (27%)
  waiting for transfers between devices  11.8 us (20%)
    pallas_call x1, Pallas kernels, attend(): pl.pallas_call(functools.partial(attend_kernel, (heads, blocks, group, di...  16 us
    ppermute x17, starting transfers between devices, across(): lax.ppermute(array, axis, [(i, i ^ step) for i in range(lax.axis_size(axi...  15.7 us
    ppermute x17, waiting for transfers between devices, across(): lax.ppermute(array, axis, [(i, i ^ step) for i in range(lax.axis_size(axi...  11.8 us
    pallas_call x3, Pallas kernels, project(): pl.pallas_call(functools.partial(project_kernel, pieces), in_specs=[SMEM,...  11.5 us
    pallas_call x1, Pallas kernels, sort_rows(): pl.pallas_call(functools.partial(sort_kernel, tiles, group), in_specs=[VM...  2.78 us
  transfers between devices with their start and end apart: 17, of which 7 were waited for; matrix products, arithmetic and copies ran while one was open for 0% of the time, Pallas kernels for 19%

profile of v4, /device:TPU:0, one launch (start us, length us, event | category | flops | bytes accessed | tf_op | source)
XLA Modules:
  0.0 58.3 jit_solution(16512683558612362256)
XLA Ops:
  0.0 3.3 %shard_map.65 = f32[96,512]{1,0:T(8,128)S(1)} custom-call(s32[1]{0:T(128)} %bitcast.2.block_ref, bf16[96,3840]{1,0:T(8,128)(2,1)} %vision_hbm_ref.5, bf16[3840,2048]{1,0:T(8,128)(2,1)} %weight_ref.5), custom_call_target="tpu_custom_call" | custom-call | bytes 11520000 | tf_op jit(solution)/shard_map/pallas_call | solution.py:64
  3.3 3.1 %collective-permute-start = (f32[96,512]{1,0:T(8,128)S(1)}, f32[96,512]{1,0:T(8,128)S(1)}, u32[]{:S(2)}, u32[]{:S(2)}) collective-permute-start(f32[96,512]{1,0:T(8,128)S(1)} %shard_map.65), channel_id=1, source_target_pairs={{0,1},{1,0},{2,3},{3,2},{4,5},{5,4},{6,7},{7,6},{8,9},{9,8},{10,11... | collective-permute-start | bytes 589832 | tf_op jit(solution)/shard_map/ppermute | solution.py:302
  6.4 3.3 %shard_map.66 = f32[96,512]{1,0:T(8,128)S(1)} custom-call(s32[1]{0:T(128)} %bitcast.3.block_ref, bf16[96,3840]{1,0:T(8,128)(2,1)} %vision_hbm_ref.5, bf16[3840,2048]{1,0:T(8,128)(2,1)} %weight_ref.5), custom_call_target="tpu_custom_call" | custom-call | bytes 11520000 | tf_op jit(solution)/shard_map/pallas_call | solution.py:64
  9.8 5.0 %shard_map.64.own_ref = f32[96,1024]{1,0:T(8,128)S(1)} custom-call(s32[1]{0:T(128)} %bitcast.1.block_ref, bf16[96,3840]{1,0:T(8,128)(2,1)} %vision_hbm_ref.5, bf16[3840,2048]{1,0:T(8,128)(2,1)} %weight_ref.5), custom_call_target="tpu_custom_call" | custom-call | bytes 11520000 | tf_op jit(solution)/shard_map/pallas_call | solution.py:64
  14.8 1.3 %collective-permute-done.1.refs_1_ = f32[96,512]{1,0:T(8,128)S(1)} collective-permute-done((f32[96,512]{1,0:T(8,128)S(1)}, f32[96,512]{1,0:T(8,128)S(1)}, u32[]{:S(2)}, u32[]{:S(2)}) %collective-permute-start.1) | collective-permute-done | bytes 196640 | tf_op jit(solution)/shard_map/ppermute | solution.py:302
  16.1 0.2 shard_map.67.refs_0_
  16.3 2.7 %collective-permute-start.2 = (bf16[4,96,256]{2,1,0:T(8,128)(2,1)S(1)}, bf16[4,96,256]{2,1,0:T(8,128)(2,1)S(1)}, u32[]{:S(2)}, u32[]{:S(2)}) collective-permute-start(bf16[4,96,256]{2,1,0:T(8,128)(2,1)S(1)} %shard_map.67.refs_0_), channel_id=1, source_target_pairs={{0,8},{2,10},{4,12},{6,14},{8,0},{10,2},{12,4},{14,6},{1,9},{3,11}... | collective-permute-start | bytes 589832 | tf_op jit(solution)/shard_map/ppermute | solution.py:302
  18.9 1.5 %collective-permute-start.6 = (bf16[4,96,256]{2,1,0:T(8,128)(2,1)S(1)}, bf16[4,96,256]{2,1,0:T(8,128)(2,1)S(1)}, u32[]{:S(2)}, u32[]{:S(2)}) collective-permute-start(bf16[4,96,256]{2,1,0:T(8,128)(2,1)S(1)} %shard_map.67.refs_0_), channel_id=1, source_target_pairs={{0,16},{16,0},{1,17},{17,1},{2,18},{18,2},{3,19},{19,3},{4,20},{20... | collective-permute-start | bytes 589832 | tf_op jit(solution)/shard_map/ppermute | solution.py:302
  20.4 1.6 %collective-permute-start.4 = (bf16[4,96,256]{2,1,0:T(8,128)(2,1)S(1)}, bf16[4,96,256]{2,1,0:T(8,128)(2,1)S(1)}, u32[]{:S(2)}, u32[]{:S(2)}) collective-permute-start(bf16[4,96,256]{2,1,0:T(8,128)(2,1)S(1)} %shard_map.67.refs_0_), channel_id=1, source_target_pairs={{0,4},{2,6},{4,0},{6,2},{8,12},{10,14},{12,8},{14,10},{1,5},{3,7},... | collective-permute-start | bytes 589832 | tf_op jit(solution)/shard_map/ppermute | solution.py:302
  22.0 5.0 %collective-permute-done.2.refs_2_ = bf16[4,96,256]{2,1,0:T(8,128)(2,1)S(1)} collective-permute-done((bf16[4,96,256]{2,1,0:T(8,128)(2,1)S(1)}, bf16[4,96,256]{2,1,0:T(8,128)(2,1)S(1)}, u32[]{:S(2)}, u32[]{:S(2)}) %collective-permute-start.2) | collective-permute-done | bytes 196640 | tf_op jit(solution)/shard_map/ppermute | solution.py:302
  27.0 0.6 %collective-permute-start.5 = (bf16[4,96,256]{2,1,0:T(8,128)(2,1)S(1)}, bf16[4,96,256]{2,1,0:T(8,128)(2,1)}, u32[]{:S(2)}, u32[]{:S(2)}) collective-permute-start(bf16[4,96,256]{2,1,0:T(8,128)(2,1)S(1)} %collective-permute-done.2.refs_2_), channel_id=1, source_target_pairs={{0,4},{2,6},{4,0},{6,2},{8,12},{10,14},{12,8},{14,10},{1,5},{3,7},... | collective-permute-start | bytes 589832 | tf_op jit(solution)/shard_map/ppermute | solution.py:302
  27.6 1.5 %collective-permute-start.3 = (bf16[4,96,256]{2,1,0:T(8,128)(2,1)S(1)}, bf16[4,96,256]{2,1,0:T(8,128)(2,1)}, u32[]{:S(2)}, u32[]{:S(2)}) collective-permute-start(bf16[4,96,256]{2,1,0:T(8,128)(2,1)S(1)} %collective-permute-done.2.refs_2_), channel_id=1, source_target_pairs={{0,16},{16,0},{1,17},{17,1},{2,18},{18,2},{3,19},{19,3},{4,20},{20... | collective-permute-start | bytes 589832 | tf_op jit(solution)/shard_map/ppermute | solution.py:302
  29.1 0.5 collective-permute-start.13
  29.7 3.1 %collective-permute-done.5.refs_3_ = bf16[4,96,256]{2,1,0:T(8,128)(2,1)} collective-permute-done((bf16[4,96,256]{2,1,0:T(8,128)(2,1)S(1)}, bf16[4,96,256]{2,1,0:T(8,128)(2,1)}, u32[]{:S(2)}, u32[]{:S(2)}) %collective-permute-start.5) | collective-permute-done | bytes 196640 | tf_op jit(solution)/shard_map/ppermute | solution.py:302
  32.7 1.7 %collective-permute-start.7 = (bf16[4,96,256]{2,1,0:T(8,128)(2,1)S(1)}, bf16[4,96,256]{2,1,0:T(8,128)(2,1)}, u32[]{:S(2)}, u32[]{:S(2)}) collective-permute-start(bf16[4,96,256]{2,1,0:T(8,128)(2,1)S(1)} %collective-permute-done.6.refs_4_), channel_id=1, source_target_pairs={{0,4},{2,6},{4,0},{6,2},{8,12},{10,14},{12,8},{14,10},{1,5},{3,7},... | collective-permute-start | bytes 589832 | tf_op jit(solution)/shard_map/ppermute | solution.py:302
  34.4 1.4 %collective-permute-start.8 = (bf16[4,96,256]{2,1,0:T(8,128)(2,1)}, bf16[4,96,256]{2,1,0:T(8,128)(2,1)}, u32[]{:S(2)}, u32[]{:S(2)}) collective-permute-start(bf16[4,96,256]{2,1,0:T(8,128)(2,1)} %collective-permute-done.5.refs_3_), channel_id=1, source_target_pairs={{0,16},{16,0},{1,17},{17,1},{2,18},{18,2},{3,19},{19,3},{4,20},{20... | collective-permute-start | bytes 589832 | tf_op jit(solution)/shard_map/ppermute | solution.py:302
  35.8 2.8 %shard_map.68 = (bf16[4,2048,128]{2,1,0:T(8,128)(2,1)S(1)}, bf16[512,128]{1,0:T(8,128)(2,1)S(1)}, bf16[512,512]{1,0:T(8,128)(2,1)S(1)}, s32[3,4]{1,0:T(4,128)S(1)}) custom-call(bf16[512,4,512]{2,1,0:T(4,128)(2,1)S(1)} %copy-done, s32[2,512]{1,0:T(2,128)S(1)} %bitcast.6), custom_call_target="tpu_custom_call" | custom-call | bytes 360000 | tf_op jit(solution)/shard_map/pallas_call | solution.py:150
  38.7 0.5 collective-permute-start.15
  39.3 0.4 collective-permute-start.14
  39.7 0.7 %collective-permute-done.8.refs_7_ = bf16[4,96,256]{2,1,0:T(8,128)(2,1)} collective-permute-done((bf16[4,96,256]{2,1,0:T(8,128)(2,1)}, bf16[4,96,256]{2,1,0:T(8,128)(2,1)}, u32[]{:S(2)}, u32[]{:S(2)}) %collective-permute-start.8) | collective-permute-done | bytes 196640 | tf_op jit(solution)/shard_map/ppermute | solution.py:302
  40.4 0.6 %collective-permute-done.12.refs_11_ = bf16[4,96,256]{2,1,0:T(8,128)(2,1)} collective-permute-done((bf16[4,96,256]{2,1,0:T(8,128)(2,1)}, bf16[4,96,256]{2,1,0:T(8,128)(2,1)}, u32[]{:S(2)}, u32[]{:S(2)}) %collective-permute-start.12) | collective-permute-done | bytes 196640 | tf_op jit(solution)/shard_map/ppermute | solution.py:302
  41.0 0.3 collective-permute-done.14.refs_13_
  41.3 0.9 %collective-permute-done.16.refs_15_ = bf16[4,96,256]{2,1,0:T(8,128)(2,1)} collective-permute-done((bf16[4,96,256]{2,1,0:T(8,128)(2,1)}, bf16[4,96,256]{2,1,0:T(8,128)(2,1)}, u32[]{:S(2)}, u32[]{:S(2)}) %collective-permute-start.16) | collective-permute-done | bytes 196640 | tf_op jit(solution)/shard_map/ppermute | solution.py:302
  42.2 16.0 %shard_map.69 = bf16[512,4,512]{2,1,0:T(4,128)(2,1)} custom-call(s32[1]{0:T(128)} %bitcast.home_ref, s32[4]{0:T(128)S(1)} %copy-done.4, s32[3,4]{1,0:T(4,128)S(1)} %get-tuple-element.19.hull_ref, bf16[4,96,256]{2,1,0:T(8,128)(2,1)} %copy-done.1, bf16[4,96,256]{2,1,0:T(8,128)(2,1)} %copy-done.7, bf16[4,96,256]{2,1,0:T(8,128)(2,1)} %copy-done.5, ...), custom_call_target="tpu_custom_call" | custom-call | bytes 54000000 | tf_op jit(solution)/shard_map/pallas_call | solution.py:254
  (38 shorter events, 0.4 us)
Async XLA Ops:
  3.3 11.5 %collective-permute-start = (f32[96,512]{1,0:T(8,128)S(1)}, f32[96,512]{1,0:T(8,128)S(1)}, u32[]{:S(2)}, u32[]{:S(2)}) collective-permute-start(f32[96,512]{1,0:T(8,128)S(1)} %shard_map.65), channel_id=1, source_target_pairs={{0,1},{1,0},{2,3},{3,2},{4,5},{5,4},{6,7},{7,6},{8,9},{9,8},{10,11... | collective-permute-start | bytes 589832 | tf_op jit(solution)/shard_map/ppermute | solution.py:302
  9.7 6.4 %collective-permute-start.1 = (f32[96,512]{1,0:T(8,128)S(1)}, f32[96,512]{1,0:T(8,128)S(1)}, u32[]{:S(2)}, u32[]{:S(2)}) collective-permute-start(f32[96,512]{1,0:T(8,128)S(1)} %shard_map.66), channel_id=1, source_target_pairs={{0,1},{1,0},{2,3},{3,2},{4,5},{5,4},{6,7},{7,6},{8,9},{9,8},{10,11... | collective-permute-start | bytes 589832 | tf_op jit(solution)/shard_map/ppermute | solution.py:302
  9.8 26.0 %copy-start = (bf16[512,4,512]{2,1,0:T(4,128)(2,1)S(1)}, bf16[512,4,512]{2,1,0:T(4,128)(2,1)}, u32[]{:S(2)}) copy-start(bf16[512,4,512]{2,1,0:T(4,128)(2,1)} %q_ref.1) | copy-start | bytes 6291460
  9.8 26.0 %copy-start.2 = (s32[512,2]{0,1:T(2,128)S(1)}, s32[512,2]{0,1:T(2,128)}, u32[]{:S(2)}) copy-start(s32[512,2]{0,1:T(2,128)} %param.11) | copy-start | bytes 12292
  14.8 27.4 %copy-start.4 = (s32[4]{0:T(128)S(1)}, s32[4]{0:T(128)}, u32[]{:S(2)}) copy-start(s32[4]{0:T(128)} %tokens_ref.1) | copy-start | bytes 52
  16.3 25.9 %copy-start.1 = (bf16[4,96,256]{2,1,0:T(8,128)(2,1)}, bf16[4,96,256]{2,1,0:T(8,128)(2,1)S(1)}, u32[]{:S(2)}) copy-start(bf16[4,96,256]{2,1,0:T(8,128)(2,1)S(1)} %shard_map.67.refs_0_) | copy-start | bytes 589828
  16.3 10.7 %collective-permute-start.2 = (bf16[4,96,256]{2,1,0:T(8,128)(2,1)S(1)}, bf16[4,96,256]{2,1,0:T(8,128)(2,1)S(1)}, u32[]{:S(2)}, u32[]{:S(2)}) collective-permute-start(bf16[4,96,256]{2,1,0:T(8,128)(2,1)S(1)} %shard_map.67.refs_0_), channel_id=1, source_target_pairs={{0,8},{2,10},{4,12},{6,14},{8,0},{10,2},{12,4},{14,6},{1,9},{3,11}... | collective-permute-start | bytes 589832 | tf_op jit(solution)/shard_map/ppermute | solution.py:302
  18.9 10.1 %collective-permute-start.6 = (bf16[4,96,256]{2,1,0:T(8,128)(2,1)S(1)}, bf16[4,96,256]{2,1,0:T(8,128)(2,1)S(1)}, u32[]{:S(2)}, u32[]{:S(2)}) collective-permute-start(bf16[4,96,256]{2,1,0:T(8,128)(2,1)S(1)} %shard_map.67.refs_0_), channel_id=1, source_target_pairs={{0,16},{16,0},{1,17},{17,1},{2,18},{18,2},{3,19},{19,3},{4,20},{20... | collective-permute-start | bytes 589832 | tf_op jit(solution)/shard_map/ppermute | solution.py:302
  20.4 9.2 %collective-permute-start.4 = (bf16[4,96,256]{2,1,0:T(8,128)(2,1)S(1)}, bf16[4,96,256]{2,1,0:T(8,128)(2,1)S(1)}, u32[]{:S(2)}, u32[]{:S(2)}) collective-permute-start(bf16[4,96,256]{2,1,0:T(8,128)(2,1)S(1)} %shard_map.67.refs_0_), channel_id=1, source_target_pairs={{0,4},{2,6},{4,0},{6,2},{8,12},{10,14},{12,8},{14,10},{1,5},{3,7},... | collective-permute-start | bytes 589832 | tf_op jit(solution)/shard_map/ppermute | solution.py:302
  27.0 15.2 %copy-start.5 = (bf16[4,96,256]{2,1,0:T(8,128)(2,1)}, bf16[4,96,256]{2,1,0:T(8,128)(2,1)S(1)}, u32[]{:S(2)}) copy-start(bf16[4,96,256]{2,1,0:T(8,128)(2,1)S(1)} %collective-permute-done.2.refs_2_) | copy-start | bytes 589828
  27.0 5.8 %collective-permute-start.5 = (bf16[4,96,256]{2,1,0:T(8,128)(2,1)S(1)}, bf16[4,96,256]{2,1,0:T(8,128)(2,1)}, u32[]{:S(2)}, u32[]{:S(2)}) collective-permute-start(bf16[4,96,256]{2,1,0:T(8,128)(2,1)S(1)} %collective-permute-done.2.refs_2_), channel_id=1, source_target_pairs={{0,4},{2,6},{4,0},{6,2},{8,12},{10,14},{12,8},{14,10},{1,5},{3,7},... | collective-permute-start | bytes 589832 | tf_op jit(solution)/shard_map/ppermute | solution.py:302
  27.6 6.8 %collective-permute-start.3 = (bf16[4,96,256]{2,1,0:T(8,128)(2,1)S(1)}, bf16[4,96,256]{2,1,0:T(8,128)(2,1)}, u32[]{:S(2)}, u32[]{:S(2)}) collective-permute-start(bf16[4,96,256]{2,1,0:T(8,128)(2,1)S(1)} %collective-permute-done.2.refs_2_), channel_id=1, source_target_pairs={{0,16},{16,0},{1,17},{17,1},{2,18},{18,2},{3,19},{19,3},{4,20},{20... | collective-permute-start | bytes 589832 | tf_op jit(solution)/shard_map/ppermute | solution.py:302
  29.1 9.5 %collective-permute-start.9 = (bf16[4,96,256]{2,1,0:T(8,128)(2,1)S(1)}, bf16[4,96,256]{2,1,0:T(8,128)(2,1)S(1)}, u32[]{:S(2)}, u32[]{:S(2)}) collective-permute-start(bf16[4,96,256]{2,1,0:T(8,128)(2,1)S(1)} %shard_map.67.refs_0_), channel_id=1, source_target_pairs={{0,2},{2,0},{4,6},{6,4},{8,10},{10,8},{12,14},{14,12},{1,3},{3,1},... | collective-permute-start | bytes 589832 | tf_op jit(solution)/shard_map/ppermute | solution.py:302
  29.1 13.1 %copy-start.6 = (bf16[4,96,256]{2,1,0:T(8,128)(2,1)}, bf16[4,96,256]{2,1,0:T(8,128)(2,1)S(1)}, u32[]{:S(2)}) copy-start(bf16[4,96,256]{2,1,0:T(8,128)(2,1)S(1)} %collective-permute-done.6.refs_4_) | copy-start | bytes 589828
  29.1 9.6 %collective-permute-start.13 = (bf16[4,96,256]{2,1,0:T(8,128)(2,1)S(1)}, bf16[4,96,256]{2,1,0:T(8,128)(2,1)S(1)}, u32[]{:S(2)}, u32[]{:S(2)}) collective-permute-start(bf16[4,96,256]{2,1,0:T(8,128)(2,1)S(1)} %collective-permute-done.6.refs_4_), channel_id=1, source_target_pairs={{0,2},{2,0},{4,6},{6,4},{8,10},{10,8},{12,14},{14,12},{1,3},{3,1},... | collective-permute-start | bytes 589832 | tf_op jit(solution)/shard_map/ppermute | solution.py:302
  29.6 12.6 %copy-start.7 = (bf16[4,96,256]{2,1,0:T(8,128)(2,1)}, bf16[4,96,256]{2,1,0:T(8,128)(2,1)S(1)}, u32[]{:S(2)}) copy-start(bf16[4,96,256]{2,1,0:T(8,128)(2,1)S(1)} %collective-permute-done.4.refs_1_) | copy-start | bytes 589828
  29.6 9.6 %collective-permute-start.10 = (bf16[4,96,256]{2,1,0:T(8,128)(2,1)S(1)}, bf16[4,96,256]{2,1,0:T(8,128)(2,1)S(1)}, u32[]{:S(2)}, u32[]{:S(2)}) collective-permute-start(bf16[4,96,256]{2,1,0:T(8,128)(2,1)S(1)} %collective-permute-done.4.refs_1_), channel_id=1, source_target_pairs={{0,2},{2,0},{4,6},{6,4},{8,10},{10,8},{12,14},{14,12},{1,3},{3,1},... | collective-permute-start | bytes 589832 | tf_op jit(solution)/shard_map/ppermute | solution.py:302
  32.7 6.5 %collective-permute-start.7 = (bf16[4,96,256]{2,1,0:T(8,128)(2,1)S(1)}, bf16[4,96,256]{2,1,0:T(8,128)(2,1)}, u32[]{:S(2)}, u32[]{:S(2)}) collective-permute-start(bf16[4,96,256]{2,1,0:T(8,128)(2,1)S(1)} %collective-permute-done.6.refs_4_), channel_id=1, source_target_pairs={{0,4},{2,6},{4,0},{6,2},{8,12},{10,14},{12,8},{14,10},{1,5},{3,7},... | collective-permute-start | bytes 589832 | tf_op jit(solution)/shard_map/ppermute | solution.py:302
  34.4 6.0 %collective-permute-start.8 = (bf16[4,96,256]{2,1,0:T(8,128)(2,1)}, bf16[4,96,256]{2,1,0:T(8,128)(2,1)}, u32[]{:S(2)}, u32[]{:S(2)}) collective-permute-start(bf16[4,96,256]{2,1,0:T(8,128)(2,1)} %collective-permute-done.5.refs_3_), channel_id=1, source_target_pairs={{0,16},{16,0},{1,17},{17,1},{2,18},{18,2},{3,19},{19,3},{4,20},{20... | collective-permute-start | bytes 589832 | tf_op jit(solution)/shard_map/ppermute | solution.py:302
  38.6 1.8 %collective-permute-start.11 = (bf16[4,96,256]{2,1,0:T(8,128)(2,1)S(1)}, bf16[4,96,256]{2,1,0:T(8,128)(2,1)}, u32[]{:S(2)}, u32[]{:S(2)}) collective-permute-start(bf16[4,96,256]{2,1,0:T(8,128)(2,1)S(1)} %collective-permute-done.2.refs_2_), channel_id=1, source_target_pairs={{0,2},{2,0},{4,6},{6,4},{8,10},{10,8},{12,14},{14,12},{1,3},{3,1},... | collective-permute-start | bytes 589832 | tf_op jit(solution)/shard_map/ppermute | solution.py:302
  38.7 2.3 %collective-permute-start.15 = (bf16[4,96,256]{2,1,0:T(8,128)(2,1)}, bf16[4,96,256]{2,1,0:T(8,128)(2,1)}, u32[]{:S(2)}, u32[]{:S(2)}) collective-permute-start(bf16[4,96,256]{2,1,0:T(8,128)(2,1)} %collective-permute-done.3.refs_6_), channel_id=1, source_target_pairs={{0,2},{2,0},{4,6},{6,4},{8,10},{10,8},{12,14},{14,12},{1,3},{3,1},... | collective-permute-start | bytes 589832 | tf_op jit(solution)/shard_map/ppermute | solution.py:302
  39.2 1.8 %collective-permute-start.12 = (bf16[4,96,256]{2,1,0:T(8,128)(2,1)}, bf16[4,96,256]{2,1,0:T(8,128)(2,1)}, u32[]{:S(2)}, u32[]{:S(2)}) collective-permute-start(bf16[4,96,256]{2,1,0:T(8,128)(2,1)} %collective-permute-done.5.refs_3_), channel_id=1, source_target_pairs={{0,2},{2,0},{4,6},{6,4},{8,10},{10,8},{12,14},{14,12},{1,3},{3,1},... | collective-permute-start | bytes 589832 | tf_op jit(solution)/shard_map/ppermute | solution.py:302
  39.3 2.0 %collective-permute-start.14 = (bf16[4,96,256]{2,1,0:T(8,128)(2,1)}, bf16[4,96,256]{2,1,0:T(8,128)(2,1)}, u32[]{:S(2)}, u32[]{:S(2)}) collective-permute-start(bf16[4,96,256]{2,1,0:T(8,128)(2,1)} %collective-permute-done.7.refs_5_), channel_id=1, source_target_pairs={{0,2},{2,0},{4,6},{6,4},{8,10},{10,8},{12,14},{14,12},{1,3},{3,1},... | collective-permute-start | bytes 589832 | tf_op jit(solution)/shard_map/ppermute | solution.py:302
  40.4 1.8 %collective-permute-start.16 = (bf16[4,96,256]{2,1,0:T(8,128)(2,1)}, bf16[4,96,256]{2,1,0:T(8,128)(2,1)}, u32[]{:S(2)}, u32[]{:S(2)}) collective-permute-start(bf16[4,96,256]{2,1,0:T(8,128)(2,1)} %collective-permute-done.8.refs_7_), channel_id=1, source_target_pairs={{0,2},{2,0},{4,6},{6,4},{8,10},{10,8},{12,14},{14,12},{1,3},{3,1},... | collective-permute-start | bytes 589832 | tf_op jit(solution)/shard_map/ppermute | solution.py:302
  (4 other events, 9.3 us)

commit v5 on v4

--- a/solution.py
+++ b/solution.py
@@ -312,10 +312,9 @@
     arrived = [across(half, "tensor", 1) for half in theirs]
     (mine,) = parts(1, me_tensor)
     block = finish(mine, arrived, key_gain, heads, dim)
-    near, far, side = across(block, "seq", 2), across(block, "seq", 4), across(block, "segment", 1)
-    far_near, side_far = across(far, "seq", 2), across(far, "segment", 1)
-    side_near = across(after(far_near, side), "seq", 2)
-    side_far, text = lax.optimization_barrier((side_far, text))
+    near, far, side = across(block, "seq", 2), across(block, "seq", 4), across(after(text, block), "segment", 1)
+    far_near, side_far = across(after(near, far), "seq", 2), across(far, "segment", 1)
+    side_near = across(side, "seq", 2)
     lane = [block, near, far, far_near, side, side_near, side_far, across(far_near, "segment", 1)]
     kv = lane + [across(piece, "seq", 1) for piece in lane]
     return attend(text, kv, offsets, home, tile_tokens, tile_len)

time: 58.6 us -> 58.4 us (level)
  starting transfers between devices: 15.7 us -> 14.7 us
  waiting for transfers between devices: 11.8 us -> 12.6 us
    ppermute x17, starting transfers between devices: 15.7 us -> 14.7 us  [across(): lax.ppermute(array, axis, [(i, i ^ step) for i in range(lax.axis_size(axi...]
    ppermute x17, waiting for transfers between devices: 11.8 us -> 12.6 us  [across(): lax.ppermute(array, axis, [(i, i ^ step) for i in range(lax.axis_size(axi...]
  transfers between devices with their start and end apart: 17 -> 17, of which waited for: 7 -> 9; matrix products, arithmetic and copies ran while one was open for 0% -> 0% of each run, Pallas kernels for 19% -> 19%
where the time goes in v5:
time: 58.4 us; the launch traced here: 58.2 us
  Pallas kernels  30.4 us (52%)
  starting transfers between devices  14.7 us (25%)
  waiting for transfers between devices  12.6 us (22%)
    pallas_call x1, Pallas kernels, attend(): pl.pallas_call(functools.partial(attend_kernel, (heads, blocks, group, di...  16 us
    ppermute x17, starting transfers between devices, across(): lax.ppermute(array, axis, [(i, i ^ step) for i in range(lax.axis_size(axi...  14.7 us
    ppermute x17, waiting for transfers between devices, across(): lax.ppermute(array, axis, [(i, i ^ step) for i in range(lax.axis_size(axi...  12.6 us
    pallas_call x3, Pallas kernels, project(): pl.pallas_call(functools.partial(project_kernel, pieces), in_specs=[SMEM,...  11.5 us
    pallas_call x1, Pallas kernels, sort_rows(): pl.pallas_call(functools.partial(sort_kernel, tiles, group), in_specs=[VM...  2.78 us
  transfers between devices with their start and end apart: 17, of which 9 were waited for; matrix products, arithmetic and copies ran while one was open for 0% of the time, Pallas kernels for 19%

profile of v5, /device:TPU:0, one launch (start us, length us, event | category | flops | bytes accessed | tf_op | source)
XLA Modules:
  0.0 58.2 jit_solution(3792726334728834324)
XLA Ops:
  0.0 3.3 %shard_map.66 = f32[96,512]{1,0:T(8,128)S(1)} custom-call(s32[1]{0:T(128)} %bitcast.3.block_ref, bf16[96,3840]{1,0:T(8,128)(2,1)} %vision_hbm_ref.5, bf16[3840,2048]{1,0:T(8,128)(2,1)} %weight_ref.5), custom_call_target="tpu_custom_call" | custom-call | bytes 11520000 | tf_op jit(solution)/shard_map/pallas_call | solution.py:64
  3.3 3.1 %collective-permute-start = (f32[96,512]{1,0:T(8,128)S(1)}, f32[96,512]{1,0:T(8,128)S(1)}, u32[]{:S(2)}, u32[]{:S(2)}) collective-permute-start(f32[96,512]{1,0:T(8,128)S(1)} %shard_map.66), channel_id=1, source_target_pairs={{0,1},{1,0},{2,3},{3,2},{4,5},{5,4},{6,7},{7,6},{8,9},{9,8},{10,11... | collective-permute-start | bytes 589832 | tf_op jit(solution)/shard_map/ppermute | solution.py:302
  6.4 3.3 %shard_map.67 = f32[96,512]{1,0:T(8,128)S(1)} custom-call(s32[1]{0:T(128)} %bitcast.4.block_ref, bf16[96,3840]{1,0:T(8,128)(2,1)} %vision_hbm_ref.5, bf16[3840,2048]{1,0:T(8,128)(2,1)} %weight_ref.5), custom_call_target="tpu_custom_call" | custom-call | bytes 11520000 | tf_op jit(solution)/shard_map/pallas_call | solution.py:64
  9.8 5.0 %shard_map.65.own_ref = f32[96,1024]{1,0:T(8,128)S(1)} custom-call(s32[1]{0:T(128)} %bitcast.2.block_ref, bf16[96,3840]{1,0:T(8,128)(2,1)} %vision_hbm_ref.5, bf16[3840,2048]{1,0:T(8,128)(2,1)} %weight_ref.5), custom_call_target="tpu_custom_call" | custom-call | bytes 11520000 | tf_op jit(solution)/shard_map/pallas_call | solution.py:64
  14.8 1.3 %collective-permute-done.1.refs_1_ = f32[96,512]{1,0:T(8,128)S(1)} collective-permute-done((f32[96,512]{1,0:T(8,128)S(1)}, f32[96,512]{1,0:T(8,128)S(1)}, u32[]{:S(2)}, u32[]{:S(2)}) %collective-permute-start.1) | collective-permute-done | bytes 196640 | tf_op jit(solution)/shard_map/ppermute | solution.py:302
  16.3 2.7 %collective-permute-start.3 = (bf16[4,96,256]{2,1,0:T(8,128)(2,1)S(1)}, bf16[4,96,256]{2,1,0:T(8,128)(2,1)S(1)}, u32[]{:S(2)}, u32[]{:S(2)}) collective-permute-start(bf16[4,96,256]{2,1,0:T(8,128)(2,1)S(1)} %shard_map.68.refs_0_), channel_id=1, source_target_pairs={{0,8},{2,10},{4,12},{6,14},{8,0},{10,2},{12,4},{14,6},{1,9},{3,11}... | collective-permute-start | bytes 589832 | tf_op jit(solution)/shard_map/ppermute | solution.py:302
  18.9 1.6 %collective-permute-start.2 = (bf16[4,96,256]{2,1,0:T(8,128)(2,1)S(1)}, bf16[4,96,256]{2,1,0:T(8,128)(2,1)S(1)}, u32[]{:S(2)}, u32[]{:S(2)}) collective-permute-start(bf16[4,96,256]{2,1,0:T(8,128)(2,1)S(1)} %shard_map.68.refs_0_), channel_id=1, source_target_pairs={{0,4},{2,6},{4,0},{6,2},{8,12},{10,14},{12,8},{14,10},{1,5},{3,7},... | collective-permute-start | bytes 589832 | tf_op jit(solution)/shard_map/ppermute | solution.py:302
  20.5 2.8 %shard_map.64 = (bf16[4,2048,128]{2,1,0:T(8,128)(2,1)S(1)}, bf16[512,128]{1,0:T(8,128)(2,1)S(1)}, bf16[512,512]{1,0:T(8,128)(2,1)S(1)}, s32[3,4]{1,0:T(4,128)S(1)}) custom-call(bf16[512,4,512]{2,1,0:T(4,128)(2,1)S(1)} %copy-done, s32[2,512]{1,0:T(2,128)S(1)} %bitcast.6), custom_call_target="tpu_custom_call" | custom-call | bytes 360000 | tf_op jit(solution)/shard_map/pallas_call | solution.py:150
  23.4 1.6 %collective-permute-start.5 = (bf16[4,96,256]{2,1,0:T(8,128)(2,1)S(1)}, bf16[4,96,256]{2,1,0:T(8,128)(2,1)}, u32[]{:S(2)}, u32[]{:S(2)}) collective-permute-start(bf16[4,96,256]{2,1,0:T(8,128)(2,1)S(1)} %shard_map.68.refs_0_), channel_id=1, source_target_pairs={{0,16},{16,0},{1,17},{17,1},{2,18},{18,2},{3,19},{19,3},{4,20},{20... | collective-permute-start | bytes 589832 | tf_op jit(solution)/shard_map/ppermute | solution.py:302
  24.9 2.0 %collective-permute-done.3.refs_2_ = bf16[4,96,256]{2,1,0:T(8,128)(2,1)S(1)} collective-permute-done((bf16[4,96,256]{2,1,0:T(8,128)(2,1)S(1)}, bf16[4,96,256]{2,1,0:T(8,128)(2,1)S(1)}, u32[]{:S(2)}, u32[]{:S(2)}) %collective-permute-start.3) | collective-permute-done | bytes 196640 | tf_op jit(solution)/shard_map/ppermute | solution.py:302
  27.0 0.2 collective-permute-done.2.refs_1_
  27.2 1.4 %collective-permute-start.4 = (bf16[4,96,256]{2,1,0:T(8,128)(2,1)S(1)}, bf16[4,96,256]{2,1,0:T(8,128)(2,1)}, u32[]{:S(2)}, u32[]{:S(2)}) collective-permute-start(bf16[4,96,256]{2,1,0:T(8,128)(2,1)S(1)} %collective-permute-done.3.refs_2_), channel_id=1, source_target_pairs={{0,4},{2,6},{4,0},{6,2},{8,12},{10,14},{12,8},{14,10},{1,5},{3,7},... | collective-permute-start | bytes 589832 | tf_op jit(solution)/shard_map/ppermute | solution.py:302
  28.6 1.5 %collective-permute-start.7 = (bf16[4,96,256]{2,1,0:T(8,128)(2,1)S(1)}, bf16[4,96,256]{2,1,0:T(8,128)(2,1)}, u32[]{:S(2)}, u32[]{:S(2)}) collective-permute-start(bf16[4,96,256]{2,1,0:T(8,128)(2,1)S(1)} %collective-permute-done.3.refs_2_), channel_id=1, source_target_pairs={{0,16},{16,0},{1,17},{17,1},{2,18},{18,2},{3,19},{19,3},{4,20},{20... | collective-permute-start | bytes 589832 | tf_op jit(solution)/shard_map/ppermute | solution.py:302
  30.1 0.2 collective-permute-start.10
  30.4 0.4 collective-permute-done.5.refs_4_
  30.8 0.4 collective-permute-start.6
  31.2 1.7 %collective-permute-done.4.refs_3_ = bf16[4,96,256]{2,1,0:T(8,128)(2,1)} collective-permute-done((bf16[4,96,256]{2,1,0:T(8,128)(2,1)S(1)}, bf16[4,96,256]{2,1,0:T(8,128)(2,1)}, u32[]{:S(2)}, u32[]{:S(2)}) %collective-permute-start.4) | collective-permute-done | bytes 196640 | tf_op jit(solution)/shard_map/ppermute | solution.py:302
  33.0 1.5 %collective-permute-start.8 = (bf16[4,96,256]{2,1,0:T(8,128)(2,1)}, bf16[4,96,256]{2,1,0:T(8,128)(2,1)}, u32[]{:S(2)}, u32[]{:S(2)}) collective-permute-start(bf16[4,96,256]{2,1,0:T(8,128)(2,1)} %collective-permute-done.4.refs_3_), channel_id=1, source_target_pairs={{0,16},{16,0},{1,17},{17,1},{2,18},{18,2},{3,19},{19,3},{4,20},{20... | collective-permute-start | bytes 589832 | tf_op jit(solution)/shard_map/ppermute | solution.py:302
  34.5 2.0 %collective-permute-done.7.refs_6_ = bf16[4,96,256]{2,1,0:T(8,128)(2,1)} collective-permute-done((bf16[4,96,256]{2,1,0:T(8,128)(2,1)S(1)}, bf16[4,96,256]{2,1,0:T(8,128)(2,1)}, u32[]{:S(2)}, u32[]{:S(2)}) %collective-permute-start.7) | collective-permute-done | bytes 196640 | tf_op jit(solution)/shard_map/ppermute | solution.py:302
  36.5 0.6 collective-permute-start.15
  37.1 0.6 %collective-permute-done.6.refs_5_ = bf16[4,96,256]{2,1,0:T(8,128)(2,1)} collective-permute-done((bf16[4,96,256]{2,1,0:T(8,128)(2,1)}, bf16[4,96,256]{2,1,0:T(8,128)(2,1)}, u32[]{:S(2)}, u32[]{:S(2)}) %collective-permute-start.6) | collective-permute-done | bytes 196640 | tf_op jit(solution)/shard_map/ppermute | solution.py:302
  37.8 2.5 %collective-permute-done.8.refs_7_ = bf16[4,96,256]{2,1,0:T(8,128)(2,1)} collective-permute-done((bf16[4,96,256]{2,1,0:T(8,128)(2,1)}, bf16[4,96,256]{2,1,0:T(8,128)(2,1)}, u32[]{:S(2)}, u32[]{:S(2)}) %collective-permute-start.8) | collective-permute-done | bytes 196640 | tf_op jit(solution)/shard_map/ppermute | solution.py:302
  40.3 1.8 %collective-permute-done.16.refs_15_ = bf16[4,96,256]{2,1,0:T(8,128)(2,1)} collective-permute-done((bf16[4,96,256]{2,1,0:T(8,128)(2,1)}, bf16[4,96,256]{2,1,0:T(8,128)(2,1)}, u32[]{:S(2)}, u32[]{:S(2)}) %collective-permute-start.16) | collective-permute-done | bytes 196640 | tf_op jit(solution)/shard_map/ppermute | solution.py:302
  42.1 16.0 %shard_map.69 = bf16[512,4,512]{2,1,0:T(4,128)(2,1)} custom-call(s32[1]{0:T(128)} %bitcast.home_ref, s32[4]{0:T(128)S(1)} %copy-done.4, s32[3,4]{1,0:T(4,128)S(1)} %get-tuple-element.11.hull_ref, bf16[4,96,256]{2,1,0:T(8,128)(2,1)} %copy-done.1, bf16[4,96,256]{2,1,0:T(8,128)(2,1)} %copy-done.6, bf16[4,96,256]{2,1,0:T(8,128)(2,1)} %copy-done.5, ...), custom_call_target="tpu_custom_call" | custom-call | bytes 54000000 | tf_op jit(solution)/shard_map/pallas_call | solution.py:254
  (36 shorter events, 0.5 us)
Async XLA Ops:
  3.3 11.5 %collective-permute-start = (f32[96,512]{1,0:T(8,128)S(1)}, f32[96,512]{1,0:T(8,128)S(1)}, u32[]{:S(2)}, u32[]{:S(2)}) collective-permute-start(f32[96,512]{1,0:T(8,128)S(1)} %shard_map.66), channel_id=1, source_target_pairs={{0,1},{1,0},{2,3},{3,2},{4,5},{5,4},{6,7},{7,6},{8,9},{9,8},{10,11... | collective-permute-start | bytes 589832 | tf_op jit(solution)/shard_map/ppermute | solution.py:302
  9.7 6.4 %collective-permute-start.1 = (f32[96,512]{1,0:T(8,128)S(1)}, f32[96,512]{1,0:T(8,128)S(1)}, u32[]{:S(2)}, u32[]{:S(2)}) collective-permute-start(f32[96,512]{1,0:T(8,128)S(1)} %shard_map.67), channel_id=1, source_target_pairs={{0,1},{1,0},{2,3},{3,2},{4,5},{5,4},{6,7},{7,6},{8,9},{9,8},{10,11... | collective-permute-start | bytes 589832 | tf_op jit(solution)/shard_map/ppermute | solution.py:302
  9.8 10.8 %copy-start = (bf16[512,4,512]{2,1,0:T(4,128)(2,1)S(1)}, bf16[512,4,512]{2,1,0:T(4,128)(2,1)}, u32[]{:S(2)}) copy-start(bf16[512,4,512]{2,1,0:T(4,128)(2,1)} %q_ref.1) | copy-start | bytes 6291460
  9.8 10.7 %copy-start.2 = (s32[512,2]{0,1:T(2,128)S(1)}, s32[512,2]{0,1:T(2,128)}, u32[]{:S(2)}) copy-start(s32[512,2]{0,1:T(2,128)} %param.11) | copy-start | bytes 12292
  14.8 27.3 %copy-start.4 = (s32[4]{0:T(128)S(1)}, s32[4]{0:T(128)}, u32[]{:S(2)}) copy-start(s32[4]{0:T(128)} %tokens_ref.1) | copy-start | bytes 52
  16.3 25.8 %copy-start.1 = (bf16[4,96,256]{2,1,0:T(8,128)(2,1)}, bf16[4,96,256]{2,1,0:T(8,128)(2,1)S(1)}, u32[]{:S(2)}) copy-start(bf16[4,96,256]{2,1,0:T(8,128)(2,1)S(1)} %shard_map.68.refs_0_) | copy-start | bytes 589828
  16.3 10.7 %collective-permute-start.3 = (bf16[4,96,256]{2,1,0:T(8,128)(2,1)S(1)}, bf16[4,96,256]{2,1,0:T(8,128)(2,1)S(1)}, u32[]{:S(2)}, u32[]{:S(2)}) collective-permute-start(bf16[4,96,256]{2,1,0:T(8,128)(2,1)S(1)} %shard_map.68.refs_0_), channel_id=1, source_target_pairs={{0,8},{2,10},{4,12},{6,14},{8,0},{10,2},{12,4},{14,6},{1,9},{3,11}... | collective-permute-start | bytes 589832 | tf_op jit(solution)/shard_map/ppermute | solution.py:302
  18.9 8.3 %collective-permute-start.2 = (bf16[4,96,256]{2,1,0:T(8,128)(2,1)S(1)}, bf16[4,96,256]{2,1,0:T(8,128)(2,1)S(1)}, u32[]{:S(2)}, u32[]{:S(2)}) collective-permute-start(bf16[4,96,256]{2,1,0:T(8,128)(2,1)S(1)} %shard_map.68.refs_0_), channel_id=1, source_target_pairs={{0,4},{2,6},{4,0},{6,2},{8,12},{10,14},{12,8},{14,10},{1,5},{3,7},... | collective-permute-start | bytes 589832 | tf_op jit(solution)/shard_map/ppermute | solution.py:302
  23.3 6.8 %collective-permute-start.9 = (bf16[4,96,256]{2,1,0:T(8,128)(2,1)S(1)}, bf16[4,96,256]{2,1,0:T(8,128)(2,1)S(1)}, u32[]{:S(2)}, u32[]{:S(2)}) collective-permute-start(bf16[4,96,256]{2,1,0:T(8,128)(2,1)S(1)} %shard_map.68.refs_0_), channel_id=1, source_target_pairs={{0,2},{2,0},{4,6},{6,4},{8,10},{10,8},{12,14},{14,12},{1,3},{3,1},... | collective-permute-start | bytes 589832 | tf_op jit(solution)/shard_map/ppermute | solution.py:302
  23.4 7.4 %collective-permute-start.5 = (bf16[4,96,256]{2,1,0:T(8,128)(2,1)S(1)}, bf16[4,96,256]{2,1,0:T(8,128)(2,1)}, u32[]{:S(2)}, u32[]{:S(2)}) collective-permute-start(bf16[4,96,256]{2,1,0:T(8,128)(2,1)S(1)} %shard_map.68.refs_0_), channel_id=1, source_target_pairs={{0,16},{16,0},{1,17},{17,1},{2,18},{18,2},{3,19},{19,3},{4,20},{20... | collective-permute-start | bytes 589832 | tf_op jit(solution)/shard_map/ppermute | solution.py:302
  27.0 15.1 %copy-start.5 = (bf16[4,96,256]{2,1,0:T(8,128)(2,1)}, bf16[4,96,256]{2,1,0:T(8,128)(2,1)S(1)}, u32[]{:S(2)}) copy-start(bf16[4,96,256]{2,1,0:T(8,128)(2,1)S(1)} %collective-permute-done.3.refs_2_) | copy-start | bytes 589828
  27.2 14.9 %copy-start.6 = (bf16[4,96,256]{2,1,0:T(8,128)(2,1)}, bf16[4,96,256]{2,1,0:T(8,128)(2,1)S(1)}, u32[]{:S(2)}) copy-start(bf16[4,96,256]{2,1,0:T(8,128)(2,1)S(1)} %collective-permute-done.2.refs_1_) | copy-start | bytes 589828
  27.2 5.8 %collective-permute-start.4 = (bf16[4,96,256]{2,1,0:T(8,128)(2,1)S(1)}, bf16[4,96,256]{2,1,0:T(8,128)(2,1)}, u32[]{:S(2)}, u32[]{:S(2)}) collective-permute-start(bf16[4,96,256]{2,1,0:T(8,128)(2,1)S(1)} %collective-permute-done.3.refs_2_), channel_id=1, source_target_pairs={{0,4},{2,6},{4,0},{6,2},{8,12},{10,14},{12,8},{14,10},{1,5},{3,7},... | collective-permute-start | bytes 589832 | tf_op jit(solution)/shard_map/ppermute | solution.py:302
  28.6 5.8 %collective-permute-start.11 = (bf16[4,96,256]{2,1,0:T(8,128)(2,1)S(1)}, bf16[4,96,256]{2,1,0:T(8,128)(2,1)S(1)}, u32[]{:S(2)}, u32[]{:S(2)}) collective-permute-start(bf16[4,96,256]{2,1,0:T(8,128)(2,1)S(1)} %collective-permute-done.3.refs_2_), channel_id=1, source_target_pairs={{0,2},{2,0},{4,6},{6,4},{8,10},{10,8},{12,14},{14,12},{1,3},{3,1},... | collective-permute-start | bytes 589832 | tf_op jit(solution)/shard_map/ppermute | solution.py:302
  28.6 7.8 %collective-permute-start.7 = (bf16[4,96,256]{2,1,0:T(8,128)(2,1)S(1)}, bf16[4,96,256]{2,1,0:T(8,128)(2,1)}, u32[]{:S(2)}, u32[]{:S(2)}) collective-permute-start(bf16[4,96,256]{2,1,0:T(8,128)(2,1)S(1)} %collective-permute-done.3.refs_2_), channel_id=1, source_target_pairs={{0,16},{16,0},{1,17},{17,1},{2,18},{18,2},{3,19},{19,3},{4,20},{20... | collective-permute-start | bytes 589832 | tf_op jit(solution)/shard_map/ppermute | solution.py:302
  30.1 11.9 %copy-start.7 = (bf16[4,96,256]{2,1,0:T(8,128)(2,1)}, bf16[4,96,256]{2,1,0:T(8,128)(2,1)S(1)}, u32[]{:S(2)}) copy-start(bf16[4,96,256]{2,1,0:T(8,128)(2,1)S(1)} %collective-permute-done.9.refs_8_) | copy-start | bytes 589828
  30.1 6.3 %collective-permute-start.10 = (bf16[4,96,256]{2,1,0:T(8,128)(2,1)S(1)}, bf16[4,96,256]{2,1,0:T(8,128)(2,1)S(1)}, u32[]{:S(2)}, u32[]{:S(2)}) collective-permute-start(bf16[4,96,256]{2,1,0:T(8,128)(2,1)S(1)} %collective-permute-done.2.refs_1_), channel_id=1, source_target_pairs={{0,2},{2,0},{4,6},{6,4},{8,10},{10,8},{12,14},{14,12},{1,3},{3,1},... | collective-permute-start | bytes 589832 | tf_op jit(solution)/shard_map/ppermute | solution.py:302
  30.8 7.0 %collective-permute-start.6 = (bf16[4,96,256]{2,1,0:T(8,128)(2,1)}, bf16[4,96,256]{2,1,0:T(8,128)(2,1)}, u32[]{:S(2)}, u32[]{:S(2)}) collective-permute-start(bf16[4,96,256]{2,1,0:T(8,128)(2,1)} %collective-permute-done.5.refs_4_), channel_id=1, source_target_pairs={{0,4},{2,6},{4,0},{6,2},{8,12},{10,14},{12,8},{14,10},{1,5},{3,7},... | collective-permute-start | bytes 589832 | tf_op jit(solution)/shard_map/ppermute | solution.py:302
  33.0 7.3 %collective-permute-start.8 = (bf16[4,96,256]{2,1,0:T(8,128)(2,1)}, bf16[4,96,256]{2,1,0:T(8,128)(2,1)}, u32[]{:S(2)}, u32[]{:S(2)}) collective-permute-start(bf16[4,96,256]{2,1,0:T(8,128)(2,1)} %collective-permute-done.4.refs_3_), channel_id=1, source_target_pairs={{0,16},{16,0},{1,17},{17,1},{2,18},{18,2},{3,19},{19,3},{4,20},{20... | collective-permute-start | bytes 589832 | tf_op jit(solution)/shard_map/ppermute | solution.py:302
  34.5 5.8 %collective-permute-start.13 = (bf16[4,96,256]{2,1,0:T(8,128)(2,1)}, bf16[4,96,256]{2,1,0:T(8,128)(2,1)}, u32[]{:S(2)}, u32[]{:S(2)}) collective-permute-start(bf16[4,96,256]{2,1,0:T(8,128)(2,1)} %collective-permute-done.5.refs_4_), channel_id=1, source_target_pairs={{0,2},{2,0},{4,6},{6,4},{8,10},{10,8},{12,14},{14,12},{1,3},{3,1},... | collective-permute-start | bytes 589832 | tf_op jit(solution)/shard_map/ppermute | solution.py:302
  36.4 3.8 %collective-permute-start.12 = (bf16[4,96,256]{2,1,0:T(8,128)(2,1)}, bf16[4,96,256]{2,1,0:T(8,128)(2,1)}, u32[]{:S(2)}, u32[]{:S(2)}) collective-permute-start(bf16[4,96,256]{2,1,0:T(8,128)(2,1)} %collective-permute-done.4.refs_3_), channel_id=1, source_target_pairs={{0,2},{2,0},{4,6},{6,4},{8,10},{10,8},{12,14},{14,12},{1,3},{3,1},... | collective-permute-start | bytes 589832 | tf_op jit(solution)/shard_map/ppermute | solution.py:302
  36.5 3.8 %collective-permute-start.15 = (bf16[4,96,256]{2,1,0:T(8,128)(2,1)}, bf16[4,96,256]{2,1,0:T(8,128)(2,1)}, u32[]{:S(2)}, u32[]{:S(2)}) collective-permute-start(bf16[4,96,256]{2,1,0:T(8,128)(2,1)} %collective-permute-done.7.refs_6_), channel_id=1, source_target_pairs={{0,2},{2,0},{4,6},{6,4},{8,10},{10,8},{12,14},{14,12},{1,3},{3,1},... | collective-permute-start | bytes 589832 | tf_op jit(solution)/shard_map/ppermute | solution.py:302
  37.8 2.5 %collective-permute-start.14 = (bf16[4,96,256]{2,1,0:T(8,128)(2,1)}, bf16[4,96,256]{2,1,0:T(8,128)(2,1)}, u32[]{:S(2)}, u32[]{:S(2)}) collective-permute-start(bf16[4,96,256]{2,1,0:T(8,128)(2,1)} %collective-permute-done.6.refs_5_), channel_id=1, source_target_pairs={{0,2},{2,0},{4,6},{6,4},{8,10},{10,8},{12,14},{14,12},{1,3},{3,1},... | collective-permute-start | bytes 589832 | tf_op jit(solution)/shard_map/ppermute | solution.py:302
  40.3 1.8 %collective-permute-start.16 = (bf16[4,96,256]{2,1,0:T(8,128)(2,1)}, bf16[4,96,256]{2,1,0:T(8,128)(2,1)}, u32[]{:S(2)}, u32[]{:S(2)}) collective-permute-start(bf16[4,96,256]{2,1,0:T(8,128)(2,1)} %collective-permute-done.8.refs_7_), channel_id=1, source_target_pairs={{0,2},{2,0},{4,6},{6,4},{8,10},{10,8},{12,14},{14,12},{1,3},{3,1},... | collective-permute-start | bytes 589832 | tf_op jit(solution)/shard_map/ppermute | solution.py:302
  (3 other events, 9.0 us)

commit v6 on v5

--- a/solution.py
+++ b/solution.py
@@ -27,56 +27,46 @@
     return pl.CostEstimate(flops=0, bytes_accessed=int(3.6e6 * microseconds), transcendentals=0)
 
 
-def project_kernel(pieces, block_ref, vision_hbm_ref, weight_ref, *refs):
-    count = block_ref.shape[0]
-    out_hbm_refs, (vision_ref, held_ref, out_ref, vision_sem, sems, out_sems) = refs[:count], refs[count:]
-    depth, cols = held_ref.shape[1:]
-    load = pltpu.make_async_copy(vision_hbm_ref, vision_ref, vision_sem)
+def project_kernel(bounds, block_ref, vision_hbm_ref, weight_ref, out_hbm_ref, vision_ref, held_ref, out_ref, load_sem, sems):
+    cols = held_ref.shape[1]
+    load = pltpu.make_async_copy(vision_hbm_ref, vision_ref, load_sem)
     load.start()
+    across = pl.ds(pl.multiple_of(block_ref[0] * cols, cols), cols)
+    spans = [pl.ds(low, high - low) for low, high in zip(bounds, bounds[1:])]
     copies = []
-    for step in range(count * pieces):
-        which, piece = divmod(step, pieces)
-        across = pl.ds(pl.multiple_of(block_ref[which] * cols, cols), cols)
-        copies.append(
-            pltpu.make_async_copy(weight_ref.at[pl.ds(piece * depth, depth), across], held_ref.at[step], sems.at[step])
-        )
+    for piece, span in enumerate(spans):
+        copies.append(pltpu.make_async_copy(weight_ref.at[span, across], held_ref.at[span], sems.at[piece]))
         copies[-1].start()
     load.wait()
-    stores = []
-    for which in range(count):
-        total = None
-        for piece in range(pieces):
-            copies[which * pieces + piece].wait()
-            part = vision_ref[:, piece * depth : (piece + 1) * depth]
-            product = jnp.dot(part, held_ref[which * pieces + piece], preferred_element_type=jnp.float32)
-            total = product if piece == 0 else total + product
-        out_ref[which] = total
-        stores.append(pltpu.make_async_copy(out_ref.at[which], out_hbm_refs[which], out_sems.at[which]))
-        stores[-1].start()
-    for store in stores:
-        store.wait()
-
-
-def project(vision, weight, blocks, cols):
+    total = None
+    for piece, span in enumerate(spans):
+        copies[piece].wait()
+        product = jnp.dot(vision_ref[:, span], held_ref[span], preferred_element_type=jnp.float32)
+        total = product if piece == 0 else total + product
+    out_ref[...] = total
+    store = pltpu.make_async_copy(out_ref, out_hbm_ref, load_sem)
+    store.start()
+    store.wait()
+
+
+def project(vision, weight, block, cols):
     rows, depth = vision.shape
-    count = len(blocks)
-    pieces = next(parts for parts in (5, 3, 2, 1) if depth % (parts * 128) == 0)
+    bounds = [0, depth // 3, depth * 2 // 3, depth] if depth % 768 == 0 else [0, depth]
     return pl.pallas_call(
-        functools.partial(project_kernel, pieces),
+        functools.partial(project_kernel, bounds),
         in_specs=[SMEM, ANY, ANY],
-        out_specs=[ANY] * count,
-        out_shape=[jax.ShapeDtypeStruct((rows, cols), jnp.float32)] * count,
+        out_specs=ANY,
+        out_shape=jax.ShapeDtypeStruct((rows, cols), jnp.float32),
         scratch_shapes=[
             pltpu.VMEM((rows, depth), jnp.bfloat16),
-            pltpu.VMEM((count * pieces, depth // pieces, cols), jnp.bfloat16),
-            pltpu.VMEM((count, rows, cols), jnp.float32),
+            pltpu.VMEM((depth, cols), jnp.bfloat16),
+            pltpu.VMEM((rows, cols), jnp.float32),
             pltpu.SemaphoreType.DMA,
-            pltpu.SemaphoreType.DMA((count * pieces,)),
-            pltpu.SemaphoreType.DMA((count,)),
+            pltpu.SemaphoreType.DMA((len(bounds) - 1,)),
         ],
         compiler_params=pltpu.CompilerParams(vmem_limit_bytes=LARGE_VMEM),
-        cost_estimate=lasting(2 + 1.2 * count),
-    )(jnp.stack(blocks), pltpu.with_memory_space_constraint(vision, pltpu.HBM), weight)
+        cost_estimate=lasting(3 if cols < 1024 else 5),
+    )(block.reshape(1), pltpu.with_memory_space_constraint(vision, pltpu.HBM), weight)
 
 
 def finish_kernel(heads, dim, parts, own_ref, *refs):
@@ -301,16 +291,16 @@
     def across(array, axis, step):
         return lax.ppermute(array, axis, [(i, i ^ step) for i in range(lax.axis_size(axis))])
 
-    def parts(count, *blocks):
-        return project(vision_states, kv_weight, [block.astype(jnp.int32) for block in blocks], heads * 2 * dim // count)
+    def part(count, index):
+        return project(vision_states, kv_weight, index.astype(jnp.int32), heads * 2 * dim // count)
 
     text = sort_rows(queries, text_tiles, tile_tokens.shape[0], dim)
     home = me_segment * 8 + me_seq
     offsets = [8 * side + 2 * far + core for core in range(2) for side in range(2) for far in range(4)]
     other = 1 - me_tensor
-    theirs = [parts(HALVES, other * HALVES + half)[0] for half in range(HALVES)]
+    theirs = [part(HALVES, other * HALVES + half) for half in range(HALVES)]
     arrived = [across(half, "tensor", 1) for half in theirs]
-    (mine,) = parts(1, me_tensor)
+    mine = part(1, me_tensor)
     block = finish(mine, arrived, key_gain, heads, dim)
     near, far, side = across(block, "seq", 2), across(block, "seq", 4), across(after(text, block), "segment", 1)
     far_near, side_far = across(after(near, far), "seq", 2), across(far, "segment", 1)

time: 58.4 us -> 58 us (level)
  Pallas kernels: 30.4 us -> 29.7 us
    pallas_call x3, Pallas kernels: 11.5 us -> 10.8 us  [project(): pl.pallas_call(functools.partial(project_kernel, bounds), in_specs=[SMEM,...]
  transfers between devices with their start and end apart: 17 -> 17, of which waited for: 9 -> 9; matrix products, arithmetic and copies ran while one was open for 0% -> 0% of each run, Pallas kernels for 19% -> 18%
where the time goes in v6:
time: 58 us; the launch traced here: 57.8 us
  Pallas kernels  29.7 us (51%)
  starting transfers between devices  14.7 us (25%)
  waiting for transfers between devices  12.9 us (22%)
    pallas_call x1, Pallas kernels, attend(): pl.pallas_call(functools.partial(attend_kernel, (heads, blocks, group, di...  16 us
    ppermute x17, starting transfers between devices, across(): lax.ppermute(array, axis, [(i, i ^ step) for i in range(lax.axis_size(axi...  14.7 us
    ppermute x17, waiting for transfers between devices, across(): lax.ppermute(array, axis, [(i, i ^ step) for i in range(lax.axis_size(axi...  12.9 us
    pallas_call x3, Pallas kernels, project(): pl.pallas_call(functools.partial(project_kernel, bounds), in_specs=[SMEM,...  10.8 us
    pallas_call x1, Pallas kernels, sort_rows(): pl.pallas_call(functools.partial(sort_kernel, tiles, group), in_specs=[VM...  2.78 us
  transfers between devices with their start and end apart: 17, of which 9 were waited for; matrix products, arithmetic and copies ran while one was open for 0% of the time, Pallas kernels for 18%

profile of v6, /device:TPU:0, one launch (start us, length us, event | category | flops | bytes accessed | tf_op | source)
XLA Modules:
  0.0 57.8 jit_solution(3696930221249441847)
XLA Ops:
  0.0 3.1 %shard_map.66 = f32[96,512]{1,0:T(8,128)S(1)} custom-call(s32[1]{0:T(128)} %bitcast.3.block_ref, bf16[96,3840]{1,0:T(8,128)(2,1)} %vision_hbm_ref.5, bf16[3840,2048]{1,0:T(8,128)(2,1)} %weight_ref.5), custom_call_target="tpu_custom_call" | custom-call | bytes 10800000 | tf_op jit(solution)/shard_map/pallas_call | solution.py:55
  3.1 3.1 %collective-permute-start = (f32[96,512]{1,0:T(8,128)S(1)}, f32[96,512]{1,0:T(8,128)S(1)}, u32[]{:S(2)}, u32[]{:S(2)}) collective-permute-start(f32[96,512]{1,0:T(8,128)S(1)} %shard_map.66), channel_id=1, source_target_pairs={{0,1},{1,0},{2,3},{3,2},{4,5},{5,4},{6,7},{7,6},{8,9},{9,8},{10,11... | collective-permute-start | bytes 589832 | tf_op jit(solution)/shard_map/ppermute | solution.py:292
  6.2 3.1 %shard_map.67 = f32[96,512]{1,0:T(8,128)S(1)} custom-call(s32[1]{0:T(128)} %bitcast.4.block_ref, bf16[96,3840]{1,0:T(8,128)(2,1)} %vision_hbm_ref.5, bf16[3840,2048]{1,0:T(8,128)(2,1)} %weight_ref.5), custom_call_target="tpu_custom_call" | custom-call | bytes 10800000 | tf_op jit(solution)/shard_map/pallas_call | solution.py:55
  9.4 4.6 %shard_map.65.own_ref = f32[96,1024]{1,0:T(8,128)S(1)} custom-call(s32[1]{0:T(128)} %bitcast.2.block_ref, bf16[96,3840]{1,0:T(8,128)(2,1)} %vision_hbm_ref.5, bf16[3840,2048]{1,0:T(8,128)(2,1)} %weight_ref.5), custom_call_target="tpu_custom_call" | custom-call | bytes 18000000 | tf_op jit(solution)/shard_map/pallas_call | solution.py:55
  14.1 1.6 %collective-permute-done.1.refs_1_ = f32[96,512]{1,0:T(8,128)S(1)} collective-permute-done((f32[96,512]{1,0:T(8,128)S(1)}, f32[96,512]{1,0:T(8,128)S(1)}, u32[]{:S(2)}, u32[]{:S(2)}) %collective-permute-start.1) | collective-permute-done | bytes 196640 | tf_op jit(solution)/shard_map/ppermute | solution.py:292
  15.9 2.7 %collective-permute-start.3 = (bf16[4,96,256]{2,1,0:T(8,128)(2,1)S(1)}, bf16[4,96,256]{2,1,0:T(8,128)(2,1)S(1)}, u32[]{:S(2)}, u32[]{:S(2)}) collective-permute-start(bf16[4,96,256]{2,1,0:T(8,128)(2,1)S(1)} %shard_map.68.refs_0_), channel_id=1, source_target_pairs={{0,8},{2,10},{4,12},{6,14},{8,0},{10,2},{12,4},{14,6},{1,9},{3,11}... | collective-permute-start | bytes 589832 | tf_op jit(solution)/shard_map/ppermute | solution.py:292
  18.5 1.6 %collective-permute-start.2 = (bf16[4,96,256]{2,1,0:T(8,128)(2,1)S(1)}, bf16[4,96,256]{2,1,0:T(8,128)(2,1)S(1)}, u32[]{:S(2)}, u32[]{:S(2)}) collective-permute-start(bf16[4,96,256]{2,1,0:T(8,128)(2,1)S(1)} %shard_map.68.refs_0_), channel_id=1, source_target_pairs={{0,4},{2,6},{4,0},{6,2},{8,12},{10,14},{12,8},{14,10},{1,5},{3,7},... | collective-permute-start | bytes 589832 | tf_op jit(solution)/shard_map/ppermute | solution.py:292
  20.1 2.8 %shard_map.64 = (bf16[4,2048,128]{2,1,0:T(8,128)(2,1)S(1)}, bf16[512,128]{1,0:T(8,128)(2,1)S(1)}, bf16[512,512]{1,0:T(8,128)(2,1)S(1)}, s32[3,4]{1,0:T(4,128)S(1)}) custom-call(bf16[512,4,512]{2,1,0:T(4,128)(2,1)S(1)} %copy-done, s32[2,512]{1,0:T(2,128)S(1)} %bitcast.6), custom_call_target="tpu_custom_call" | custom-call | bytes 360000 | tf_op jit(solution)/shard_map/pallas_call | solution.py:140
  23.0 1.6 %collective-permute-start.5 = (bf16[4,96,256]{2,1,0:T(8,128)(2,1)S(1)}, bf16[4,96,256]{2,1,0:T(8,128)(2,1)}, u32[]{:S(2)}, u32[]{:S(2)}) collective-permute-start(bf16[4,96,256]{2,1,0:T(8,128)(2,1)S(1)} %shard_map.68.refs_0_), channel_id=1, source_target_pairs={{0,16},{16,0},{1,17},{17,1},{2,18},{18,2},{3,19},{19,3},{4,20},{20... | collective-permute-start | bytes 589832 | tf_op jit(solution)/shard_map/ppermute | solution.py:292
  24.6 2.0 %collective-permute-done.3.refs_2_ = bf16[4,96,256]{2,1,0:T(8,128)(2,1)S(1)} collective-permute-done((bf16[4,96,256]{2,1,0:T(8,128)(2,1)S(1)}, bf16[4,96,256]{2,1,0:T(8,128)(2,1)S(1)}, u32[]{:S(2)}, u32[]{:S(2)}) %collective-permute-start.3) | collective-permute-done | bytes 196640 | tf_op jit(solution)/shard_map/ppermute | solution.py:292
  26.6 0.2 collective-permute-done.2.refs_1_
  26.8 1.4 %collective-permute-start.4 = (bf16[4,96,256]{2,1,0:T(8,128)(2,1)S(1)}, bf16[4,96,256]{2,1,0:T(8,128)(2,1)}, u32[]{:S(2)}, u32[]{:S(2)}) collective-permute-start(bf16[4,96,256]{2,1,0:T(8,128)(2,1)S(1)} %collective-permute-done.3.refs_2_), channel_id=1, source_target_pairs={{0,4},{2,6},{4,0},{6,2},{8,12},{10,14},{12,8},{14,10},{1,5},{3,7},... | collective-permute-start | bytes 589832 | tf_op jit(solution)/shard_map/ppermute | solution.py:292
  28.3 1.5 %collective-permute-start.7 = (bf16[4,96,256]{2,1,0:T(8,128)(2,1)S(1)}, bf16[4,96,256]{2,1,0:T(8,128)(2,1)}, u32[]{:S(2)}, u32[]{:S(2)}) collective-permute-start(bf16[4,96,256]{2,1,0:T(8,128)(2,1)S(1)} %collective-permute-done.3.refs_2_), channel_id=1, source_target_pairs={{0,16},{16,0},{1,17},{17,1},{2,18},{18,2},{3,19},{19,3},{4,20},{20... | collective-permute-start | bytes 589832 | tf_op jit(solution)/shard_map/ppermute | solution.py:292
  29.8 0.2 collective-permute-start.10
  30.0 0.4 collective-permute-done.5.refs_4_
  30.4 0.4 collective-permute-start.6
  30.9 1.7 %collective-permute-done.4.refs_3_ = bf16[4,96,256]{2,1,0:T(8,128)(2,1)} collective-permute-done((bf16[4,96,256]{2,1,0:T(8,128)(2,1)S(1)}, bf16[4,96,256]{2,1,0:T(8,128)(2,1)}, u32[]{:S(2)}, u32[]{:S(2)}) %collective-permute-start.4) | collective-permute-done | bytes 196640 | tf_op jit(solution)/shard_map/ppermute | solution.py:292
  32.6 1.5 %collective-permute-start.8 = (bf16[4,96,256]{2,1,0:T(8,128)(2,1)}, bf16[4,96,256]{2,1,0:T(8,128)(2,1)}, u32[]{:S(2)}, u32[]{:S(2)}) collective-permute-start(bf16[4,96,256]{2,1,0:T(8,128)(2,1)} %collective-permute-done.4.refs_3_), channel_id=1, source_target_pairs={{0,16},{16,0},{1,17},{17,1},{2,18},{18,2},{3,19},{19,3},{4,20},{20... | collective-permute-start | bytes 589832 | tf_op jit(solution)/shard_map/ppermute | solution.py:292
  34.1 2.0 %collective-permute-done.7.refs_6_ = bf16[4,96,256]{2,1,0:T(8,128)(2,1)} collective-permute-done((bf16[4,96,256]{2,1,0:T(8,128)(2,1)S(1)}, bf16[4,96,256]{2,1,0:T(8,128)(2,1)}, u32[]{:S(2)}, u32[]{:S(2)}) %collective-permute-start.7) | collective-permute-done | bytes 196640 | tf_op jit(solution)/shard_map/ppermute | solution.py:292
  36.1 0.6 collective-permute-start.15
  36.8 0.6 %collective-permute-done.6.refs_5_ = bf16[4,96,256]{2,1,0:T(8,128)(2,1)} collective-permute-done((bf16[4,96,256]{2,1,0:T(8,128)(2,1)}, bf16[4,96,256]{2,1,0:T(8,128)(2,1)}, u32[]{:S(2)}, u32[]{:S(2)}) %collective-permute-start.6) | collective-permute-done | bytes 196640 | tf_op jit(solution)/shard_map/ppermute | solution.py:292
  37.4 2.5 %collective-permute-done.8.refs_7_ = bf16[4,96,256]{2,1,0:T(8,128)(2,1)} collective-permute-done((bf16[4,96,256]{2,1,0:T(8,128)(2,1)}, bf16[4,96,256]{2,1,0:T(8,128)(2,1)}, u32[]{:S(2)}, u32[]{:S(2)}) %collective-permute-start.8) | collective-permute-done | bytes 196640 | tf_op jit(solution)/shard_map/ppermute | solution.py:292
  39.9 1.8 %collective-permute-done.16.refs_15_ = bf16[4,96,256]{2,1,0:T(8,128)(2,1)} collective-permute-done((bf16[4,96,256]{2,1,0:T(8,128)(2,1)}, bf16[4,96,256]{2,1,0:T(8,128)(2,1)}, u32[]{:S(2)}, u32[]{:S(2)}) %collective-permute-start.16) | collective-permute-done | bytes 196640 | tf_op jit(solution)/shard_map/ppermute | solution.py:292
  41.7 16.0 %shard_map.69 = bf16[512,4,512]{2,1,0:T(4,128)(2,1)} custom-call(s32[1]{0:T(128)} %bitcast.home_ref, s32[4]{0:T(128)S(1)} %copy-done.4, s32[3,4]{1,0:T(4,128)S(1)} %get-tuple-element.11.hull_ref, bf16[4,96,256]{2,1,0:T(8,128)(2,1)} %copy-done.1, bf16[4,96,256]{2,1,0:T(8,128)(2,1)} %copy-done.6, bf16[4,96,256]{2,1,0:T(8,128)(2,1)} %copy-done.5, ...), custom_call_target="tpu_custom_call" | custom-call | bytes 54000000 | tf_op jit(solution)/shard_map/pallas_call | solution.py:244
  (36 shorter events, 0.5 us)
Async XLA Ops:
  3.1 11.0 %collective-permute-start = (f32[96,512]{1,0:T(8,128)S(1)}, f32[96,512]{1,0:T(8,128)S(1)}, u32[]{:S(2)}, u32[]{:S(2)}) collective-permute-start(f32[96,512]{1,0:T(8,128)S(1)} %shard_map.66), channel_id=1, source_target_pairs={{0,1},{1,0},{2,3},{3,2},{4,5},{5,4},{6,7},{7,6},{8,9},{9,8},{10,11... | collective-permute-start | bytes 589832 | tf_op jit(solution)/shard_map/ppermute | solution.py:292
  9.3 6.4 %collective-permute-start.1 = (f32[96,512]{1,0:T(8,128)S(1)}, f32[96,512]{1,0:T(8,128)S(1)}, u32[]{:S(2)}, u32[]{:S(2)}) collective-permute-start(f32[96,512]{1,0:T(8,128)S(1)} %shard_map.67), channel_id=1, source_target_pairs={{0,1},{1,0},{2,3},{3,2},{4,5},{5,4},{6,7},{7,6},{8,9},{9,8},{10,11... | collective-permute-start | bytes 589832 | tf_op jit(solution)/shard_map/ppermute | solution.py:292
  9.4 10.7 %copy-start = (bf16[512,4,512]{2,1,0:T(4,128)(2,1)S(1)}, bf16[512,4,512]{2,1,0:T(4,128)(2,1)}, u32[]{:S(2)}) copy-start(bf16[512,4,512]{2,1,0:T(4,128)(2,1)} %q_ref.1) | copy-start | bytes 6291460
  9.4 10.7 %copy-start.2 = (s32[512,2]{0,1:T(2,128)S(1)}, s32[512,2]{0,1:T(2,128)}, u32[]{:S(2)}) copy-start(s32[512,2]{0,1:T(2,128)} %param.11) | copy-start | bytes 12292
  14.1 27.6 %copy-start.4 = (s32[4]{0:T(128)S(1)}, s32[4]{0:T(128)}, u32[]{:S(2)}) copy-start(s32[4]{0:T(128)} %tokens_ref.1) | copy-start | bytes 52
  15.9 25.8 %copy-start.1 = (bf16[4,96,256]{2,1,0:T(8,128)(2,1)}, bf16[4,96,256]{2,1,0:T(8,128)(2,1)S(1)}, u32[]{:S(2)}) copy-start(bf16[4,96,256]{2,1,0:T(8,128)(2,1)S(1)} %shard_map.68.refs_0_) | copy-start | bytes 589828
  15.9 10.7 %collective-permute-start.3 = (bf16[4,96,256]{2,1,0:T(8,128)(2,1)S(1)}, bf16[4,96,256]{2,1,0:T(8,128)(2,1)S(1)}, u32[]{:S(2)}, u32[]{:S(2)}) collective-permute-start(bf16[4,96,256]{2,1,0:T(8,128)(2,1)S(1)} %shard_map.68.refs_0_), channel_id=1, source_target_pairs={{0,8},{2,10},{4,12},{6,14},{8,0},{10,2},{12,4},{14,6},{1,9},{3,11}... | collective-permute-start | bytes 589832 | tf_op jit(solution)/shard_map/ppermute | solution.py:292
  18.5 8.3 %collective-permute-start.2 = (bf16[4,96,256]{2,1,0:T(8,128)(2,1)S(1)}, bf16[4,96,256]{2,1,0:T(8,128)(2,1)S(1)}, u32[]{:S(2)}, u32[]{:S(2)}) collective-permute-start(bf16[4,96,256]{2,1,0:T(8,128)(2,1)S(1)} %shard_map.68.refs_0_), channel_id=1, source_target_pairs={{0,4},{2,6},{4,0},{6,2},{8,12},{10,14},{12,8},{14,10},{1,5},{3,7},... | collective-permute-start | bytes 589832 | tf_op jit(solution)/shard_map/ppermute | solution.py:292
  22.9 6.8 %collective-permute-start.9 = (bf16[4,96,256]{2,1,0:T(8,128)(2,1)S(1)}, bf16[4,96,256]{2,1,0:T(8,128)(2,1)S(1)}, u32[]{:S(2)}, u32[]{:S(2)}) collective-permute-start(bf16[4,96,256]{2,1,0:T(8,128)(2,1)S(1)} %shard_map.68.refs_0_), channel_id=1, source_target_pairs={{0,2},{2,0},{4,6},{6,4},{8,10},{10,8},{12,14},{14,12},{1,3},{3,1},... | collective-permute-start | bytes 589832 | tf_op jit(solution)/shard_map/ppermute | solution.py:292
  23.0 7.4 %collective-permute-start.5 = (bf16[4,96,256]{2,1,0:T(8,128)(2,1)S(1)}, bf16[4,96,256]{2,1,0:T(8,128)(2,1)}, u32[]{:S(2)}, u32[]{:S(2)}) collective-permute-start(bf16[4,96,256]{2,1,0:T(8,128)(2,1)S(1)} %shard_map.68.refs_0_), channel_id=1, source_target_pairs={{0,16},{16,0},{1,17},{17,1},{2,18},{18,2},{3,19},{19,3},{4,20},{20... | collective-permute-start | bytes 589832 | tf_op jit(solution)/shard_map/ppermute | solution.py:292
  26.6 15.1 %copy-start.5 = (bf16[4,96,256]{2,1,0:T(8,128)(2,1)}, bf16[4,96,256]{2,1,0:T(8,128)(2,1)S(1)}, u32[]{:S(2)}) copy-start(bf16[4,96,256]{2,1,0:T(8,128)(2,1)S(1)} %collective-permute-done.3.refs_2_) | copy-start | bytes 589828
  26.8 14.9 %copy-start.6 = (bf16[4,96,256]{2,1,0:T(8,128)(2,1)}, bf16[4,96,256]{2,1,0:T(8,128)(2,1)S(1)}, u32[]{:S(2)}) copy-start(bf16[4,96,256]{2,1,0:T(8,128)(2,1)S(1)} %collective-permute-done.2.refs_1_) | copy-start | bytes 589828
  26.8 5.8 %collective-permute-start.4 = (bf16[4,96,256]{2,1,0:T(8,128)(2,1)S(1)}, bf16[4,96,256]{2,1,0:T(8,128)(2,1)}, u32[]{:S(2)}, u32[]{:S(2)}) collective-permute-start(bf16[4,96,256]{2,1,0:T(8,128)(2,1)S(1)} %collective-permute-done.3.refs_2_), channel_id=1, source_target_pairs={{0,4},{2,6},{4,0},{6,2},{8,12},{10,14},{12,8},{14,10},{1,5},{3,7},... | collective-permute-start | bytes 589832 | tf_op jit(solution)/shard_map/ppermute | solution.py:292
  28.3 5.8 %collective-permute-start.11 = (bf16[4,96,256]{2,1,0:T(8,128)(2,1)S(1)}, bf16[4,96,256]{2,1,0:T(8,128)(2,1)S(1)}, u32[]{:S(2)}, u32[]{:S(2)}) collective-permute-start(bf16[4,96,256]{2,1,0:T(8,128)(2,1)S(1)} %collective-permute-done.3.refs_2_), channel_id=1, source_target_pairs={{0,2},{2,0},{4,6},{6,4},{8,10},{10,8},{12,14},{14,12},{1,3},{3,1},... | collective-permute-start | bytes 589832 | tf_op jit(solution)/shard_map/ppermute | solution.py:292
  28.3 7.8 %collective-permute-start.7 = (bf16[4,96,256]{2,1,0:T(8,128)(2,1)S(1)}, bf16[4,96,256]{2,1,0:T(8,128)(2,1)}, u32[]{:S(2)}, u32[]{:S(2)}) collective-permute-start(bf16[4,96,256]{2,1,0:T(8,128)(2,1)S(1)} %collective-permute-done.3.refs_2_), channel_id=1, source_target_pairs={{0,16},{16,0},{1,17},{17,1},{2,18},{18,2},{3,19},{19,3},{4,20},{20... | collective-permute-start | bytes 589832 | tf_op jit(solution)/shard_map/ppermute | solution.py:292
  29.7 11.9 %copy-start.7 = (bf16[4,96,256]{2,1,0:T(8,128)(2,1)}, bf16[4,96,256]{2,1,0:T(8,128)(2,1)S(1)}, u32[]{:S(2)}) copy-start(bf16[4,96,256]{2,1,0:T(8,128)(2,1)S(1)} %collective-permute-done.9.refs_8_) | copy-start | bytes 589828
  29.8 6.3 %collective-permute-start.10 = (bf16[4,96,256]{2,1,0:T(8,128)(2,1)S(1)}, bf16[4,96,256]{2,1,0:T(8,128)(2,1)S(1)}, u32[]{:S(2)}, u32[]{:S(2)}) collective-permute-start(bf16[4,96,256]{2,1,0:T(8,128)(2,1)S(1)} %collective-permute-done.2.refs_1_), channel_id=1, source_target_pairs={{0,2},{2,0},{4,6},{6,4},{8,10},{10,8},{12,14},{14,12},{1,3},{3,1},... | collective-permute-start | bytes 589832 | tf_op jit(solution)/shard_map/ppermute | solution.py:292
  30.4 7.0 %collective-permute-start.6 = (bf16[4,96,256]{2,1,0:T(8,128)(2,1)}, bf16[4,96,256]{2,1,0:T(8,128)(2,1)}, u32[]{:S(2)}, u32[]{:S(2)}) collective-permute-start(bf16[4,96,256]{2,1,0:T(8,128)(2,1)} %collective-permute-done.5.refs_4_), channel_id=1, source_target_pairs={{0,4},{2,6},{4,0},{6,2},{8,12},{10,14},{12,8},{14,10},{1,5},{3,7},... | collective-permute-start | bytes 589832 | tf_op jit(solution)/shard_map/ppermute | solution.py:292
  32.6 7.3 %collective-permute-start.8 = (bf16[4,96,256]{2,1,0:T(8,128)(2,1)}, bf16[4,96,256]{2,1,0:T(8,128)(2,1)}, u32[]{:S(2)}, u32[]{:S(2)}) collective-permute-start(bf16[4,96,256]{2,1,0:T(8,128)(2,1)} %collective-permute-done.4.refs_3_), channel_id=1, source_target_pairs={{0,16},{16,0},{1,17},{17,1},{2,18},{18,2},{3,19},{19,3},{4,20},{20... | collective-permute-start | bytes 589832 | tf_op jit(solution)/shard_map/ppermute | solution.py:292
  34.1 5.8 %collective-permute-start.13 = (bf16[4,96,256]{2,1,0:T(8,128)(2,1)}, bf16[4,96,256]{2,1,0:T(8,128)(2,1)}, u32[]{:S(2)}, u32[]{:S(2)}) collective-permute-start(bf16[4,96,256]{2,1,0:T(8,128)(2,1)} %collective-permute-done.5.refs_4_), channel_id=1, source_target_pairs={{0,2},{2,0},{4,6},{6,4},{8,10},{10,8},{12,14},{14,12},{1,3},{3,1},... | collective-permute-start | bytes 589832 | tf_op jit(solution)/shard_map/ppermute | solution.py:292
  36.1 3.8 %collective-permute-start.12 = (bf16[4,96,256]{2,1,0:T(8,128)(2,1)}, bf16[4,96,256]{2,1,0:T(8,128)(2,1)}, u32[]{:S(2)}, u32[]{:S(2)}) collective-permute-start(bf16[4,96,256]{2,1,0:T(8,128)(2,1)} %collective-permute-done.4.refs_3_), channel_id=1, source_target_pairs={{0,2},{2,0},{4,6},{6,4},{8,10},{10,8},{12,14},{14,12},{1,3},{3,1},... | collective-permute-start | bytes 589832 | tf_op jit(solution)/shard_map/ppermute | solution.py:292
  36.1 3.8 %collective-permute-start.15 = (bf16[4,96,256]{2,1,0:T(8,128)(2,1)}, bf16[4,96,256]{2,1,0:T(8,128)(2,1)}, u32[]{:S(2)}, u32[]{:S(2)}) collective-permute-start(bf16[4,96,256]{2,1,0:T(8,128)(2,1)} %collective-permute-done.7.refs_6_), channel_id=1, source_target_pairs={{0,2},{2,0},{4,6},{6,4},{8,10},{10,8},{12,14},{14,12},{1,3},{3,1},... | collective-permute-start | bytes 589832 | tf_op jit(solution)/shard_map/ppermute | solution.py:292
  37.4 2.5 %collective-permute-start.14 = (bf16[4,96,256]{2,1,0:T(8,128)(2,1)}, bf16[4,96,256]{2,1,0:T(8,128)(2,1)}, u32[]{:S(2)}, u32[]{:S(2)}) collective-permute-start(bf16[4,96,256]{2,1,0:T(8,128)(2,1)} %collective-permute-done.6.refs_5_), channel_id=1, source_target_pairs={{0,2},{2,0},{4,6},{6,4},{8,10},{10,8},{12,14},{14,12},{1,3},{3,1},... | collective-permute-start | bytes 589832 | tf_op jit(solution)/shard_map/ppermute | solution.py:292
  39.9 1.8 %collective-permute-start.16 = (bf16[4,96,256]{2,1,0:T(8,128)(2,1)}, bf16[4,96,256]{2,1,0:T(8,128)(2,1)}, u32[]{:S(2)}, u32[]{:S(2)}) collective-permute-start(bf16[4,96,256]{2,1,0:T(8,128)(2,1)} %collective-permute-done.8.refs_7_), channel_id=1, source_target_pairs={{0,2},{2,0},{4,6},{6,4},{8,10},{10,8},{12,14},{14,12},{1,3},{3,1},... | collective-permute-start | bytes 589832 | tf_op jit(solution)/shard_map/ppermute | solution.py:292
  (3 other events, 9.0 us)

commit v7 on v6

--- a/solution.py
+++ b/solution.py
@@ -226,9 +226,13 @@
             for head in range(heads)
         ]
         whole = jnp.stack([head.astype(jnp.bfloat16) for head in whole], axis=0)
-        result_ref[here] = jnp.transpose(whole, (1, 0, 2))
-        stores.append(pltpu.make_async_copy(result_ref.at[here], result_hbm_ref.at[here], store_sems.at[part]))
-        stores[-1].start()
+        piece = rows // STORES
+        for step in range(STORES):
+            here = pl.ds(part * rows + step * piece, piece)
+            result_ref[here] = jnp.transpose(whole[:, step * piece : (step + 1) * piece], (1, 0, 2))
+            sem = store_sems.at[part * STORES + step]
+            stores.append(pltpu.make_async_copy(result_ref.at[here], result_hbm_ref.at[here], sem))
+            stores[-1].start()
     for store in stores:
         store.wait()
 
@@ -252,7 +256,7 @@
             pltpu.VMEM((heads, width, text_rows), jnp.bfloat16),
             pltpu.VMEM((text_rows, heads, width), jnp.bfloat16),
             pltpu.SemaphoreType.DMA((len(kv),)),
-            pltpu.SemaphoreType.DMA((STORES,)),
+            pltpu.SemaphoreType.DMA((STORES * STORES,)),
         ],
         compiler_params=pltpu.CompilerParams(vmem_limit_bytes=MIDDLE_VMEM),
         cost_estimate=lasting(15),

time: 58 us -> 58 us (level)
  no operation moved by 1% of the time
where the time goes in v7:
time: 58 us; the launch traced here: 57.8 us
  Pallas kernels  29.7 us (51%)
  starting transfers between devices  14.7 us (25%)
  waiting for transfers between devices  12.9 us (22%)
    pallas_call x1, Pallas kernels, attend(): pl.pallas_call(functools.partial(attend_kernel, (heads, blocks, group, di...  16 us
    ppermute x17, starting transfers between devices, across(): lax.ppermute(array, axis, [(i, i ^ step) for i in range(lax.axis_size(axi...  14.7 us
    ppermute x17, waiting for transfers between devices, across(): lax.ppermute(array, axis, [(i, i ^ step) for i in range(lax.axis_size(axi...  12.9 us
    pallas_call x3, Pallas kernels, project(): pl.pallas_call(functools.partial(project_kernel, bounds), in_specs=[SMEM,...  10.8 us
    pallas_call x1, Pallas kernels, sort_rows(): pl.pallas_call(functools.partial(sort_kernel, tiles, group), in_specs=[VM...  2.78 us
  transfers between devices with their start and end apart: 17, of which 9 were waited for; matrix products, arithmetic and copies ran while one was open for 0% of the time, Pallas kernels for 18%

profile of v7, /device:TPU:0, one launch (start us, length us, event | category | flops | bytes accessed | tf_op | source)
XLA Modules:
  0.0 57.8 jit_solution(7697725994964866265)
XLA Ops:
  0.0 3.1 %shard_map.66 = f32[96,512]{1,0:T(8,128)S(1)} custom-call(s32[1]{0:T(128)} %bitcast.3.block_ref, bf16[96,3840]{1,0:T(8,128)(2,1)} %vision_hbm_ref.5, bf16[3840,2048]{1,0:T(8,128)(2,1)} %weight_ref.5), custom_call_target="tpu_custom_call" | custom-call | bytes 10800000 | tf_op jit(solution)/shard_map/pallas_call | solution.py:55
  3.1 3.1 %collective-permute-start = (f32[96,512]{1,0:T(8,128)S(1)}, f32[96,512]{1,0:T(8,128)S(1)}, u32[]{:S(2)}, u32[]{:S(2)}) collective-permute-start(f32[96,512]{1,0:T(8,128)S(1)} %shard_map.66), channel_id=1, source_target_pairs={{0,1},{1,0},{2,3},{3,2},{4,5},{5,4},{6,7},{7,6},{8,9},{9,8},{10,11... | collective-permute-start | bytes 589832 | tf_op jit(solution)/shard_map/ppermute | solution.py:296
  6.2 3.1 %shard_map.67 = f32[96,512]{1,0:T(8,128)S(1)} custom-call(s32[1]{0:T(128)} %bitcast.4.block_ref, bf16[96,3840]{1,0:T(8,128)(2,1)} %vision_hbm_ref.5, bf16[3840,2048]{1,0:T(8,128)(2,1)} %weight_ref.5), custom_call_target="tpu_custom_call" | custom-call | bytes 10800000 | tf_op jit(solution)/shard_map/pallas_call | solution.py:55
  9.4 4.6 %shard_map.65.own_ref = f32[96,1024]{1,0:T(8,128)S(1)} custom-call(s32[1]{0:T(128)} %bitcast.2.block_ref, bf16[96,3840]{1,0:T(8,128)(2,1)} %vision_hbm_ref.5, bf16[3840,2048]{1,0:T(8,128)(2,1)} %weight_ref.5), custom_call_target="tpu_custom_call" | custom-call | bytes 18000000 | tf_op jit(solution)/shard_map/pallas_call | solution.py:55
  14.1 1.6 %collective-permute-done.1.refs_1_ = f32[96,512]{1,0:T(8,128)S(1)} collective-permute-done((f32[96,512]{1,0:T(8,128)S(1)}, f32[96,512]{1,0:T(8,128)S(1)}, u32[]{:S(2)}, u32[]{:S(2)}) %collective-permute-start.1) | collective-permute-done | bytes 196640 | tf_op jit(solution)/shard_map/ppermute | solution.py:296
  15.9 2.7 %collective-permute-start.3 = (bf16[4,96,256]{2,1,0:T(8,128)(2,1)S(1)}, bf16[4,96,256]{2,1,0:T(8,128)(2,1)S(1)}, u32[]{:S(2)}, u32[]{:S(2)}) collective-permute-start(bf16[4,96,256]{2,1,0:T(8,128)(2,1)S(1)} %shard_map.68.refs_0_), channel_id=1, source_target_pairs={{0,8},{2,10},{4,12},{6,14},{8,0},{10,2},{12,4},{14,6},{1,9},{3,11}... | collective-permute-start | bytes 589832 | tf_op jit(solution)/shard_map/ppermute | solution.py:296
  18.5 1.6 %collective-permute-start.2 = (bf16[4,96,256]{2,1,0:T(8,128)(2,1)S(1)}, bf16[4,96,256]{2,1,0:T(8,128)(2,1)S(1)}, u32[]{:S(2)}, u32[]{:S(2)}) collective-permute-start(bf16[4,96,256]{2,1,0:T(8,128)(2,1)S(1)} %shard_map.68.refs_0_), channel_id=1, source_target_pairs={{0,4},{2,6},{4,0},{6,2},{8,12},{10,14},{12,8},{14,10},{1,5},{3,7},... | collective-permute-start | bytes 589832 | tf_op jit(solution)/shard_map/ppermute | solution.py:296
  20.1 2.8 %shard_map.64 = (bf16[4,2048,128]{2,1,0:T(8,128)(2,1)S(1)}, bf16[512,128]{1,0:T(8,128)(2,1)S(1)}, bf16[512,512]{1,0:T(8,128)(2,1)S(1)}, s32[3,4]{1,0:T(4,128)S(1)}) custom-call(bf16[512,4,512]{2,1,0:T(4,128)(2,1)S(1)} %copy-done, s32[2,512]{1,0:T(2,128)S(1)} %bitcast.6), custom_call_target="tpu_custom_call" | custom-call | bytes 360000 | tf_op jit(solution)/shard_map/pallas_call | solution.py:140
  23.0 1.6 %collective-permute-start.5 = (bf16[4,96,256]{2,1,0:T(8,128)(2,1)S(1)}, bf16[4,96,256]{2,1,0:T(8,128)(2,1)}, u32[]{:S(2)}, u32[]{:S(2)}) collective-permute-start(bf16[4,96,256]{2,1,0:T(8,128)(2,1)S(1)} %shard_map.68.refs_0_), channel_id=1, source_target_pairs={{0,16},{16,0},{1,17},{17,1},{2,18},{18,2},{3,19},{19,3},{4,20},{20... | collective-permute-start | bytes 589832 | tf_op jit(solution)/shard_map/ppermute | solution.py:296
  24.6 2.0 %collective-permute-done.3.refs_2_ = bf16[4,96,256]{2,1,0:T(8,128)(2,1)S(1)} collective-permute-done((bf16[4,96,256]{2,1,0:T(8,128)(2,1)S(1)}, bf16[4,96,256]{2,1,0:T(8,128)(2,1)S(1)}, u32[]{:S(2)}, u32[]{:S(2)}) %collective-permute-start.3) | collective-permute-done | bytes 196640 | tf_op jit(solution)/shard_map/ppermute | solution.py:296
  26.6 0.2 collective-permute-done.2.refs_1_
  26.8 1.4 %collective-permute-start.4 = (bf16[4,96,256]{2,1,0:T(8,128)(2,1)S(1)}, bf16[4,96,256]{2,1,0:T(8,128)(2,1)}, u32[]{:S(2)}, u32[]{:S(2)}) collective-permute-start(bf16[4,96,256]{2,1,0:T(8,128)(2,1)S(1)} %collective-permute-done.3.refs_2_), channel_id=1, source_target_pairs={{0,4},{2,6},{4,0},{6,2},{8,12},{10,14},{12,8},{14,10},{1,5},{3,7},... | collective-permute-start | bytes 589832 | tf_op jit(solution)/shard_map/ppermute | solution.py:296
  28.3 1.5 %collective-permute-start.7 = (bf16[4,96,256]{2,1,0:T(8,128)(2,1)S(1)}, bf16[4,96,256]{2,1,0:T(8,128)(2,1)}, u32[]{:S(2)}, u32[]{:S(2)}) collective-permute-start(bf16[4,96,256]{2,1,0:T(8,128)(2,1)S(1)} %collective-permute-done.3.refs_2_), channel_id=1, source_target_pairs={{0,16},{16,0},{1,17},{17,1},{2,18},{18,2},{3,19},{19,3},{4,20},{20... | collective-permute-start | bytes 589832 | tf_op jit(solution)/shard_map/ppermute | solution.py:296
  29.8 0.2 collective-permute-start.10
  30.0 0.4 collective-permute-done.5.refs_4_
  30.4 0.4 collective-permute-start.6
  30.9 1.7 %collective-permute-done.4.refs_3_ = bf16[4,96,256]{2,1,0:T(8,128)(2,1)} collective-permute-done((bf16[4,96,256]{2,1,0:T(8,128)(2,1)S(1)}, bf16[4,96,256]{2,1,0:T(8,128)(2,1)}, u32[]{:S(2)}, u32[]{:S(2)}) %collective-permute-start.4) | collective-permute-done | bytes 196640 | tf_op jit(solution)/shard_map/ppermute | solution.py:296
  32.6 1.5 %collective-permute-start.8 = (bf16[4,96,256]{2,1,0:T(8,128)(2,1)}, bf16[4,96,256]{2,1,0:T(8,128)(2,1)}, u32[]{:S(2)}, u32[]{:S(2)}) collective-permute-start(bf16[4,96,256]{2,1,0:T(8,128)(2,1)} %collective-permute-done.4.refs_3_), channel_id=1, source_target_pairs={{0,16},{16,0},{1,17},{17,1},{2,18},{18,2},{3,19},{19,3},{4,20},{20... | collective-permute-start | bytes 589832 | tf_op jit(solution)/shard_map/ppermute | solution.py:296
  34.1 2.0 %collective-permute-done.7.refs_6_ = bf16[4,96,256]{2,1,0:T(8,128)(2,1)} collective-permute-done((bf16[4,96,256]{2,1,0:T(8,128)(2,1)S(1)}, bf16[4,96,256]{2,1,0:T(8,128)(2,1)}, u32[]{:S(2)}, u32[]{:S(2)}) %collective-permute-start.7) | collective-permute-done | bytes 196640 | tf_op jit(solution)/shard_map/ppermute | solution.py:296
  36.1 0.6 collective-permute-start.15
  36.8 0.6 %collective-permute-done.6.refs_5_ = bf16[4,96,256]{2,1,0:T(8,128)(2,1)} collective-permute-done((bf16[4,96,256]{2,1,0:T(8,128)(2,1)}, bf16[4,96,256]{2,1,0:T(8,128)(2,1)}, u32[]{:S(2)}, u32[]{:S(2)}) %collective-permute-start.6) | collective-permute-done | bytes 196640 | tf_op jit(solution)/shard_map/ppermute | solution.py:296
  37.4 2.5 %collective-permute-done.8.refs_7_ = bf16[4,96,256]{2,1,0:T(8,128)(2,1)} collective-permute-done((bf16[4,96,256]{2,1,0:T(8,128)(2,1)}, bf16[4,96,256]{2,1,0:T(8,128)(2,1)}, u32[]{:S(2)}, u32[]{:S(2)}) %collective-permute-start.8) | collective-permute-done | bytes 196640 | tf_op jit(solution)/shard_map/ppermute | solution.py:296
  39.9 1.8 %collective-permute-done.16.refs_15_ = bf16[4,96,256]{2,1,0:T(8,128)(2,1)} collective-permute-done((bf16[4,96,256]{2,1,0:T(8,128)(2,1)}, bf16[4,96,256]{2,1,0:T(8,128)(2,1)}, u32[]{:S(2)}, u32[]{:S(2)}) %collective-permute-start.16) | collective-permute-done | bytes 196640 | tf_op jit(solution)/shard_map/ppermute | solution.py:296
  41.7 16.0 %shard_map.69 = bf16[512,4,512]{2,1,0:T(4,128)(2,1)} custom-call(s32[1]{0:T(128)} %bitcast.home_ref, s32[4]{0:T(128)S(1)} %copy-done.4, s32[3,4]{1,0:T(4,128)S(1)} %get-tuple-element.11.hull_ref, bf16[4,96,256]{2,1,0:T(8,128)(2,1)} %copy-done.1, bf16[4,96,256]{2,1,0:T(8,128)(2,1)} %copy-done.6, bf16[4,96,256]{2,1,0:T(8,128)(2,1)} %copy-done.5, ...), custom_call_target="tpu_custom_call" | custom-call | bytes 54000000 | tf_op jit(solution)/shard_map/pallas_call | solution.py:248
  (36 shorter events, 0.5 us)
Async XLA Ops:
  3.1 11.0 %collective-permute-start = (f32[96,512]{1,0:T(8,128)S(1)}, f32[96,512]{1,0:T(8,128)S(1)}, u32[]{:S(2)}, u32[]{:S(2)}) collective-permute-start(f32[96,512]{1,0:T(8,128)S(1)} %shard_map.66), channel_id=1, source_target_pairs={{0,1},{1,0},{2,3},{3,2},{4,5},{5,4},{6,7},{7,6},{8,9},{9,8},{10,11... | collective-permute-start | bytes 589832 | tf_op jit(solution)/shard_map/ppermute | solution.py:296
  9.3 6.4 %collective-permute-start.1 = (f32[96,512]{1,0:T(8,128)S(1)}, f32[96,512]{1,0:T(8,128)S(1)}, u32[]{:S(2)}, u32[]{:S(2)}) collective-permute-start(f32[96,512]{1,0:T(8,128)S(1)} %shard_map.67), channel_id=1, source_target_pairs={{0,1},{1,0},{2,3},{3,2},{4,5},{5,4},{6,7},{7,6},{8,9},{9,8},{10,11... | collective-permute-start | bytes 589832 | tf_op jit(solution)/shard_map/ppermute | solution.py:296
  9.4 10.7 %copy-start = (bf16[512,4,512]{2,1,0:T(4,128)(2,1)S(1)}, bf16[512,4,512]{2,1,0:T(4,128)(2,1)}, u32[]{:S(2)}) copy-start(bf16[512,4,512]{2,1,0:T(4,128)(2,1)} %q_ref.1) | copy-start | bytes 6291460
  9.4 10.7 %copy-start.2 = (s32[512,2]{0,1:T(2,128)S(1)}, s32[512,2]{0,1:T(2,128)}, u32[]{:S(2)}) copy-start(s32[512,2]{0,1:T(2,128)} %param.11) | copy-start | bytes 12292
  14.1 27.6 %copy-start.4 = (s32[4]{0:T(128)S(1)}, s32[4]{0:T(128)}, u32[]{:S(2)}) copy-start(s32[4]{0:T(128)} %tokens_ref.1) | copy-start | bytes 52
  15.9 25.8 %copy-start.1 = (bf16[4,96,256]{2,1,0:T(8,128)(2,1)}, bf16[4,96,256]{2,1,0:T(8,128)(2,1)S(1)}, u32[]{:S(2)}) copy-start(bf16[4,96,256]{2,1,0:T(8,128)(2,1)S(1)} %shard_map.68.refs_0_) | copy-start | bytes 589828
  15.9 10.7 %collective-permute-start.3 = (bf16[4,96,256]{2,1,0:T(8,128)(2,1)S(1)}, bf16[4,96,256]{2,1,0:T(8,128)(2,1)S(1)}, u32[]{:S(2)}, u32[]{:S(2)}) collective-permute-start(bf16[4,96,256]{2,1,0:T(8,128)(2,1)S(1)} %shard_map.68.refs_0_), channel_id=1, source_target_pairs={{0,8},{2,10},{4,12},{6,14},{8,0},{10,2},{12,4},{14,6},{1,9},{3,11}... | collective-permute-start | bytes 589832 | tf_op jit(solution)/shard_map/ppermute | solution.py:296
  18.5 8.3 %collective-permute-start.2 = (bf16[4,96,256]{2,1,0:T(8,128)(2,1)S(1)}, bf16[4,96,256]{2,1,0:T(8,128)(2,1)S(1)}, u32[]{:S(2)}, u32[]{:S(2)}) collective-permute-start(bf16[4,96,256]{2,1,0:T(8,128)(2,1)S(1)} %shard_map.68.refs_0_), channel_id=1, source_target_pairs={{0,4},{2,6},{4,0},{6,2},{8,12},{10,14},{12,8},{14,10},{1,5},{3,7},... | collective-permute-start | bytes 589832 | tf_op jit(solution)/shard_map/ppermute | solution.py:296
  22.9 6.8 %collective-permute-start.9 = (bf16[4,96,256]{2,1,0:T(8,128)(2,1)S(1)}, bf16[4,96,256]{2,1,0:T(8,128)(2,1)S(1)}, u32[]{:S(2)}, u32[]{:S(2)}) collective-permute-start(bf16[4,96,256]{2,1,0:T(8,128)(2,1)S(1)} %shard_map.68.refs_0_), channel_id=1, source_target_pairs={{0,2},{2,0},{4,6},{6,4},{8,10},{10,8},{12,14},{14,12},{1,3},{3,1},... | collective-permute-start | bytes 589832 | tf_op jit(solution)/shard_map/ppermute | solution.py:296
  23.0 7.4 %collective-permute-start.5 = (bf16[4,96,256]{2,1,0:T(8,128)(2,1)S(1)}, bf16[4,96,256]{2,1,0:T(8,128)(2,1)}, u32[]{:S(2)}, u32[]{:S(2)}) collective-permute-start(bf16[4,96,256]{2,1,0:T(8,128)(2,1)S(1)} %shard_map.68.refs_0_), channel_id=1, source_target_pairs={{0,16},{16,0},{1,17},{17,1},{2,18},{18,2},{3,19},{19,3},{4,20},{20... | collective-permute-start | bytes 589832 | tf_op jit(solution)/shard_map/ppermute | solution.py:296
  26.6 15.1 %copy-start.5 = (bf16[4,96,256]{2,1,0:T(8,128)(2,1)}, bf16[4,96,256]{2,1,0:T(8,128)(2,1)S(1)}, u32[]{:S(2)}) copy-start(bf16[4,96,256]{2,1,0:T(8,128)(2,1)S(1)} %collective-permute-done.3.refs_2_) | copy-start | bytes 589828
  26.8 14.9 %copy-start.6 = (bf16[4,96,256]{2,1,0:T(8,128)(2,1)}, bf16[4,96,256]{2,1,0:T(8,128)(2,1)S(1)}, u32[]{:S(2)}) copy-start(bf16[4,96,256]{2,1,0:T(8,128)(2,1)S(1)} %collective-permute-done.2.refs_1_) | copy-start | bytes 589828
  26.8 5.8 %collective-permute-start.4 = (bf16[4,96,256]{2,1,0:T(8,128)(2,1)S(1)}, bf16[4,96,256]{2,1,0:T(8,128)(2,1)}, u32[]{:S(2)}, u32[]{:S(2)}) collective-permute-start(bf16[4,96,256]{2,1,0:T(8,128)(2,1)S(1)} %collective-permute-done.3.refs_2_), channel_id=1, source_target_pairs={{0,4},{2,6},{4,0},{6,2},{8,12},{10,14},{12,8},{14,10},{1,5},{3,7},... | collective-permute-start | bytes 589832 | tf_op jit(solution)/shard_map/ppermute | solution.py:296
  28.3 5.8 %collective-permute-start.11 = (bf16[4,96,256]{2,1,0:T(8,128)(2,1)S(1)}, bf16[4,96,256]{2,1,0:T(8,128)(2,1)S(1)}, u32[]{:S(2)}, u32[]{:S(2)}) collective-permute-start(bf16[4,96,256]{2,1,0:T(8,128)(2,1)S(1)} %collective-permute-done.3.refs_2_), channel_id=1, source_target_pairs={{0,2},{2,0},{4,6},{6,4},{8,10},{10,8},{12,14},{14,12},{1,3},{3,1},... | collective-permute-start | bytes 589832 | tf_op jit(solution)/shard_map/ppermute | solution.py:296
  28.3 7.8 %collective-permute-start.7 = (bf16[4,96,256]{2,1,0:T(8,128)(2,1)S(1)}, bf16[4,96,256]{2,1,0:T(8,128)(2,1)}, u32[]{:S(2)}, u32[]{:S(2)}) collective-permute-start(bf16[4,96,256]{2,1,0:T(8,128)(2,1)S(1)} %collective-permute-done.3.refs_2_), channel_id=1, source_target_pairs={{0,16},{16,0},{1,17},{17,1},{2,18},{18,2},{3,19},{19,3},{4,20},{20... | collective-permute-start | bytes 589832 | tf_op jit(solution)/shard_map/ppermute | solution.py:296
  29.7 11.9 %copy-start.7 = (bf16[4,96,256]{2,1,0:T(8,128)(2,1)}, bf16[4,96,256]{2,1,0:T(8,128)(2,1)S(1)}, u32[]{:S(2)}) copy-start(bf16[4,96,256]{2,1,0:T(8,128)(2,1)S(1)} %collective-permute-done.9.refs_8_) | copy-start | bytes 589828
  29.8 6.3 %collective-permute-start.10 = (bf16[4,96,256]{2,1,0:T(8,128)(2,1)S(1)}, bf16[4,96,256]{2,1,0:T(8,128)(2,1)S(1)}, u32[]{:S(2)}, u32[]{:S(2)}) collective-permute-start(bf16[4,96,256]{2,1,0:T(8,128)(2,1)S(1)} %collective-permute-done.2.refs_1_), channel_id=1, source_target_pairs={{0,2},{2,0},{4,6},{6,4},{8,10},{10,8},{12,14},{14,12},{1,3},{3,1},... | collective-permute-start | bytes 589832 | tf_op jit(solution)/shard_map/ppermute | solution.py:296
  30.4 7.0 %collective-permute-start.6 = (bf16[4,96,256]{2,1,0:T(8,128)(2,1)}, bf16[4,96,256]{2,1,0:T(8,128)(2,1)}, u32[]{:S(2)}, u32[]{:S(2)}) collective-permute-start(bf16[4,96,256]{2,1,0:T(8,128)(2,1)} %collective-permute-done.5.refs_4_), channel_id=1, source_target_pairs={{0,4},{2,6},{4,0},{6,2},{8,12},{10,14},{12,8},{14,10},{1,5},{3,7},... | collective-permute-start | bytes 589832 | tf_op jit(solution)/shard_map/ppermute | solution.py:296
  32.6 7.3 %collective-permute-start.8 = (bf16[4,96,256]{2,1,0:T(8,128)(2,1)}, bf16[4,96,256]{2,1,0:T(8,128)(2,1)}, u32[]{:S(2)}, u32[]{:S(2)}) collective-permute-start(bf16[4,96,256]{2,1,0:T(8,128)(2,1)} %collective-permute-done.4.refs_3_), channel_id=1, source_target_pairs={{0,16},{16,0},{1,17},{17,1},{2,18},{18,2},{3,19},{19,3},{4,20},{20... | collective-permute-start | bytes 589832 | tf_op jit(solution)/shard_map/ppermute | solution.py:296
  34.1 5.8 %collective-permute-start.13 = (bf16[4,96,256]{2,1,0:T(8,128)(2,1)}, bf16[4,96,256]{2,1,0:T(8,128)(2,1)}, u32[]{:S(2)}, u32[]{:S(2)}) collective-permute-start(bf16[4,96,256]{2,1,0:T(8,128)(2,1)} %collective-permute-done.5.refs_4_), channel_id=1, source_target_pairs={{0,2},{2,0},{4,6},{6,4},{8,10},{10,8},{12,14},{14,12},{1,3},{3,1},... | collective-permute-start | bytes 589832 | tf_op jit(solution)/shard_map/ppermute | solution.py:296
  36.1 3.8 %collective-permute-start.12 = (bf16[4,96,256]{2,1,0:T(8,128)(2,1)}, bf16[4,96,256]{2,1,0:T(8,128)(2,1)}, u32[]{:S(2)}, u32[]{:S(2)}) collective-permute-start(bf16[4,96,256]{2,1,0:T(8,128)(2,1)} %collective-permute-done.4.refs_3_), channel_id=1, source_target_pairs={{0,2},{2,0},{4,6},{6,4},{8,10},{10,8},{12,14},{14,12},{1,3},{3,1},... | collective-permute-start | bytes 589832 | tf_op jit(solution)/shard_map/ppermute | solution.py:296
  36.1 3.8 %collective-permute-start.15 = (bf16[4,96,256]{2,1,0:T(8,128)(2,1)}, bf16[4,96,256]{2,1,0:T(8,128)(2,1)}, u32[]{:S(2)}, u32[]{:S(2)}) collective-permute-start(bf16[4,96,256]{2,1,0:T(8,128)(2,1)} %collective-permute-done.7.refs_6_), channel_id=1, source_target_pairs={{0,2},{2,0},{4,6},{6,4},{8,10},{10,8},{12,14},{14,12},{1,3},{3,1},... | collective-permute-start | bytes 589832 | tf_op jit(solution)/shard_map/ppermute | solution.py:296
  37.4 2.5 %collective-permute-start.14 = (bf16[4,96,256]{2,1,0:T(8,128)(2,1)}, bf16[4,96,256]{2,1,0:T(8,128)(2,1)}, u32[]{:S(2)}, u32[]{:S(2)}) collective-permute-start(bf16[4,96,256]{2,1,0:T(8,128)(2,1)} %collective-permute-done.6.refs_5_), channel_id=1, source_target_pairs={{0,2},{2,0},{4,6},{6,4},{8,10},{10,8},{12,14},{14,12},{1,3},{3,1},... | collective-permute-start | bytes 589832 | tf_op jit(solution)/shard_map/ppermute | solution.py:296
  39.9 1.8 %collective-permute-start.16 = (bf16[4,96,256]{2,1,0:T(8,128)(2,1)}, bf16[4,96,256]{2,1,0:T(8,128)(2,1)}, u32[]{:S(2)}, u32[]{:S(2)}) collective-permute-start(bf16[4,96,256]{2,1,0:T(8,128)(2,1)} %collective-permute-done.8.refs_7_), channel_id=1, source_target_pairs={{0,2},{2,0},{4,6},{6,4},{8,10},{10,8},{12,14},{14,12},{1,3},{3,1},... | collective-permute-start | bytes 589832 | tf_op jit(solution)/shard_map/ppermute | solution.py:296
  (3 other events, 9.0 us)

commit v8 on v6

--- a/solution.py
+++ b/solution.py
@@ -302,9 +302,9 @@
     arrived = [across(half, "tensor", 1) for half in theirs]
     mine = part(1, me_tensor)
     block = finish(mine, arrived, key_gain, heads, dim)
-    near, far, side = across(block, "seq", 2), across(block, "seq", 4), across(after(text, block), "segment", 1)
+    near, far, side = across(block, "seq", 2), across(block, "seq", 4), across(block, "segment", 1)
     far_near, side_far = across(after(near, far), "seq", 2), across(far, "segment", 1)
-    side_near = across(side, "seq", 2)
+    side_near = across(after(text, side), "seq", 2)
     lane = [block, near, far, far_near, side, side_near, side_far, across(far_near, "segment", 1)]
     kv = lane + [across(piece, "seq", 1) for piece in lane]
     return attend(text, kv, offsets, home, tile_tokens, tile_len)

time: 58 us -> 61 us (1.052)
  waiting for transfers between devices: 12.9 us -> 16.5 us
    ppermute x17, waiting for transfers between devices: 12.9 us -> 16.5 us  [across(): lax.ppermute(array, axis, [(i, i ^ step) for i in range(lax.axis_size(axi...]
  transfers between devices with their start and end apart: 17 -> 17, of which waited for: 9 -> 7; matrix products, arithmetic and copies ran while one was open for 0% -> 0% of each run, Pallas kernels for 18% -> 17%
where the time goes in v8:
time: 61 us; the launch traced here: 60.8 us
  Pallas kernels  29.7 us (49%)
  waiting for transfers between devices  16.5 us (27%)
  starting transfers between devices  14.2 us (23%)
    ppermute x17, waiting for transfers between devices, across(): lax.ppermute(array, axis, [(i, i ^ step) for i in range(lax.axis_size(axi...  16.5 us
    pallas_call x1, Pallas kernels, attend(): pl.pallas_call(functools.partial(attend_kernel, (heads, blocks, group, di...  16 us
    ppermute x17, starting transfers between devices, across(): lax.ppermute(array, axis, [(i, i ^ step) for i in range(lax.axis_size(axi...  14.2 us
    pallas_call x3, Pallas kernels, project(): pl.pallas_call(functools.partial(project_kernel, bounds), in_specs=[SMEM,...  10.8 us
    pallas_call x1, Pallas kernels, sort_rows(): pl.pallas_call(functools.partial(sort_kernel, tiles, group), in_specs=[VM...  2.78 us
  transfers between devices with their start and end apart: 17, of which 7 were waited for; matrix products, arithmetic and copies ran while one was open for 0% of the time, Pallas kernels for 17%

profile of v8, /device:TPU:0, one launch (start us, length us, event | category | flops | bytes accessed | tf_op | source)
XLA Modules:
  0.0 60.8 jit_solution(5538874143762524266)
XLA Ops:
  0.0 3.1 %shard_map.66 = f32[96,512]{1,0:T(8,128)S(1)} custom-call(s32[1]{0:T(128)} %bitcast.3.block_ref, bf16[96,3840]{1,0:T(8,128)(2,1)} %vision_hbm_ref.5, bf16[3840,2048]{1,0:T(8,128)(2,1)} %weight_ref.5), custom_call_target="tpu_custom_call" | custom-call | bytes 10800000 | tf_op jit(solution)/shard_map/pallas_call | solution.py:55
  3.1 3.1 %collective-permute-start = (f32[96,512]{1,0:T(8,128)S(1)}, f32[96,512]{1,0:T(8,128)S(1)}, u32[]{:S(2)}, u32[]{:S(2)}) collective-permute-start(f32[96,512]{1,0:T(8,128)S(1)} %shard_map.66), channel_id=1, source_target_pairs={{0,1},{1,0},{2,3},{3,2},{4,5},{5,4},{6,7},{7,6},{8,9},{9,8},{10,11... | collective-permute-start | bytes 589832 | tf_op jit(solution)/shard_map/ppermute | solution.py:292
  6.2 3.1 %shard_map.67 = f32[96,512]{1,0:T(8,128)S(1)} custom-call(s32[1]{0:T(128)} %bitcast.4.block_ref, bf16[96,3840]{1,0:T(8,128)(2,1)} %vision_hbm_ref.5, bf16[3840,2048]{1,0:T(8,128)(2,1)} %weight_ref.5), custom_call_target="tpu_custom_call" | custom-call | bytes 10800000 | tf_op jit(solution)/shard_map/pallas_call | solution.py:55
  9.4 4.6 %shard_map.65.own_ref = f32[96,1024]{1,0:T(8,128)S(1)} custom-call(s32[1]{0:T(128)} %bitcast.2.block_ref, bf16[96,3840]{1,0:T(8,128)(2,1)} %vision_hbm_ref.5, bf16[3840,2048]{1,0:T(8,128)(2,1)} %weight_ref.5), custom_call_target="tpu_custom_call" | custom-call | bytes 18000000 | tf_op jit(solution)/shard_map/pallas_call | solution.py:55
  14.1 1.6 %collective-permute-done.1.refs_1_ = f32[96,512]{1,0:T(8,128)S(1)} collective-permute-done((f32[96,512]{1,0:T(8,128)S(1)}, f32[96,512]{1,0:T(8,128)S(1)}, u32[]{:S(2)}, u32[]{:S(2)}) %collective-permute-start.1) | collective-permute-done | bytes 196640 | tf_op jit(solution)/shard_map/ppermute | solution.py:292
  15.7 0.2 shard_map.68.refs_0_
  15.9 2.7 %collective-permute-start.3 = (bf16[4,96,256]{2,1,0:T(8,128)(2,1)S(1)}, bf16[4,96,256]{2,1,0:T(8,128)(2,1)S(1)}, u32[]{:S(2)}, u32[]{:S(2)}) collective-permute-start(bf16[4,96,256]{2,1,0:T(8,128)(2,1)S(1)} %shard_map.68.refs_0_), channel_id=1, source_target_pairs={{0,8},{2,10},{4,12},{6,14},{8,0},{10,2},{12,4},{14,6},{1,9},{3,11}... | collective-permute-start | bytes 589832 | tf_op jit(solution)/shard_map/ppermute | solution.py:292
  18.5 1.6 %collective-permute-start.2 = (bf16[4,96,256]{2,1,0:T(8,128)(2,1)S(1)}, bf16[4,96,256]{2,1,0:T(8,128)(2,1)S(1)}, u32[]{:S(2)}, u32[]{:S(2)}) collective-permute-start(bf16[4,96,256]{2,1,0:T(8,128)(2,1)S(1)} %shard_map.68.refs_0_), channel_id=1, source_target_pairs={{0,4},{2,6},{4,0},{6,2},{8,12},{10,14},{12,8},{14,10},{1,5},{3,7},... | collective-permute-start | bytes 589832 | tf_op jit(solution)/shard_map/ppermute | solution.py:292
  20.1 1.5 %collective-permute-start.5 = (bf16[4,96,256]{2,1,0:T(8,128)(2,1)S(1)}, bf16[4,96,256]{2,1,0:T(8,128)(2,1)S(1)}, u32[]{:S(2)}, u32[]{:S(2)}) collective-permute-start(bf16[4,96,256]{2,1,0:T(8,128)(2,1)S(1)} %shard_map.68.refs_0_), channel_id=1, source_target_pairs={{0,16},{16,0},{1,17},{17,1},{2,18},{18,2},{3,19},{19,3},{4,20},{20... | collective-permute-start | bytes 589832 | tf_op jit(solution)/shard_map/ppermute | solution.py:292
  21.6 5.0 %collective-permute-done.3.refs_2_ = bf16[4,96,256]{2,1,0:T(8,128)(2,1)S(1)} collective-permute-done((bf16[4,96,256]{2,1,0:T(8,128)(2,1)S(1)}, bf16[4,96,256]{2,1,0:T(8,128)(2,1)S(1)}, u32[]{:S(2)}, u32[]{:S(2)}) %collective-permute-start.3) | collective-permute-done | bytes 196640 | tf_op jit(solution)/shard_map/ppermute | solution.py:292
  26.6 0.2 collective-permute-done.2.refs_1_
  26.8 1.4 %collective-permute-start.4 = (bf16[4,96,256]{2,1,0:T(8,128)(2,1)S(1)}, bf16[4,96,256]{2,1,0:T(8,128)(2,1)}, u32[]{:S(2)}, u32[]{:S(2)}) collective-permute-start(bf16[4,96,256]{2,1,0:T(8,128)(2,1)S(1)} %collective-permute-done.3.refs_2_), channel_id=1, source_target_pairs={{0,4},{2,6},{4,0},{6,2},{8,12},{10,14},{12,8},{14,10},{1,5},{3,7},... | collective-permute-start | bytes 589832 | tf_op jit(solution)/shard_map/ppermute | solution.py:292
  28.3 2.8 %shard_map.64 = (bf16[4,2048,128]{2,1,0:T(8,128)(2,1)S(1)}, bf16[512,128]{1,0:T(8,128)(2,1)S(1)}, bf16[512,512]{1,0:T(8,128)(2,1)S(1)}, s32[3,4]{1,0:T(4,128)S(1)}) custom-call(bf16[512,4,512]{2,1,0:T(4,128)(2,1)S(1)} %copy-done, s32[2,512]{1,0:T(2,128)S(1)} %bitcast.6), custom_call_target="tpu_custom_call" | custom-call | bytes 360000 | tf_op jit(solution)/shard_map/pallas_call | solution.py:140
  31.1 0.5 collective-permute-start.11
  31.6 1.5 %collective-permute-start.7 = (bf16[4,96,256]{2,1,0:T(8,128)(2,1)S(1)}, bf16[4,96,256]{2,1,0:T(8,128)(2,1)}, u32[]{:S(2)}, u32[]{:S(2)}) collective-permute-start(bf16[4,96,256]{2,1,0:T(8,128)(2,1)S(1)} %collective-permute-done.3.refs_2_), channel_id=1, source_target_pairs={{0,16},{16,0},{1,17},{17,1},{2,18},{18,2},{3,19},{19,3},{4,20},{20... | collective-permute-start | bytes 589832 | tf_op jit(solution)/shard_map/ppermute | solution.py:292
  33.1 0.6 collective-permute-start.6
  33.7 0.5 collective-permute-start.8
  34.3 0.5 collective-permute-start.12
  34.8 4.7 %collective-permute-done.7.refs_6_ = bf16[4,96,256]{2,1,0:T(8,128)(2,1)} collective-permute-done((bf16[4,96,256]{2,1,0:T(8,128)(2,1)S(1)}, bf16[4,96,256]{2,1,0:T(8,128)(2,1)}, u32[]{:S(2)}, u32[]{:S(2)}) %collective-permute-start.7) | collective-permute-done | bytes 196640 | tf_op jit(solution)/shard_map/ppermute | solution.py:292
  39.5 0.3 collective-permute-done.6.refs_5_
  39.9 0.2 collective-permute-start.14
  40.0 2.8 %collective-permute-done.8.refs_7_ = bf16[4,96,256]{2,1,0:T(8,128)(2,1)} collective-permute-done((bf16[4,96,256]{2,1,0:T(8,128)(2,1)}, bf16[4,96,256]{2,1,0:T(8,128)(2,1)}, u32[]{:S(2)}, u32[]{:S(2)}) %collective-permute-start.8) | collective-permute-done | bytes 196640 | tf_op jit(solution)/shard_map/ppermute | solution.py:292
  42.9 1.7 %collective-permute-done.16.refs_15_ = bf16[4,96,256]{2,1,0:T(8,128)(2,1)} collective-permute-done((bf16[4,96,256]{2,1,0:T(8,128)(2,1)}, bf16[4,96,256]{2,1,0:T(8,128)(2,1)}, u32[]{:S(2)}, u32[]{:S(2)}) %collective-permute-start.16) | collective-permute-done | bytes 196640 | tf_op jit(solution)/shard_map/ppermute | solution.py:292
  44.7 16.0 %shard_map.69 = bf16[512,4,512]{2,1,0:T(4,128)(2,1)} custom-call(s32[1]{0:T(128)} %bitcast.home_ref, s32[4]{0:T(128)S(1)} %copy-done.4, s32[3,4]{1,0:T(4,128)S(1)} %get-tuple-element.11.hull_ref, bf16[4,96,256]{2,1,0:T(8,128)(2,1)} %copy-done.1, bf16[4,96,256]{2,1,0:T(8,128)(2,1)} %copy-done.6, bf16[4,96,256]{2,1,0:T(8,128)(2,1)} %copy-done.5, ...), custom_call_target="tpu_custom_call" | custom-call | bytes 54000000 | tf_op jit(solution)/shard_map/pallas_call | solution.py:244
  (38 shorter events, 0.2 us)
Async XLA Ops:
  3.1 11.0 %collective-permute-start = (f32[96,512]{1,0:T(8,128)S(1)}, f32[96,512]{1,0:T(8,128)S(1)}, u32[]{:S(2)}, u32[]{:S(2)}) collective-permute-start(f32[96,512]{1,0:T(8,128)S(1)} %shard_map.66), channel_id=1, source_target_pairs={{0,1},{1,0},{2,3},{3,2},{4,5},{5,4},{6,7},{7,6},{8,9},{9,8},{10,11... | collective-permute-start | bytes 589832 | tf_op jit(solution)/shard_map/ppermute | solution.py:292
  9.3 6.4 %collective-permute-start.1 = (f32[96,512]{1,0:T(8,128)S(1)}, f32[96,512]{1,0:T(8,128)S(1)}, u32[]{:S(2)}, u32[]{:S(2)}) collective-permute-start(f32[96,512]{1,0:T(8,128)S(1)} %shard_map.67), channel_id=1, source_target_pairs={{0,1},{1,0},{2,3},{3,2},{4,5},{5,4},{6,7},{7,6},{8,9},{9,8},{10,11... | collective-permute-start | bytes 589832 | tf_op jit(solution)/shard_map/ppermute | solution.py:292
  9.4 18.9 %copy-start = (bf16[512,4,512]{2,1,0:T(4,128)(2,1)S(1)}, bf16[512,4,512]{2,1,0:T(4,128)(2,1)}, u32[]{:S(2)}) copy-start(bf16[512,4,512]{2,1,0:T(4,128)(2,1)} %q_ref.1) | copy-start | bytes 6291460
  9.4 18.9 %copy-start.2 = (s32[512,2]{0,1:T(2,128)S(1)}, s32[512,2]{0,1:T(2,128)}, u32[]{:S(2)}) copy-start(s32[512,2]{0,1:T(2,128)} %param.11) | copy-start | bytes 12292
  14.1 30.6 %copy-start.4 = (s32[4]{0:T(128)S(1)}, s32[4]{0:T(128)}, u32[]{:S(2)}) copy-start(s32[4]{0:T(128)} %tokens_ref.1) | copy-start | bytes 52
  15.9 28.8 %copy-start.1 = (bf16[4,96,256]{2,1,0:T(8,128)(2,1)}, bf16[4,96,256]{2,1,0:T(8,128)(2,1)S(1)}, u32[]{:S(2)}) copy-start(bf16[4,96,256]{2,1,0:T(8,128)(2,1)S(1)} %shard_map.68.refs_0_) | copy-start | bytes 589828
  15.9 10.7 %collective-permute-start.3 = (bf16[4,96,256]{2,1,0:T(8,128)(2,1)S(1)}, bf16[4,96,256]{2,1,0:T(8,128)(2,1)S(1)}, u32[]{:S(2)}, u32[]{:S(2)}) collective-permute-start(bf16[4,96,256]{2,1,0:T(8,128)(2,1)S(1)} %shard_map.68.refs_0_), channel_id=1, source_target_pairs={{0,8},{2,10},{4,12},{6,14},{8,0},{10,2},{12,4},{14,6},{1,9},{3,11}... | collective-permute-start | bytes 589832 | tf_op jit(solution)/shard_map/ppermute | solution.py:292
  18.5 8.3 %collective-permute-start.2 = (bf16[4,96,256]{2,1,0:T(8,128)(2,1)S(1)}, bf16[4,96,256]{2,1,0:T(8,128)(2,1)S(1)}, u32[]{:S(2)}, u32[]{:S(2)}) collective-permute-start(bf16[4,96,256]{2,1,0:T(8,128)(2,1)S(1)} %shard_map.68.refs_0_), channel_id=1, source_target_pairs={{0,4},{2,6},{4,0},{6,2},{8,12},{10,14},{12,8},{14,10},{1,5},{3,7},... | collective-permute-start | bytes 589832 | tf_op jit(solution)/shard_map/ppermute | solution.py:292
  20.1 10.9 %collective-permute-start.5 = (bf16[4,96,256]{2,1,0:T(8,128)(2,1)S(1)}, bf16[4,96,256]{2,1,0:T(8,128)(2,1)S(1)}, u32[]{:S(2)}, u32[]{:S(2)}) collective-permute-start(bf16[4,96,256]{2,1,0:T(8,128)(2,1)S(1)} %shard_map.68.refs_0_), channel_id=1, source_target_pairs={{0,16},{16,0},{1,17},{17,1},{2,18},{18,2},{3,19},{19,3},{4,20},{20... | collective-permute-start | bytes 589832 | tf_op jit(solution)/shard_map/ppermute | solution.py:292
  21.6 11.5 %collective-permute-start.9 = (bf16[4,96,256]{2,1,0:T(8,128)(2,1)S(1)}, bf16[4,96,256]{2,1,0:T(8,128)(2,1)S(1)}, u32[]{:S(2)}, u32[]{:S(2)}) collective-permute-start(bf16[4,96,256]{2,1,0:T(8,128)(2,1)S(1)} %shard_map.68.refs_0_), channel_id=1, source_target_pairs={{0,2},{2,0},{4,6},{6,4},{8,10},{10,8},{12,14},{14,12},{1,3},{3,1},... | collective-permute-start | bytes 589832 | tf_op jit(solution)/shard_map/ppermute | solution.py:292
  26.6 18.1 %copy-start.5 = (bf16[4,96,256]{2,1,0:T(8,128)(2,1)}, bf16[4,96,256]{2,1,0:T(8,128)(2,1)S(1)}, u32[]{:S(2)}) copy-start(bf16[4,96,256]{2,1,0:T(8,128)(2,1)S(1)} %collective-permute-done.3.refs_2_) | copy-start | bytes 589828
  26.8 17.8 %copy-start.6 = (bf16[4,96,256]{2,1,0:T(8,128)(2,1)}, bf16[4,96,256]{2,1,0:T(8,128)(2,1)S(1)}, u32[]{:S(2)}) copy-start(bf16[4,96,256]{2,1,0:T(8,128)(2,1)S(1)} %collective-permute-done.2.refs_1_) | copy-start | bytes 589828
  26.8 6.9 %collective-permute-start.4 = (bf16[4,96,256]{2,1,0:T(8,128)(2,1)S(1)}, bf16[4,96,256]{2,1,0:T(8,128)(2,1)}, u32[]{:S(2)}, u32[]{:S(2)}) collective-permute-start(bf16[4,96,256]{2,1,0:T(8,128)(2,1)S(1)} %collective-permute-done.3.refs_2_), channel_id=1, source_target_pairs={{0,4},{2,6},{4,0},{6,2},{8,12},{10,14},{12,8},{14,10},{1,5},{3,7},... | collective-permute-start | bytes 589832 | tf_op jit(solution)/shard_map/ppermute | solution.py:292
  31.1 13.6 %copy-start.7 = (bf16[4,96,256]{2,1,0:T(8,128)(2,1)}, bf16[4,96,256]{2,1,0:T(8,128)(2,1)S(1)}, u32[]{:S(2)}) copy-start(bf16[4,96,256]{2,1,0:T(8,128)(2,1)S(1)} %collective-permute-done.5.refs_4_) | copy-start | bytes 589828
  31.1 3.2 %collective-permute-start.13 = (bf16[4,96,256]{2,1,0:T(8,128)(2,1)S(1)}, bf16[4,96,256]{2,1,0:T(8,128)(2,1)S(1)}, u32[]{:S(2)}, u32[]{:S(2)}) collective-permute-start(bf16[4,96,256]{2,1,0:T(8,128)(2,1)S(1)} %collective-permute-done.5.refs_4_), channel_id=1, source_target_pairs={{0,2},{2,0},{4,6},{6,4},{8,10},{10,8},{12,14},{14,12},{1,3},{3,1},... | collective-permute-start | bytes 589832 | tf_op jit(solution)/shard_map/ppermute | solution.py:292
  31.1 3.1 %collective-permute-start.11 = (bf16[4,96,256]{2,1,0:T(8,128)(2,1)S(1)}, bf16[4,96,256]{2,1,0:T(8,128)(2,1)S(1)}, u32[]{:S(2)}, u32[]{:S(2)}) collective-permute-start(bf16[4,96,256]{2,1,0:T(8,128)(2,1)S(1)} %collective-permute-done.3.refs_2_), channel_id=1, source_target_pairs={{0,2},{2,0},{4,6},{6,4},{8,10},{10,8},{12,14},{14,12},{1,3},{3,1},... | collective-permute-start | bytes 589832 | tf_op jit(solution)/shard_map/ppermute | solution.py:292
  31.6 7.9 %collective-permute-start.7 = (bf16[4,96,256]{2,1,0:T(8,128)(2,1)S(1)}, bf16[4,96,256]{2,1,0:T(8,128)(2,1)}, u32[]{:S(2)}, u32[]{:S(2)}) collective-permute-start(bf16[4,96,256]{2,1,0:T(8,128)(2,1)S(1)} %collective-permute-done.3.refs_2_), channel_id=1, source_target_pairs={{0,16},{16,0},{1,17},{17,1},{2,18},{18,2},{3,19},{19,3},{4,20},{20... | collective-permute-start | bytes 589832 | tf_op jit(solution)/shard_map/ppermute | solution.py:292
  33.1 6.7 %collective-permute-start.6 = (bf16[4,96,256]{2,1,0:T(8,128)(2,1)S(1)}, bf16[4,96,256]{2,1,0:T(8,128)(2,1)}, u32[]{:S(2)}, u32[]{:S(2)}) collective-permute-start(bf16[4,96,256]{2,1,0:T(8,128)(2,1)S(1)} %collective-permute-done.5.refs_4_), channel_id=1, source_target_pairs={{0,4},{2,6},{4,0},{6,2},{8,12},{10,14},{12,8},{14,10},{1,5},{3,7},... | collective-permute-start | bytes 589832 | tf_op jit(solution)/shard_map/ppermute | solution.py:292
  33.7 9.1 %collective-permute-start.8 = (bf16[4,96,256]{2,1,0:T(8,128)(2,1)}, bf16[4,96,256]{2,1,0:T(8,128)(2,1)}, u32[]{:S(2)}, u32[]{:S(2)}) collective-permute-start(bf16[4,96,256]{2,1,0:T(8,128)(2,1)} %collective-permute-done.4.refs_3_), channel_id=1, source_target_pairs={{0,16},{16,0},{1,17},{17,1},{2,18},{18,2},{3,19},{19,3},{4,20},{20... | collective-permute-start | bytes 589832 | tf_op jit(solution)/shard_map/ppermute | solution.py:292
  34.3 8.6 %collective-permute-start.10 = (bf16[4,96,256]{2,1,0:T(8,128)(2,1)S(1)}, bf16[4,96,256]{2,1,0:T(8,128)(2,1)}, u32[]{:S(2)}, u32[]{:S(2)}) collective-permute-start(bf16[4,96,256]{2,1,0:T(8,128)(2,1)S(1)} %collective-permute-done.2.refs_1_), channel_id=1, source_target_pairs={{0,2},{2,0},{4,6},{6,4},{8,10},{10,8},{12,14},{14,12},{1,3},{3,1},... | collective-permute-start | bytes 589832 | tf_op jit(solution)/shard_map/ppermute | solution.py:292
  34.3 8.6 %collective-permute-start.12 = (bf16[4,96,256]{2,1,0:T(8,128)(2,1)}, bf16[4,96,256]{2,1,0:T(8,128)(2,1)}, u32[]{:S(2)}, u32[]{:S(2)}) collective-permute-start(bf16[4,96,256]{2,1,0:T(8,128)(2,1)} %collective-permute-done.4.refs_3_), channel_id=1, source_target_pairs={{0,2},{2,0},{4,6},{6,4},{8,10},{10,8},{12,14},{14,12},{1,3},{3,1},... | collective-permute-start | bytes 589832 | tf_op jit(solution)/shard_map/ppermute | solution.py:292
  39.5 3.4 %collective-permute-start.15 = (bf16[4,96,256]{2,1,0:T(8,128)(2,1)}, bf16[4,96,256]{2,1,0:T(8,128)(2,1)}, u32[]{:S(2)}, u32[]{:S(2)}) collective-permute-start(bf16[4,96,256]{2,1,0:T(8,128)(2,1)} %collective-permute-done.7.refs_6_), channel_id=1, source_target_pairs={{0,2},{2,0},{4,6},{6,4},{8,10},{10,8},{12,14},{14,12},{1,3},{3,1},... | collective-permute-start | bytes 589832 | tf_op jit(solution)/shard_map/ppermute | solution.py:292
  39.9 3.0 %collective-permute-start.14 = (bf16[4,96,256]{2,1,0:T(8,128)(2,1)}, bf16[4,96,256]{2,1,0:T(8,128)(2,1)}, u32[]{:S(2)}, u32[]{:S(2)}) collective-permute-start(bf16[4,96,256]{2,1,0:T(8,128)(2,1)} %collective-permute-done.6.refs_5_), channel_id=1, source_target_pairs={{0,2},{2,0},{4,6},{6,4},{8,10},{10,8},{12,14},{14,12},{1,3},{3,1},... | collective-permute-start | bytes 589832 | tf_op jit(solution)/shard_map/ppermute | solution.py:292
  42.8 1.8 %collective-permute-start.16 = (bf16[4,96,256]{2,1,0:T(8,128)(2,1)}, bf16[4,96,256]{2,1,0:T(8,128)(2,1)}, u32[]{:S(2)}, u32[]{:S(2)}) collective-permute-start(bf16[4,96,256]{2,1,0:T(8,128)(2,1)} %collective-permute-done.8.refs_7_), channel_id=1, source_target_pairs={{0,2},{2,0},{4,6},{6,4},{8,10},{10,8},{12,14},{14,12},{1,3},{3,1},... | collective-permute-start | bytes 589832 | tf_op jit(solution)/shard_map/ppermute | solution.py:292
  (4 other events, 27.4 us)
